TPU v7x, 32 devices: a whole 2x2x4 slice. The times are simulated.
32 devices in a mesh: dp: 4 (over z), context: 4 (over x, core), experts: 2 (over y).
Axes of the slice: x: 2, y: 2, z: 4, core: 2. Of those that a mesh axis runs over, the one named last changes fastest.
Arguments:
- block_input: bfloat16 [16, 1024, 1024], P('dp', ('context', 'experts')), may hold values from -6 to 6
- teacher: bfloat16 [16, 1024, 1024], P('dp', ('context', 'experts')), may hold values from -6 to 6
- lengths: int32 [16], replicated, may hold values from 128 to 1024, as said below
- routes: int32 [16, 1024, 8], P('dp', ('context', 'experts')), may hold values from 0 to 31, all different within a row; in each aligned block of 128 rows (0 to 127, 128 to 255, ..., all dimensions but the last counted through in order) at most 40 rows name the same one
- w_query: bfloat16 [1024, 1024], replicated, may hold values from -0.1875 to 0.1875
- w_key: bfloat16 [1024, 512], replicated, may hold values from -0.1875 to 0.1875
- w_value: bfloat16 [1024, 512], replicated, may hold values from -0.1875 to 0.1875
- w_out: bfloat16 [1024, 1024], replicated, may hold values from -1.5 to 1.5
- query_gain: float32 [64], replicated, may hold values from 0.1 to 1.9
- key_gain: float32 [64], replicated, may hold values from 0.1 to 1.9
- attn_gain: float32 [1024], replicated, may hold values from 0.1 to 1.9
- ffn_gain: float32 [1024], replicated, may hold values from 0.1 to 1.9
- w_router: bfloat16 [1024, 32], replicated, may hold values from -0.09375 to 0.09375
- w_gate: bfloat16 [32, 1024, 512], P(('context', 'experts')), may hold values from -0.1875 to 0.1875
- w_up: bfloat16 [32, 1024, 512], P(('context', 'experts')), may hold values from -0.1875 to 0.1875
- w_down: bfloat16 [32, 512, 1024], P(('context', 'experts')), may hold values from -1 to 1
Outputs:
- loss_mean: float32 [], replicated
- block_output: bfloat16 [16, 1024, 1024], P('dp', ('context', 'experts'))
- input_grad: float32 [16, 1024, 1024], P('dp', ('context', 'experts'))
- query_w_grad: float32 [1024, 1024], replicated
- key_w_grad: float32 [1024, 512], replicated
- value_w_grad: float32 [1024, 512], replicated
- out_w_grad: float32 [1024, 1024], replicated
- query_gain_grad: float32 [64], replicated
- key_gain_grad: float32 [64], replicated
- attn_gain_grad: float32 [1024], replicated
- ffn_gain_grad: float32 [1024], replicated
- router_grad: float32 [1024, 32], replicated
- gate_w_grad: float32 [32, 1024, 512], P(('context', 'experts'))
- up_w_grad: float32 [32, 1024, 512], P(('context', 'experts'))
- down_w_grad: float32 [32, 512, 1024], P(('context', 'experts'))
Inputs may be any that keep to these rules, and one draw needn't show every extreme that they name: `lengths`: in each aligned group of 4 slots (those of one index of dp) one slot, drawn from the seed, has length 1024. `routes`: each position names 8 different experts; among the 128 positions of one slot that one device holds, no expert is named more than 40 times.
All inputs are finite; a program needn't handle non-finite values.
Results may differ from a plain program's by a relative error of at most 0.017.
Values may be sent and summed in bfloat16 or wider, within the bound.
A program may use at most 384 MiB of HBM per device.

v0:
```python
from functools import partial
import math

import jax
import jax.numpy as jnp
from jax import lax
from jax.sharding import PartitionSpec as P

CAP = 160


EPSILON = 1e-06
MASKED = -1e30


def rounded(tensor):
    return lax.optimization_barrier(tensor.astype(jnp.bfloat16)).astype(jnp.float32)


def rms_scale(tensor, gain):
    return tensor * lax.rsqrt(jnp.mean(tensor * tensor, axis=-1, keepdims=True) + EPSILON) * gain


def rotary(tensor, cosine, sine_part):
    half_width = tensor.shape[-1] // 2
    former = tensor[..., :half_width]
    latter = tensor[..., half_width:]
    return jnp.concatenate(
        [former * cosine - latter * sine_part, latter * cosine + former * sine_part], axis=-1
    )


def head_prep(cosine, sine_part, raw_heads, gain):
    return rotary(rms_scale(raw_heads, gain), cosine, sine_part)


def angles(positions, head_size):
    half_width = head_size // 2
    inverse = 10000.0 ** (-(jnp.arange(half_width, dtype=jnp.float32) * 2.0 / head_size))
    turned = positions.astype(jnp.float32)[:, None] * inverse[None, :]
    return (jnp.cos(turned)[None, :, None, :], jnp.sin(turned)[None, :, None, :])


def score_block(query_five, whole_kv, start, block, query_pos, slot_lengths):
    piece = lax.dynamic_slice_in_dim(whole_kv, start, block, 1)
    slot_count = piece.shape[0]
    kv_heads = query_five.shape[2]
    head_size = query_five.shape[-1]
    kv_width = kv_heads * head_size
    key_rows = piece[..., :kv_width].reshape(slot_count, block, kv_heads, head_size)
    value_projected = piece[..., kv_width:].reshape(slot_count, block, kv_heads, head_size)
    scores = (
        jnp.einsum("sqagd,sbad->sagqb", query_five, key_rows, preferred_element_type=jnp.float32)
        * 0.125
    )
    key_pos = start + jnp.arange(block, dtype=jnp.int32)
    allowed = (key_pos[None, None, :] <= query_pos[None, :, None]) & (
        key_pos[None, None, :] < slot_lengths[:, None, None]
    )
    return (scores, allowed[:, None, None], key_rows, value_projected)


def to_owner(send_rows, expert_total):
    model_width = send_rows.shape[-1]
    shaped = send_rows.reshape(expert_total, -1, model_width)
    moved = lax.all_to_all(shaped, ("context", "experts"), split_axis=0, concat_axis=1, tiled=True)
    return moved


def to_source(owner_rows):
    model_width = owner_rows.shape[-1]
    moved = lax.all_to_all(
        owner_rows, ("context", "experts"), split_axis=1, concat_axis=0, tiled=True
    )
    return moved.reshape(-1, model_width)


def experts_forward(received, w_gate, w_up, w_down):
    gate_part = jnp.einsum("emd,edf->emf", received, w_gate, preferred_element_type=jnp.float32)
    up_part = jnp.einsum("emd,edf->emf", received, w_up, preferred_element_type=jnp.float32)
    hidden = (jax.nn.silu(gate_part) * up_part).astype(jnp.bfloat16)
    result = jnp.einsum("emf,efd->emd", hidden, w_down, preferred_element_type=jnp.float32).astype(
        jnp.bfloat16
    )
    return (gate_part, up_part, hidden, result)


def per_device(
    block_input,
    teacher,
    lengths,
    routes,
    w_query,
    w_key,
    w_value,
    w_out,
    query_gain,
    key_gain,
    attn_gain,
    ffn_gain,
    w_router,
    w_gate,
    w_up,
    w_down,
):
    slot_count, local_rows, model_width = block_input.shape
    head_size = query_gain.shape[0]
    query_width = w_query.shape[1]
    kv_width = w_key.shape[1]
    kv_heads = kv_width // head_size
    group_size = query_width // kv_width
    token_rows = slot_count * local_rows
    top_count = routes.shape[-1]
    expert_total = w_router.shape[1]
    span_length = local_rows * lax.axis_size(("context", "experts"))
    block = math.gcd(512, span_length)
    block_count = span_length // block
    slot_first = lax.axis_index("dp") * slot_count
    slot_lengths = lax.dynamic_slice_in_dim(lengths, slot_first, slot_count)
    query_pos = lax.axis_index(("context", "experts")) * local_rows + jnp.arange(
        local_rows, dtype=jnp.int32
    )
    valid_mask = (query_pos[None, :] < slot_lengths[:, None]).astype(jnp.float32)
    cosine, sine_part = angles(query_pos, head_size)
    count_all = jnp.sum(lengths).astype(jnp.float32)
    positions_all = lengths.shape[0] * span_length
    inputs = block_input.astype(jnp.float32)
    rows_one = rms_scale(inputs, attn_gain).astype(jnp.bfloat16).reshape(token_rows, model_width)
    query_unrotated = jnp.dot(rows_one, w_query, preferred_element_type=jnp.float32).reshape(
        slot_count, local_rows, -1, head_size
    )
    key_unrotated = jnp.dot(rows_one, w_key, preferred_element_type=jnp.float32).reshape(
        slot_count, local_rows, -1, head_size
    )
    value_projected = jnp.dot(rows_one, w_value, preferred_element_type=jnp.float32).astype(
        jnp.bfloat16
    )
    query_rot, query_pull = jax.vjp(
        partial(head_prep, cosine, sine_part), query_unrotated, query_gain
    )
    key_rot, key_pull = jax.vjp(partial(head_prep, cosine, sine_part), key_unrotated, key_gain)
    query_five = query_rot.astype(jnp.bfloat16).reshape(
        slot_count, local_rows, kv_heads, group_size, head_size
    )
    key_local = key_rot.astype(jnp.bfloat16)
    kv_local = jnp.concatenate(
        [
            key_local.reshape(slot_count, local_rows, kv_width),
            value_projected.reshape(slot_count, local_rows, kv_width),
        ],
        axis=-1,
    )
    whole_kv = lax.all_gather(kv_local, ("context", "experts"), axis=1, tiled=True)

    def max_step(index, carry):
        top_score, mass = carry
        scores, allowed, unused_keys, unused_values = score_block(
            query_five, whole_kv, index * block, block, query_pos, slot_lengths
        )
        newest = jnp.maximum(top_score, jnp.max(jnp.where(allowed, scores, MASKED), axis=-1))
        mass = mass * jnp.exp(top_score - newest) + jnp.sum(
            jnp.where(allowed, jnp.exp(scores - newest[..., None]), 0.0), axis=-1
        )
        return (newest, mass)

    stat_shape = (slot_count, kv_heads, group_size, local_rows)
    top_score, mass = lax.fori_loop(
        0,
        block_count,
        max_step,
        (jnp.full(stat_shape, MASKED, jnp.float32), jnp.zeros(stat_shape, jnp.float32)),
    )
    log_total = top_score + jnp.log(mass)

    def soft_block(start, size):
        scores, allowed, key_rows, value_rows_blk = score_block(
            query_five, whole_kv, start, size, query_pos, slot_lengths
        )
        weights_soft = jnp.where(allowed, jnp.exp(scores - log_total[..., None]), 0.0)
        return (weights_soft, key_rows, value_rows_blk)

    def mix_step(index, total):
        weights_soft, unused_keys, value_blk = soft_block(index * block, block)
        return total + jnp.einsum(
            "sagqb,sbad->sqagd",
            weights_soft.astype(jnp.bfloat16),
            value_blk,
            preferred_element_type=jnp.float32,
        )

    head_shape = (slot_count, local_rows, kv_heads, group_size, head_size)
    mixed_heads = lax.fori_loop(0, block_count, mix_step, jnp.zeros(head_shape, jnp.float32))
    joined_group_vectors = mixed_heads.reshape(token_rows, query_width).astype(jnp.bfloat16)
    context_mixture = jnp.dot(
        joined_group_vectors, w_out, preferred_element_type=jnp.float32
    ).reshape(slot_count, local_rows, model_width)
    after_attn = inputs + valid_mask[..., None] * context_mixture
    second_normed_input, norm_two_pull = jax.vjp(rms_scale, after_attn, ffn_gain)
    rows_two = second_normed_input.astype(jnp.bfloat16).reshape(token_rows, model_width)
    router_logits = jnp.dot(rows_two, w_router, preferred_element_type=jnp.float32)
    route_rows = routes.reshape(token_rows, top_count)
    gate_soft = jax.nn.softmax(jnp.take_along_axis(router_logits, route_rows, axis=1), axis=-1)
    token_valid = valid_mask.reshape(token_rows)
    gates = gate_soft * token_valid[:, None]
    route_ids = route_rows.reshape(-1)
    route_live = jnp.repeat(token_valid > 0.5, top_count)
    hits = (
        (route_ids[:, None] == jnp.arange(expert_total, dtype=jnp.int32)[None, :])
        & route_live[:, None]
    ).astype(jnp.int32)
    place = jnp.sum((jnp.cumsum(hits, axis=0) - hits) * hits, axis=1)
    dest = jnp.where(route_live, route_ids * CAP + place, expert_total * CAP)
    send_rows = (
        jnp.zeros((expert_total * CAP, model_width), jnp.bfloat16)
        .at[dest]
        .set(jnp.repeat(rows_two, top_count, axis=0), mode="drop")
    )
    received = to_owner(send_rows, expert_total)
    gate_part, up_part, hidden, result = experts_forward(received, w_gate, w_up, w_down)
    returned = to_source(result)
    route_out = (
        jnp.take(returned, dest, axis=0, mode="fill", fill_value=0)
        .reshape(token_rows, top_count, model_width)
        .astype(jnp.float32)
    )
    expert_mix = jnp.einsum("tk,tkd->td", gates, route_out)
    output = after_attn + expert_mix.reshape(slot_count, local_rows, model_width)
    difference = output - teacher.astype(jnp.float32)
    loss_part = jnp.sum(valid_mask[..., None] * difference * difference)
    grad_output = valid_mask[..., None] * difference * (positions_all / count_all)
    grad_rows = grad_output.reshape(token_rows, model_width)
    gate_grad_soft = jnp.einsum("tkd,td->tk", route_out, grad_rows) * token_valid[:, None]
    chosen_grad = gate_soft * (
        gate_grad_soft - jnp.sum(gate_soft * gate_grad_soft, axis=-1, keepdims=True)
    )
    route_grad = (
        (gates[:, :, None] * grad_rows[:, None, :]).astype(jnp.bfloat16).reshape(-1, model_width)
    )
    send_grads = (
        jnp.zeros((expert_total * CAP, model_width), jnp.bfloat16)
        .at[dest]
        .set(route_grad, mode="drop")
    )
    grad_recv = to_owner(send_grads, expert_total)
    hidden_grad = jnp.einsum("emd,efd->emf", grad_recv, w_down, preferred_element_type=jnp.float32)
    down_w_grad = jnp.einsum("emf,emd->efd", hidden, grad_recv, preferred_element_type=jnp.float32)
    sigma = jax.nn.sigmoid(gate_part)
    gate_grad = (hidden_grad * up_part * sigma * (1.0 + gate_part * (1.0 - sigma))).astype(
        jnp.bfloat16
    )
    up_grad = (hidden_grad * gate_part * sigma).astype(jnp.bfloat16)
    owner_input_grad = (
        jnp.einsum("emf,edf->emd", gate_grad, w_gate, preferred_element_type=jnp.float32)
        + jnp.einsum("emf,edf->emd", up_grad, w_up, preferred_element_type=jnp.float32)
    ).astype(jnp.bfloat16)
    gate_w_grad = jnp.einsum(
        "emd,emf->edf", received, gate_grad, preferred_element_type=jnp.float32
    )
    up_w_grad = jnp.einsum("emd,emf->edf", received, up_grad, preferred_element_type=jnp.float32)
    back_rows = to_source(owner_input_grad)
    expert_sums = (
        lax.psum(gate_w_grad.astype(jnp.bfloat16), "dp").astype(jnp.float32),
        lax.psum(up_w_grad.astype(jnp.bfloat16), "dp").astype(jnp.float32),
        lax.psum(down_w_grad.astype(jnp.bfloat16), "dp").astype(jnp.float32),
    )
    moe_input_grad = jnp.sum(
        jnp.take(back_rows, dest, axis=0, mode="fill", fill_value=0)
        .reshape(token_rows, top_count, model_width)
        .astype(jnp.float32),
        axis=1,
    )
    onehot_routes = (
        route_rows[:, :, None] == jnp.arange(expert_total, dtype=jnp.int32)[None, None, :]
    ).astype(jnp.float32)
    logit_grad = jnp.einsum("tk,tke->te", chosen_grad, onehot_routes).astype(jnp.bfloat16)
    router_grad = jnp.einsum("td,te->de", rows_two, logit_grad, preferred_element_type=jnp.float32)
    normed_two_grad = moe_input_grad + jnp.einsum(
        "te,de->td", logit_grad, w_router, preferred_element_type=jnp.float32
    )
    after_part, ffn_gain_grad = norm_two_pull(
        normed_two_grad.reshape(slot_count, local_rows, model_width)
    )
    after_grad = grad_output + after_part
    attn_grad = (
        (valid_mask[..., None] * after_grad).astype(jnp.bfloat16).reshape(token_rows, model_width)
    )
    out_w_grad = jnp.einsum(
        "tf,td->fd", joined_group_vectors, attn_grad, preferred_element_type=jnp.float32
    )
    mixed_grad = (
        jnp.einsum("td,fd->tf", attn_grad, w_out, preferred_element_type=jnp.float32)
        .astype(jnp.bfloat16)
        .reshape(head_shape)
    )

    def delta_step(index, total):
        weights_soft, unused_keys, value_blk = soft_block(index * block, block)
        pressure = jnp.einsum(
            "sqagd,sbad->sagqb", mixed_grad, value_blk, preferred_element_type=jnp.float32
        )
        return total + jnp.sum(weights_soft * pressure, axis=-1)

    delta = lax.fori_loop(0, block_count, delta_step, jnp.zeros(stat_shape, jnp.float32))

    def grad_parts(start, size):
        weights_soft, key_rows, value_blk = soft_block(start, size)
        pressure = jnp.einsum(
            "sqagd,sbad->sagqb", mixed_grad, value_blk, preferred_element_type=jnp.float32
        )
        score_grad = (weights_soft * (pressure - delta[..., None]) * 0.125).astype(jnp.bfloat16)
        return (weights_soft, score_grad, key_rows)

    def query_step(index, total):
        unused_soft, score_grad, key_rows = grad_parts(index * block, block)
        return total + jnp.einsum(
            "sagqb,sbad->sqagd", score_grad, key_rows, preferred_element_type=jnp.float32
        )

    query_grad_five = lax.fori_loop(0, block_count, query_step, jnp.zeros(head_shape, jnp.float32))
    count = lax.axis_size(("context", "experts")) * local_rows
    stride_length = 512

    def one_block(sub_start):
        weights_soft, score_grad, unused_keys = grad_parts(sub_start, stride_length)
        key_grad = jnp.einsum(
            "sagqb,sqagd->bsad", score_grad, query_five, preferred_element_type=jnp.float32
        )
        value_grad = jnp.einsum(
            "sagqb,sqagd->bsad",
            weights_soft.astype(jnp.bfloat16),
            mixed_grad,
            preferred_element_type=jnp.float32,
        )
        return jnp.concatenate(
            [
                key_grad.reshape(stride_length, slot_count, kv_width),
                value_grad.reshape(stride_length, slot_count, kv_width),
            ],
            axis=-1,
        )

    starts = stride_length * jnp.arange(count // stride_length, dtype=jnp.int32)
    kv_grad = jnp.transpose(
        lax.psum_scatter(
            lax.map(one_block, starts)
            .reshape(count, slot_count, 2 * kv_width)
            .astype(jnp.bfloat16),
            ("context", "experts"),
            scatter_dimension=0,
            tiled=True,
        ).astype(jnp.float32),
        (1, 0, 2),
    )
    query_rot_grad = rounded(query_grad_five.reshape(slot_count, local_rows, -1, head_size))
    query_raw_grad, query_gain_grad = query_pull(query_rot_grad)
    key_rot_grad = rounded(
        kv_grad[..., :kv_width].reshape(slot_count, local_rows, kv_heads, head_size)
    )
    key_raw_grad, key_gain_grad = key_pull(key_rot_grad)
    query_rows_grad = query_raw_grad.astype(jnp.bfloat16).reshape(token_rows, query_width)
    key_rows_grad = key_raw_grad.astype(jnp.bfloat16).reshape(token_rows, kv_width)
    value_rows_grad = kv_grad[..., kv_width:].astype(jnp.bfloat16).reshape(token_rows, kv_width)
    query_w_grad = jnp.einsum(
        "td,tf->df", rows_one, query_rows_grad, preferred_element_type=jnp.float32
    )
    key_w_grad = jnp.einsum(
        "td,tf->df", rows_one, key_rows_grad, preferred_element_type=jnp.float32
    )
    value_w_grad = jnp.einsum(
        "td,tf->df", rows_one, value_rows_grad, preferred_element_type=jnp.float32
    )
    normed_one_grad = jnp.einsum(
        "tf,df->td", query_rows_grad, w_query, preferred_element_type=jnp.float32
    )
    normed_one_grad = normed_one_grad + jnp.einsum(
        "tf,df->td", key_rows_grad, w_key, preferred_element_type=jnp.float32
    )
    normed_one_grad = normed_one_grad + jnp.einsum(
        "tf,df->td", value_rows_grad, w_value, preferred_element_type=jnp.float32
    )
    unused_norm, norm_one_pull = jax.vjp(rms_scale, inputs, attn_gain)
    input_part, attn_gain_grad = norm_one_pull(
        normed_one_grad.reshape(slot_count, local_rows, model_width)
    )
    input_grad = after_grad + input_part
    summed = lax.psum(
        (
            query_w_grad,
            key_w_grad,
            value_w_grad,
            out_w_grad,
            query_gain_grad,
            key_gain_grad,
            attn_gain_grad,
            ffn_gain_grad,
            router_grad,
            loss_part,
        ),
        ("dp", "context", "experts"),
    )
    loss_mean = summed[9] / (count_all * model_width)
    return (
        loss_mean,
        output.astype(jnp.bfloat16),
        input_grad,
        summed[0],
        summed[1],
        summed[2],
        summed[3],
        summed[4],
        summed[5],
        summed[6],
        summed[7],
        summed[8],
        expert_sums[0],
        expert_sums[1],
        expert_sums[2],
    )


def solution(mesh):
    return jax.shard_map(
        per_device,
        mesh=mesh,
        in_specs=(
            P("dp", ("context", "experts"), None),
            P("dp", ("context", "experts"), None),
            P(),
            P("dp", ("context", "experts"), None),
            P(),
            P(),
            P(),
            P(),
            P(),
            P(),
            P(),
            P(),
            P(),
            P(("context", "experts"), None, None),
            P(("context", "experts"), None, None),
            P(("context", "experts"), None, None),
        ),
        out_specs=(
            P(),
            P("dp", ("context", "experts"), None),
            P("dp", ("context", "experts"), None),
            P(),
            P(),
            P(),
            P(),
            P(),
            P(),
            P(),
            P(),
            P(),
            P(("context", "experts"), None, None),
            P(("context", "experts"), None, None),
            P(("context", "experts"), None, None),
        ),
        check_vma=False,
    )
```

profile of v0, /device:TPU:0, one launch (start us, length us, event | category | flops | bytes accessed | tf_op | source)
XLA Modules:
  0.0 1848.4 jit_solution(12182539223334786193)
XLA Ops:
  34.4 18.1 reduce-window.6
  63.0 20.3 %all-gather.2.cloned.1.call-done = bf16[4,1024,1024]{1,2,0:T(8,128)(2,1)} async-done(((bf16[4,128,1024]{1,2,0:T(8,128)(2,1)}), bf16[4,1024,1024]{1,2,0:T(8,128)(2,1)}) %all-gather.2.cloned.1.call-update) | async-done | bytes 8388624 | tf_op jit(solution)/shard_map/all_gather | solution.py:153
  83.3 39.8 %while.70 = (s32[]{:T(128)}, f32[4,8,2,128]{3,2,1,0:T(2,128)S(1)}, f32[4,8,2,128]{3,2,1,0:T(2,128)S(1)}, s32[4]{0:T(128)}, bf16[4,1024,1024]{1,2,0:T(8,128)(2,1)...) while((s32[]{:T(128)}, f32[4,8,2,128]{3,2,1,0:T(2,128)S(1)}, ...), condition=%wide.region_6.0_spmd.clone, body=%wide.region_3.6_spmd.clone.sunk | while | flops 566602368 | bytes 42249408 | solution.py:167
  123.1 29.0 %while.71 = (s32[]{:T(128)}, f32[4,128,8,2,64]{1,4,3,2,0:T(8,128)}, bf16[4,1024,1024]{1,2,0:T(8,128)(2,1)}, s32[4]{0:T(128)}, bf16[4,128,8,2,64]{1,4,3,2,0:T(8,1...) while((s32[]{:T(128)}, f32[4,128,8,2,64]{1,4,3,2,0:T(8,128)}, ...), condition=%wide.region_8.9_spmd.clone, body=%wide.region_7.8_spmd.clone.sunk | while | flops 1091897984 | bytes 18525400 | solution.py:192
  159.0 24.7 %scatter_custom_fusion = bf16[5120,1024]{1,0:T(8,128)(2,1)} fusion(s32[4096]{0:T(1024)} %bitcast.533, bf16[]{:T(256)} %constant.286.clone.1, bf16[512,1024]{1,0:T(8,128)(2,1)S(1)} %bitcast.485), kind=kCustom, calls=%fused_computation.113 | custom fusion | bytes 11534848 | tf_op jit(solution)/shard_map/scatter | solution.py:216
  183.8 122.1 %all_to_all.66 = bf16[32,160,1024]{2,1,0:T(8,128)(2,1)} all-to-all(bf16[32,160,1024]{2,1,0:T(8,128)(2,1)} %bitcast.478), channel_id=1, replica_groups=mesh['dp'=4,'context'=4,'experts'=2] {'context','experts'}, dimensions={0} | all-to-all | bytes 20971520 | tf_op jit(solution)/shard_map/all_to_all | solution.py:66
  315.8 12.0 fusion.128
  327.9 16.1 multiply_convert_fusion.2
  352.3 28.2 %copy.238 = bf16[4,1280,1024]{2,0,1:T(4,128)(2,1)} copy(bf16[4,1280,1024]{2,1,0:T(8,128)(2,1)S(1)} %convolution_convert_fusion) | data formatting | bytes 20971520 | tf_op jit(solution)/shard_map/convert_element_type | solution.py:82
  389.3 33.0 %gather_fusion = f32[4096]{0:T(1024)S(1)} fusion(f32[512,32]{0,1:T(8,128)S(1)} %fusion.127, s32[4096]{0:T(1024)S(1)} %reshape.951), kind=kCustom, calls=%fused_computation.2 | custom fusion | bytes 65536 | tf_op jit(solution)/shard_map/jit(take_along_axis)/gather | solution.py:202
  423.7 78.0 %all-to-all-done.1 = bf16[4,1280,1024]{2,0,1:T(4,128)(2,1)} async-done(((bf16[4,1280,1024]{2,0,1:T(4,128)(2,1)}), bf16[4,1280,1024]{2,0,1:T(4,128)(2,1)}, u32[]{:S(2)}, u32[]{:S(2)}) %all-to-all-start.1) | async-done | bytes 10485792 | tf_op jit(solution)/shard_map/all_to_all | solution.py:72
  501.7 12.0 copy.239
  513.6 26.1 %gather_fusion.1 = bf16[4096,1024]{1,0:T(8,128)(2,1)} fusion(bf16[5120,1024]{1,0:T(8,128)(2,1)} %bitcast.463, s32[4096]{0:T(1024)S(1)} %broadcast_clamp_fusion), kind=kCustom, calls=%fused_computation.clone | custom fusion | bytes 16793600 | tf_op jit(solution)/shard_map/jit(_take)/gather | solution.py:222
  549.3 26.2 %scatter_custom_fusion.1 = bf16[5120,1024]{1,0:T(8,128)(2,1)} fusion(s32[4096]{0:T(1024)} %bitcast.534, f32[512,1024]{1,0:T(8,128)} %bitcast.500, f32[4096]{0:T(1024)S(1)} %divide_multiply_fusion, bf16[]{:T(256)} %constant.286.clone.1), kind=kCustom, calls=%fused_computation.108 | custom fusion | flops 8388608 | bytes 12599808 | tf_op jit(solution)/shard_map/scatter | solution.py:242
  575.5 122.1 %all_to_all.67 = bf16[32,160,1024]{2,1,0:T(8,128)(2,1)} all-to-all(bf16[32,160,1024]{2,1,0:T(8,128)(2,1)} %bitcast.475), channel_id=1, replica_groups=mesh['dp'=4,'context'=4,'experts'=2] {'context','experts'}, dimensions={0} | all-to-all | bytes 20971520 | tf_op jit(solution)/shard_map/all_to_all | solution.py:66
  707.5 17.9 multiply_convert_fusion
  725.3 13.3 fusion.129
  738.6 15.0 add_convert_fusion
  753.6 14.6 copy.244
  784.2 104.8 %all-to-all-done.3 = bf16[4,1280,1024]{2,0,1:T(4,128)(2,1)} async-done(((bf16[4,1280,1024]{2,0,1:T(4,128)(2,1)}), bf16[4,1280,1024]{2,0,1:T(4,128)(2,1)}, u32[]{:S(2)}, u32[]{:S(2)}) %all-to-all-start.3) | async-done | bytes 10485792 | tf_op jit(solution)/shard_map/all_to_all | solution.py:72
  900.9 26.1 %gather_fusion.2 = bf16[4096,1024]{1,0:T(8,128)(2,1)} fusion(bf16[5120,1024]{1,0:T(8,128)(2,1)} %bitcast.462, s32[4096]{0:T(1024)S(1)} %broadcast_clamp_fusion), kind=kCustom, calls=%fused_computation.1.clone | custom fusion | bytes 16793600 | tf_op jit(solution)/shard_map/jit(_take)/gather | solution.py:267
  953.7 23.2 %while.72 = (s32[]{:T(128)}, f32[4,8,2,128]{3,2,1,0:T(2,128)S(1)}, s32[4]{0:T(128)}, bf16[4,1024,1024]{1,2,0:T(8,128)(2,1)}, bf16[4,128,8,2,64]{1,4,3,2,0:T(8,12...) while((s32[]{:T(128)}, f32[4,8,2,128]{3,2,1,0:T(2,128)S(1)}, ...), condition=%wide.region_25.27_spmd.clone, body=%wide.region_23.26_spmd.clone.sunk | while | flops 1095051904 | bytes 53259512 | solution.py:303
  976.9 92.8 %while.69 = (s32[]{:T(128)}, bf16[2,512,4,1024]{1,3,2,0:T(8,128)(2,1)}, s32[2]{0:T(128)S(1)}, s32[4]{0:T(128)}, bf16[4,1024,1024]{1,2,0:T(8,128)(2,1)}, /*index=...) while((s32[]{:T(128)}, ...), condition=%wide.region_30.32_spmd.clone, body=%wide.region_29.31_spmd.clone.sunk | while | flops 2202339840 | bytes 84913912 | solution.py:345
  996.7 12.1 fusion.232
  1042.6 12.1 fusion.232
  1092.6 12.8 convolution_convert_fusion.2
  1116.8 58.8 %while.73 = (s32[]{:T(128)}, f32[4,128,8,2,64]{1,4,3,2,0:T(8,128)}, bf16[4,1024,1024]{1,2,0:T(8,128)(2,1)}, s32[4]{0:T(128)}, bf16[4,128,8,2,64]{1,4,3,2,0:T(8,1...) while((s32[]{:T(128)}, f32[4,128,8,2,64]{1,4,3,2,0:T(8,128)}, ...), condition=%wide.region_27.29_spmd.clone, body=%wide.region_26.28_spmd.clone.sunk | while | flops 1641351808 | bytes 57355524 | solution.py:319
  1130.6 14.8 bitcast_add_fusion.5
  1158.9 16.4 bitcast_add_fusion.5
  1201.7 381.9 %all-reduce.12.cloned.1.call-done = (bf16[4,1024,512]{2,1,0:T(8,128)(2,1)}, bf16[4,1024,512]{2,1,0:T(8,128)(2,1)}, bf16[4,512,1024]{2,1,0:T(8,128)(2,1)}) async-done(((bf16[4,1024,512]{2,1,0:T(8,128)(2,1)}, bf16[4,1024,512]{2,1,0:T(8,128)(2,1)}, bf16[4,512,1024]{2,1,0:T(8,128)(2,1)}), (bf16[4,1024,512]{2,1,0:T(8,128)(2,1)}, bf16[4,1024,512]{2,1,0:T(8,128)(2,1)}, ...) | async-done | bytes 12582928 | tf_op jit(solution)/shard_map/psum | solution.py:262
  1603.0 40.8 %all-reduce.4 = (f32[]{:T(128)}, f32[64]{0:T(128)}, f32[64]{0:T(128)}, f32[1024]{0:T(1024)}, f32[1024]{0:T(1024)}) all-reduce(f32[]{:T(128)} %get-tuple-element.926, f32[64]{0:T(128)S(1)} %get-tuple-element.923, f32[64]{0:T(128)S(1)} %get-tuple-element.928, ...), channel_id=1, replica_groups=mesh['dp'=4,'context'=4,'experts'=2] {'dp','context','experts'}, use_global_device_ids=true, to_apply=%region_17.19 | all-reduce | flops 2177 | bytes 17416 | tf_op jit(solution)/shard_map/psum | solution.py:386
  1647.9 181.0 %all-reduce.10.cloned.1.call-done = (f32[1024,1024]{1,0:T(8,128)}, f32[1024,512]{1,0:T(8,128)}, f32[1024,512]{1,0:T(8,128)}, f32[1024,1024]{1,0:T(8,128)}, f32[1024,32]{0,1:T(8,128)}) async-done(((f32[1024,1024]{1,0:T(8,128)}, f32[1024,512]{1,0:T(8,128)}, f32[1024,512]{1,0:T(8,128)}, f32[1024,1024]{1,0:T(8,128)}, f32[1024,32]{0,1:T(8,128)}), (f32[1024,1024]{1,0:T(8,128)}, f32[1024,512]{1,0:T(8,128)}, ...) | async-done | bytes 12714000 | tf_op jit(solution)/shard_map/psum | solution.py:386
  (442 shorter events, 421.8 us)
Async XLA Ops:
  7.2 147.2 %copy-start = (bf16[1024,1024]{1,0:T(8,128)(2,1)S(1)}, bf16[1024,1024]{1,0:T(8,128)(2,1)}, u32[]{:S(2)}) copy-start(bf16[1024,1024]{1,0:T(8,128)(2,1)} %param.35) | copy-start | bytes 6291460
  7.2 76.1 %all-gather.2.cloned.1.call-start = ((), (), s32[]{:S(2)}) async-start(), calls=%async_computation.5 | async-start | bytes 9437184 | tf_op jit(solution)/shard_map/all_gather | solution.py:153
  13.3 42.1 %copy-start.17 = (bf16[4,128,1024]{2,1,0:T(8,128)(2,1)}, bf16[4,128,1024]{2,1,0:T(8,128)(2,1)S(1)}, u32[]{:S(2)}) copy-start(bf16[4,128,1024]{2,1,0:T(8,128)(2,1)S(1)} %fusion.67) | copy-start | bytes 3145732
  13.3 8.4 copy-start.86
  16.8 9.4 copy-start.88
  21.7 37.9 %copy-start.47 = (f32[128,32]{0,1:T(8,128)}, f32[128,32]{0,1:T(8,128)S(1)}, u32[]{:S(2)}) copy-start(f32[128,32]{0,1:T(8,128)S(1)} %get-tuple-element.1056) | copy-start | bytes 49156
  21.7 37.9 %copy-start.49 = (f32[128,32]{0,1:T(8,128)}, f32[128,32]{0,1:T(8,128)S(1)}, u32[]{:S(2)}) copy-start(f32[128,32]{0,1:T(8,128)S(1)} %get-tuple-element.1057) | copy-start | bytes 49156
  61.0 22.3 %copy-start.56 = (s32[4096]{0:T(1024)}, s32[4096]{0:T(1024)S(1)}, u32[]{:S(2)}) copy-start(s32[4096]{0:T(1024)S(1)} %fusion.100) | copy-start | bytes 49156
  62.3 92.1 %copy-start.58 = (f32[4,128]{1,0:T(4,128)}, f32[4,128]{1,0:T(4,128)S(1)}, u32[]{:S(2)}) copy-start(f32[4,128]{1,0:T(4,128)S(1)} %get-tuple-element.1055) | copy-start | bytes 6148
  159.0 229.0 %copy-start.15 = (bf16[4,128,1024]{2,1,0:T(8,128)(2,1)}, bf16[4,128,1024]{2,1,0:T(8,128)(2,1)S(1)}, u32[]{:S(2)}) copy-start(bf16[4,128,1024]{2,1,0:T(8,128)(2,1)S(1)} %multiply_convert_fusion.4) | copy-start | bytes 3145732
  315.8 12.0 copy-start.24
  327.9 16.1 copy-start.90
  380.5 7.4 copy-start.52
  380.5 7.4 copy-start.57
  380.5 7.4 copy-start.65
  380.5 121.1 %all-to-all-start.1 = ((bf16[4,1280,1024]{2,0,1:T(4,128)(2,1)}), bf16[4,1280,1024]{2,0,1:T(4,128)(2,1)}, u32[]{:S(2)}, u32[]{:S(2)}) async-start(bf16[4,1280,1024]{2,0,1:T(4,128)(2,1)} %copy.238), calls=%async_computation.1 | async-start | bytes 20971520 | tf_op jit(solution)/shard_map/all_to_all | solution.py:72
  768.2 120.8 %all-to-all-start.3 = ((bf16[4,1280,1024]{2,0,1:T(4,128)(2,1)}), bf16[4,1280,1024]{2,0,1:T(4,128)(2,1)}, u32[]{:S(2)}, u32[]{:S(2)}) async-start(bf16[4,1280,1024]{2,0,1:T(4,128)(2,1)} %copy.244), calls=%async_computation.3 | async-start | bytes 20971520 | tf_op jit(solution)/shard_map/all_to_all | solution.py:72
  773.4 414.9 %reduce-scatter.2.cloned.1.call-start = ((), (), s32[]{:S(2)}) async-start(), calls=%async_computation.6 | async-start | bytes 9437184 | tf_op jit(solution)/shard_map/reduce_scatter | solution.py:344
  784.2 150.4 %copy-start.35 = (bf16[512,32]{1,0:T(8,128)(2,1)}, bf16[512,32]{1,0:T(8,128)(2,1)S(1)}, u32[]{:S(2)}) copy-start(bf16[512,32]{1,0:T(8,128)(2,1)S(1)} %copy.284) | copy-start | bytes 98308
  927.0 7.6 copy-start.55
  945.5 8.2 copy-start.3
  945.5 8.2 copy-start.76
  996.7 12.1 copy-start.5
  1042.6 12.1 copy-start.5
  1081.1 502.6 %all-reduce.12.cloned.1.call-start = ((), (), s32[]{:S(2)}) async-start(), calls=%async_computation.8 | async-start | bytes 25165824 | tf_op jit(solution)/shard_map/psum | solution.py:262
  1081.1 24.3 %slice-start = ((s8[10485760]{0:T(1024)(128)(4,1)}), s8[2097152]{0:T(1024)(128)(4,1)S(1)}, s32[]{:S(2)}) async-start(s8[10485760]{0:T(1024)(128)(4,1)} %bitcast.491), calls=%async_computation.9 | async-start | bytes 4194304
  1081.1 24.3 %slice-start.1 = ((s8[10485760]{0:T(1024)(128)(4,1)}), s8[4194304]{0:T(1024)(128)(4,1)S(1)}, s32[]{:S(2)}) async-start(s8[10485760]{0:T(1024)(128)(4,1)} %bitcast.491), calls=%async_computation.10 | async-start | bytes 8388608
  1081.2 24.3 %slice-start.3 = ((s8[5242880]{0:T(1024)(128)(4,1)}), s8[4194304]{0:T(1024)(128)(4,1)S(1)}, s32[]{:S(2)}) async-start(s8[5242880]{0:T(1024)(128)(4,1)} %bitcast.502), calls=%async_computation.12 | async-start | bytes 8388608
  1092.6 12.8 slice-start.2
  1092.6 12.8 slice-start.4
  1112.7 716.3 %all-reduce.10.cloned.1.call-start = ((), (), s32[]{:S(2)}) async-start(), calls=%async_computation.7 | async-start | bytes 25427968 | tf_op jit(solution)/shard_map/psum | solution.py:386
  1602.2 42.2 %copy-start.80 = (f32[4,128]{1,0:T(4,128)S(1)}, f32[4,128]{1,0:T(4,128)}, u32[]{:S(2)}) copy-start(f32[4,128]{1,0:T(4,128)} %copy-done.79) | copy-start | bytes 6148
  (75 other events, 219.4 us)
Sparse Core Ops, SparseCore 0:
  24.6 58.6 all-gather.1
  1081.2 71.2 reduce-scatter.1
  1156.1 427.4 all-reduce.11
  1592.2 236.6 all-reduce.9
where the time goes:
time: 1860 us; the launch traced here: 1850 us
  waiting for transfers between devices  766 us (41%)
  matrix products  318 us (17%)
  local copies, waits for them, and re-layouts  304 us (16%)
  blocking collectives  285 us (15%)
  other arithmetic  141 us (8%)
    psum x1, waiting for transfers between devices, per_device(): lax.psum(gate_w_grad.astype(jnp.bfloat16), 'dp').astype(jnp.float32)  382 us
    all_to_all x2, blocking collectives, to_owner(): lax.all_to_all(shaped, ('context', 'experts'), split_axis=0, concat_axis=...  244 us
    all_to_all x2, waiting for transfers between devices, to_source(): lax.all_to_all(owner_rows, ('context', 'experts'), split_axis=1, concat_a...  183 us
    psum x1, waiting for transfers between devices, per_device(): lax.psum((query_w_grad, key_w_grad, value_w_grad, out_w_grad, query_gain_...  181 us
    dot_general x6, matrix products, score_block(): jnp.einsum('sqagd,sbad->sagqb', query_five, key_rows, preferred_element_t...  41.3 us
    psum x1, blocking collectives, per_device(): lax.psum((query_w_grad, key_w_grad, value_w_grad, out_w_grad, query_gain_...  40.8 us
  transfers between devices with their start and end apart: 6, of which 5 were waited for; matrix products, arithmetic and copies ran while one was open for 12% of the time, Pallas kernels for 0%

commit v1 on v0

v1 whole, which is shorter than its diff:
```python
import functools
import math

import jax
import jax.numpy as jnp
from jax import lax
from jax.experimental import pallas as pl
from jax.experimental.pallas import tpu as pltpu
from jax.sharding import PartitionSpec as P

EPSILON = 1e-06
MOST = 40
PAIR = 2 * MOST
LANES = 128
HEAD = 64
SCALE = 0.125
EXP2_SCALE = 0.125 * math.log2(math.e)
MIB = 2**20
MESH = pl.DeviceIdType.MESH
F32 = jnp.float32
BF16 = jnp.bfloat16


def dot(a, b):
    return lax.dot_general(a, b, (((1,), (0,)), ((), ())), preferred_element_type=F32)


def dot_nt(a, b):
    return lax.dot_general(a, b, (((1,), (1,)), ((), ())), preferred_element_type=F32)


def dot_tn(a, b):
    return lax.dot_general(a, b, (((0,), (0,)), ((), ())), preferred_element_type=F32)


def lane_of(shape):
    return lax.broadcasted_iota(jnp.int32, shape, len(shape) - 1)


def row_of(shape):
    return lax.broadcasted_iota(jnp.int32, shape, len(shape) - 2)


def swap_halves(tile):
    low = lax.rem(lane_of(tile.shape), HEAD) < HEAD // 2
    return jnp.where(low, pltpu.roll(tile, LANES - HEAD // 2, 1), pltpu.roll(tile, HEAD // 2, 1))


def head_mean(tile):
    low = lane_of(tile.shape) < HEAD
    first = jnp.sum(jnp.where(low, tile, 0.0), axis=-1, keepdims=True)
    second = jnp.sum(jnp.where(low, 0.0, tile), axis=-1, keepdims=True)
    return jnp.where(low, first, second) * (1.0 / HEAD)


def rope_forward(raw, gain, cosine, sine):
    normed = raw * lax.rsqrt(head_mean(raw * raw) + EPSILON) * gain
    return normed * cosine + swap_halves(normed) * sine


def rope_backward(grad, raw, gain, cosine, sine):
    inverse = lax.rsqrt(head_mean(raw * raw) + EPSILON)
    unit = raw * inverse
    normed_grad = grad * cosine - swap_halves(grad) * sine
    gain_grad = jnp.sum(normed_grad * unit, axis=0, keepdims=True)
    unit_grad = normed_grad * gain
    return inverse * (unit_grad - unit * head_mean(unit_grad * unit)), gain_grad


def rms_parts(rows):
    inverse = lax.rsqrt(jnp.mean(rows * rows, axis=-1, keepdims=True) + EPSILON)
    return rows * inverse, inverse


def rms_backward(grad, rows, gain):
    unit, inverse = rms_parts(rows)
    gain_grad = jnp.sum(grad * unit, axis=0, keepdims=True)
    unit_grad = grad * gain
    back = inverse * (unit_grad - unit * jnp.mean(unit_grad * unit, axis=-1, keepdims=True))
    return back, gain_grad


def stack_heads(tile, masked):
    first, second = tile[:, :LANES].astype(F32), tile[:, LANES:].astype(F32)
    parts = [first, pltpu.roll(first, HEAD, 1), pltpu.roll(second, HEAD, 1), second]
    if masked:
        low = lane_of(first.shape) < HEAD
        parts = [jnp.where(low, part, 0.0) for part in parts[:2]] + [
            jnp.where(low, 0.0, part) for part in parts[2:]
        ]
    return jnp.concatenate(parts, axis=0)


def unstack_heads(rows):
    count = rows.shape[0] // 4
    one, two, three, four = (rows[k * count : (k + 1) * count] for k in range(4))
    low = lane_of(one.shape) < HEAD
    return jnp.concatenate(
        [
            jnp.where(low, one, pltpu.roll(two, HEAD, 1)),
            jnp.where(low, pltpu.roll(three, HEAD, 1), four),
        ],
        axis=1,
    )


def project_kernel(
    x_ref, gain_ref, wq_ref, wk_ref, wv_ref, qg_ref, kg_ref, cos_ref, sin_ref,
    h_ref, q_ref, kv_ref, qraw_ref, kraw_ref,
):
    slots, rows, width = x_ref.shape
    x = x_ref[...].astype(F32).reshape(slots * rows, width)
    unit, unused = rms_parts(x)
    normed = (unit * gain_ref[...]).astype(BF16)
    h_ref[...] = normed.reshape(slots, rows, width)
    cosine = jnp.concatenate([cos_ref[...]] * slots, axis=0)
    sine = jnp.concatenate([sin_ref[...]] * slots, axis=0)
    q_raw = dot(normed, wq_ref[...])
    qraw_ref[...] = q_raw.reshape(qraw_ref.shape)
    for tile in range(q_raw.shape[1] // LANES):
        lanes = slice(tile * LANES, (tile + 1) * LANES)
        turned = rope_forward(q_raw[:, lanes], qg_ref[...], cosine, sine)
        q_ref[:, :, lanes] = turned.astype(BF16).reshape(slots, rows, LANES)
    k_raw = dot(normed, wk_ref[...])
    kraw_ref[...] = k_raw.reshape(kraw_ref.shape)
    value = dot(normed, wv_ref[...]).astype(BF16)
    for tile in range(k_raw.shape[1] // LANES):
        lanes = slice(tile * LANES, (tile + 1) * LANES)
        turned = rope_forward(k_raw[:, lanes], kg_ref[...], cosine, sine)
        at = 2 * tile * LANES
        kv_ref[:, :, at : at + LANES] = turned.astype(BF16).reshape(slots, rows, LANES)
        kv_ref[:, :, at + LANES : at + 2 * LANES] = value[:, lanes].reshape(slots, rows, LANES)


def project(x, attn_gain, w_query, w_key, w_value, qg, kg, cosine, sine):
    slots, rows, width = x.shape
    step = 2
    block = lambda lanes: pl.BlockSpec((step, rows, lanes), lambda i: (i, 0, 0))
    whole = lambda a: pl.BlockSpec(a.shape, lambda i: (0,) * a.ndim)
    qw, kw = w_query.shape[1], w_key.shape[1]
    return pl.pallas_call(
        project_kernel,
        grid=(slots // step,),
        out_shape=(
            jax.ShapeDtypeStruct((slots, rows, width), BF16),
            jax.ShapeDtypeStruct((slots, rows, qw), BF16),
            jax.ShapeDtypeStruct((slots, rows, 2 * kw), BF16),
            jax.ShapeDtypeStruct((slots, rows, qw), F32),
            jax.ShapeDtypeStruct((slots, rows, kw), F32),
        ),
        in_specs=[block(width)] + [whole(a) for a in (attn_gain, w_query, w_key, w_value, qg, kg, cosine, sine)],
        out_specs=(block(width), block(qw), block(2 * kw), block(qw), block(kw)),
        compiler_params=pltpu.CompilerParams(vmem_limit_bytes=56 * MIB),
        name="project",
    )(x, attn_gain, w_query, w_key, w_value, qg, kg, cosine, sine)


def attend_kernel(
    sc_ref, q_ref, kv_ref, x_ref, wo_ref, fg_ref, wr_ref, routes_ref,
    mixed_ref, invl_ref, after_ref, xg_ref, soft_ref, acc,
):
    slot, tile = pl.program_id(0), pl.program_id(1)
    slots, tiles = pl.num_programs(0), pl.num_programs(1)
    rows = q_ref.shape[1]
    here = sc_ref[slots]
    length = sc_ref[slot]
    live = here * rows < length
    chunk = 2 * rows
    chunks = (here + 2) // 2

    @pl.when(tile == 0)
    def _():
        acc[...] = jnp.zeros_like(acc)

    @pl.when(live)
    def _():
        q4 = stack_heads(q_ref[0], True).astype(BF16)

        def step(index, carry, masked):
            mass, total = carry
            pair = kv_ref[pl.ds(2 * index, 2), 0]
            keys = pair[:, :, :LANES].reshape(chunk, LANES)
            values = pair[:, :, LANES:].reshape(chunk, LANES)
            weight = jnp.exp2(dot_nt(q4, keys) * EXP2_SCALE)
            if masked:
                at = lax.rem(row_of(weight.shape), rows) + here * rows
                weight = jnp.where(lane_of(weight.shape) + index * chunk <= at, weight, 0.0)
            for part in range(chunk // LANES):
                mass = mass + weight[:, part * LANES : (part + 1) * LANES]
            return mass, total + dot(weight.astype(BF16), values)

        blank = jnp.zeros((4 * rows, LANES), F32)
        carry = lax.fori_loop(0, chunks - 1, lambda i, c: step(i, c, False), (blank, blank))
        mass, total = step(chunks - 1, carry, True)
        inverse = 1.0 / jnp.sum(mass, axis=-1, keepdims=True)
        mixed = unstack_heads(total * inverse).astype(BF16)
        mixed_ref[0] = mixed
        invl_ref[0] = unstack_heads(jnp.broadcast_to(inverse, total.shape))
        acc[...] += dot(mixed, wo_ref[...])

    @pl.when(jnp.logical_not(live))
    def _():
        mixed_ref[...] = jnp.zeros_like(mixed_ref)
        invl_ref[...] = jnp.zeros_like(invl_ref)

    @pl.when(tile == tiles - 1)
    def _():
        width = x_ref.shape[2]
        valid = (row_of((rows, 1)) + here * rows < length).astype(F32)
        after = x_ref[0].astype(F32) + valid * acc[...]
        after_ref[0] = after
        unit, unused = rms_parts(after)
        normed = (unit * fg_ref[...]).astype(BF16)
        xg_ref[0, :, :width] = normed
        logits = dot(normed, wr_ref[...])
        lanes = lane_of(logits.shape)
        routes = routes_ref[0]
        chosen = lanes == routes[:, 0:1]
        for k in range(1, routes.shape[1]):
            chosen = chosen | (lanes == routes[:, k : k + 1])
        top = jnp.max(jnp.where(chosen, logits, -1e30), axis=-1, keepdims=True)
        weight = jnp.where(chosen, jnp.exp(jnp.minimum(logits - top, 0.0)), 0.0)
        soft = weight / jnp.sum(weight, axis=-1, keepdims=True)
        soft_ref[0] = soft
        gates = soft * valid
        high = gates.astype(BF16).astype(F32)
        half = logits.shape[1] // 2
        xg_ref[0, :, width:] = (high + pltpu.roll(gates - high, half, 1)).astype(BF16)


def attend(scalars, q, kv, x, w_out, ffn_gain, router, routes):
    slots, rows, width = x.shape
    group = kv.shape[0]
    qw = q.shape[2]
    tiles = qw // 256
    row = lambda lanes: pl.BlockSpec((1, rows, lanes), lambda s, b, sc: (s, 0, 0))
    tile = pl.BlockSpec((1, rows, 256), lambda s, b, sc: (s, 0, b))
    return pl.pallas_call(
        attend_kernel,
        grid_spec=pltpu.PrefetchScalarGridSpec(
            num_scalar_prefetch=1,
            grid=(slots, tiles),
            in_specs=[
                tile,
                pl.BlockSpec((group, 1, rows, 256), lambda s, b, sc: (0, s, 0, b)),
                row(width),
                pl.BlockSpec((256, width), lambda s, b, sc: (b, 0)),
                pl.BlockSpec(ffn_gain.shape, lambda s, b, sc: (0, 0)),
                pl.BlockSpec(router.shape, lambda s, b, sc: (0, 0)),
                row(routes.shape[2]),
            ],
            out_specs=(tile, tile, row(width), row(width + LANES), row(LANES)),
            scratch_shapes=[pltpu.VMEM((rows, width), F32)],
        ),
        out_shape=(
            jax.ShapeDtypeStruct((slots, rows, qw), BF16),
            jax.ShapeDtypeStruct((slots, rows, qw), F32),
            jax.ShapeDtypeStruct((slots, rows, width), F32),
            jax.ShapeDtypeStruct((slots, rows, width + LANES), BF16),
            jax.ShapeDtypeStruct((slots, rows, LANES), F32),
        ),
        compiler_params=pltpu.CompilerParams(vmem_limit_bytes=56 * MIB),
        name="attend",
    )(scalars, q, kv, x, w_out, ffn_gain, router, routes)


def row_gates(picked, first, owned):
    lanes = lane_of(picked.shape)
    expert = row_of(picked.shape) // PAIR + first
    half = picked.shape[1] // 2
    mine = (lanes == expert) | (lanes == expert + half)
    return jnp.sum(jnp.where(mine, picked, 0.0), axis=-1, keepdims=True)


def experts_forward_kernel(
    sc_ref, xg_ref, wg_ref, wu_ref, wd_ref, pick_ref, xe_ref, gp_ref, up_ref, hid_ref, part_ref, gates, ybuf
):
    sources, unused, rows, wide = xg_ref.shape
    owned, width, eff = wg_ref.shape
    pairs = sources // 2
    double = 2 * rows
    first = sc_ref[pl.num_programs(0)] * owned
    tokens = xg_ref[...].reshape(sources * rows, wide)
    slab = tokens[:, width:]
    chosen = (lane_of((8, LANES)) == row_of((8, LANES)) + first).astype(BF16)
    routed = dot_nt(chosen, slab) > 0.0
    before = row_of((double, double))
    after = lane_of((double, double))
    count = ((before < after) & (before // rows == after // rows)).astype(BF16)
    place = lax.broadcasted_iota(jnp.int32, (PAIR, double), 0)
    offset = (lane_of((8, double)) // rows) * MOST
    for p in range(pairs):
        mask = routed[:, p * double : (p + 1) * double]
        rank = dot(mask.astype(F32).astype(BF16), count).astype(jnp.int32) + offset
        rank = jnp.where(mask, rank, -1)
        pick = jnp.concatenate(
            [(place == rank[e : e + 1, :]).astype(F32).astype(BF16) for e in range(owned)], axis=0
        )
        pick_ref[0, p] = pick
        block = tokens[p * double : (p + 1) * double]
        picked = dot(pick, block[:, :width]).astype(BF16)
        scale = row_gates(dot(pick, block[:, width:]), first, owned)
        for e in range(owned):
            xe_ref[0, e, p * PAIR : (p + 1) * PAIR] = picked[e * PAIR : (e + 1) * PAIR]
            gates[e, p * PAIR : (p + 1) * PAIR] = jnp.broadcast_to(
                scale[e * PAIR : (e + 1) * PAIR], (PAIR, LANES)
            )

    def one(e, carry):
        rows_in = xe_ref[0, e]
        gate_part = dot(rows_in, wg_ref[e])
        up_part = dot(rows_in, wu_ref[e])
        gp_ref[0, e] = gate_part
        up_ref[0, e] = up_part
        hidden = (gate_part * jax.nn.sigmoid(gate_part) * up_part).astype(BF16)
        hid_ref[0, e] = hidden
        result = (dot(hidden, wd_ref[e]) * gates[e][:, 0:1]).astype(BF16)
        for p in range(pairs):
            ybuf[p, e] = result[p * PAIR : (p + 1) * PAIR]
        return carry

    lax.fori_loop(0, owned, one, 0)
    for p in range(pairs):
        back = dot_tn(pick_ref[0, p], ybuf[p].reshape(owned * PAIR, width))
        part_ref[2 * p : 2 * p + 2, 0] = back.astype(BF16).reshape(2, rows, width)


def step_spec(shape):
    return pl.BlockSpec((1,) + shape, lambda s, j, sc: (s * pl.num_programs(1) + j,) + (0,) * len(shape))


def resident(array):
    return pl.BlockSpec(array.shape, lambda s, j, sc: (0,) * array.ndim, pipeline_mode=pl.Buffered(1))


def experts_forward(scalars, tokens, w_gate, w_up, w_down):
    group, slots, rows, wide = tokens.shape
    owned, width, eff = w_gate.shape
    sources = 8
    parts = group // sources
    pairs = sources // 2
    steps = slots * parts
    held = pairs * PAIR
    source = lambda lanes: pl.BlockSpec((sources, 1, rows, lanes), lambda s, j, sc: (j, s, 0, 0))
    saved = [
        ((pairs, owned * PAIR, 2 * rows), BF16),
        ((owned, held, width), BF16),
        ((owned, held, eff), F32),
        ((owned, held, eff), F32),
        ((owned, held, eff), BF16),
    ]
    return pl.pallas_call(
        experts_forward_kernel,
        grid_spec=pltpu.PrefetchScalarGridSpec(
            num_scalar_prefetch=1,
            grid=(slots, parts),
            in_specs=[source(wide), resident(w_gate), resident(w_up), resident(w_down)],
            out_specs=tuple(step_spec(shape) for shape, unused in saved) + (source(width),),
            scratch_shapes=[
                pltpu.VMEM((owned, held, LANES), F32),
                pltpu.VMEM((pairs, owned, PAIR, width), BF16),
            ],
        ),
        out_shape=tuple(jax.ShapeDtypeStruct((steps,) + shape, kind) for shape, kind in saved)
        + (jax.ShapeDtypeStruct((group, slots, rows, width), BF16),),
        compiler_params=pltpu.CompilerParams(vmem_limit_bytes=60 * MIB),
        name="experts_forward",
    )(scalars, tokens, w_gate, w_up, w_down)


def experts_backward_kernel(
    sc_ref, dy_ref, slab_ref, pick_ref, gp_ref, up_ref, hid_ref, wg_ref, wu_ref, wd_ref,
    part_ref, dyw_ref, gg_ref, ug_ref, gates, dye, dxb,
):
    sources, unused, rows, width = dy_ref.shape
    owned = wg_ref.shape[0]
    pairs = sources // 2
    double = 2 * rows
    first = sc_ref[pl.num_programs(0)] * owned
    for p in range(pairs):
        pick = pick_ref[0, p]
        picked = dot(pick, dy_ref[2 * p : 2 * p + 2].reshape(double, width)).astype(BF16)
        scale = row_gates(dot(pick, slab_ref[2 * p : 2 * p + 2].reshape(double, LANES)), first, owned)
        for e in range(owned):
            dye[e, p * PAIR : (p + 1) * PAIR] = picked[e * PAIR : (e + 1) * PAIR]
            gates[e, p * PAIR : (p + 1) * PAIR] = jnp.broadcast_to(
                scale[e * PAIR : (e + 1) * PAIR], (PAIR, LANES)
            )

    def one(e, carry):
        grad_rows = dye[e]
        scale = gates[e][:, 0:1]
        plain = dot_nt(grad_rows, wd_ref[e])
        gate_part, up_part = gp_ref[0, e], up_ref[0, e]
        soft_grad = jnp.sum(plain * hid_ref[0, e].astype(F32), axis=-1, keepdims=True)
        hidden_grad = plain * scale
        sigma = jax.nn.sigmoid(gate_part)
        gate_grad = (hidden_grad * up_part * sigma * (1.0 + gate_part * (1.0 - sigma))).astype(BF16)
        up_grad = (hidden_grad * gate_part * sigma).astype(BF16)
        gg_ref[0, e] = gate_grad
        ug_ref[0, e] = up_grad
        dyw_ref[0, e] = (grad_rows.astype(F32) * scale).astype(BF16)
        input_grad = (dot_nt(gate_grad, wg_ref[e]) + dot_nt(up_grad, wu_ref[e])).astype(BF16)
        lanes = lane_of((pairs * PAIR, LANES))
        high = soft_grad.astype(BF16).astype(F32)
        spot = jnp.where(
            lanes == first + e, high, jnp.where(lanes == first + e + LANES // 2, soft_grad - high, 0.0)
        ).astype(BF16)
        for p in range(pairs):
            dxb[p, e, :, :width] = input_grad[p * PAIR : (p + 1) * PAIR]
            dxb[p, e, :, width:] = spot[p * PAIR : (p + 1) * PAIR]
        return carry

    lax.fori_loop(0, owned, one, 0)
    for p in range(pairs):
        back = dot_tn(pick_ref[0, p], dxb[p].reshape(owned * PAIR, width + LANES))
        part_ref[2 * p : 2 * p + 2, 0] = back.astype(BF16).reshape(2, rows, width + LANES)


def experts_backward(scalars, grads, tokens, pick, gate_part, up_part, hidden, w_gate, w_up, w_down):
    group, slots, rows, width = grads.shape
    owned, unused, eff = w_gate.shape
    sources = 8
    parts = group // sources
    pairs = sources // 2
    steps = slots * parts
    held = pairs * PAIR
    source = lambda lanes, at: pl.BlockSpec((sources, 1, rows, lanes), lambda s, j, sc: (j, s, 0, at))
    return pl.pallas_call(
        experts_backward_kernel,
        grid_spec=pltpu.PrefetchScalarGridSpec(
            num_scalar_prefetch=1,
            grid=(slots, parts),
            in_specs=[
                source(width, 0),
                source(LANES, width // LANES),
                step_spec((pairs, owned * PAIR, 2 * rows)),
                step_spec((owned, held, eff)),
                step_spec((owned, held, eff)),
                step_spec((owned, held, eff)),
                resident(w_gate), resident(w_up), resident(w_down),
            ],
            out_specs=(
                source(width + LANES, 0),
                step_spec((owned, held, width)),
                step_spec((owned, held, eff)),
                step_spec((owned, held, eff)),
            ),
            scratch_shapes=[
                pltpu.VMEM((owned, held, LANES), F32),
                pltpu.VMEM((owned, held, width), BF16),
                pltpu.VMEM((pairs, owned, PAIR, width + LANES), BF16),
            ],
        ),
        out_shape=(
            jax.ShapeDtypeStruct((group, slots, rows, width + LANES), BF16),
            jax.ShapeDtypeStruct((steps, owned, held, width), BF16),
            jax.ShapeDtypeStruct((steps, owned, held, eff), BF16),
            jax.ShapeDtypeStruct((steps, owned, held, eff), BF16),
        ),
        compiler_params=pltpu.CompilerParams(vmem_limit_bytes=62 * MIB),
        name="experts_backward",
    )(scalars, grads, tokens, pick, gate_part, up_part, hidden, w_gate, w_up, w_down)


def expert_weights_kernel(xe_ref, gg_ref, ug_ref, hid_ref, dyw_ref, dg_ref, du_ref, dd_ref, ag, au, ad):
    step = pl.program_id(1)
    flat = lambda ref: ref[:, 0].reshape(ref.shape[0] * ref.shape[2], ref.shape[3])
    for acc, left, right in ((ad, hid_ref, dyw_ref), (ag, xe_ref, gg_ref), (au, xe_ref, ug_ref)):
        part = dot_tn(flat(left), flat(right))

        @pl.when(step == 0)
        def _():
            acc[...] = part

        @pl.when(step > 0)
        def _():
            acc[...] += part

    @pl.when(step == pl.num_programs(1) - 1)
    def _():
        dg_ref[0] = ag[...].astype(BF16)
        du_ref[0] = au[...].astype(BF16)
        dd_ref[0] = ad[...].astype(BF16)


def expert_weights(xe, gate_grad, up_grad, hidden, weighted):
    steps, owned, held, width = xe.shape
    eff = hidden.shape[3]
    each = 4
    block = lambda lanes: pl.BlockSpec((each, 1, held, lanes), lambda e, i: (i, e, 0, 0))
    out = lambda a, b: pl.BlockSpec((1, a, b), lambda e, i: (e, 0, 0))
    return pl.pallas_call(
        expert_weights_kernel,
        grid=(owned, steps // each),
        in_specs=[block(width), block(eff), block(eff), block(eff), block(width)],
        out_specs=(out(width, eff), out(width, eff), out(eff, width)),
        out_shape=(
            jax.ShapeDtypeStruct((owned, width, eff), BF16),
            jax.ShapeDtypeStruct((owned, width, eff), BF16),
            jax.ShapeDtypeStruct((owned, eff, width), BF16),
        ),
        scratch_shapes=[pltpu.VMEM((width, eff), F32), pltpu.VMEM((width, eff), F32), pltpu.VMEM((eff, width), F32)],
        compiler_params=pltpu.CompilerParams(vmem_limit_bytes=56 * MIB),
        name="expert_weights",
    )(xe, gate_grad, up_grad, hidden, weighted)


def attend_backward_kernel(
    sc_ref, q_ref, kv_ref, mixed_ref, invl_ref, dx_ref, soft_ref, og_ref, after_ref, fg_ref, wr_ref, wo_ref,
    dq_ref, dkv_ref, ag_ref, at_ref, lg_ref, fgg_ref, mg_s,
):
    slot, tile = pl.program_id(0), pl.program_id(1)
    slots, tiles = pl.num_programs(0), pl.num_programs(1)
    rows = q_ref.shape[1]
    here = sc_ref[slots]
    length = sc_ref[slot]
    live = here * rows < length
    chunk = 2 * rows
    chunks = (here + 2) // 2
    width = og_ref.shape[2]

    @pl.when(tile == 0)
    def _():
        valid = (row_of((rows, 1)) + here * rows < length).astype(F32)
        slab = dx_ref[0, :, width:].astype(F32)
        half = slab.shape[1] // 2
        soft = soft_ref[0]
        soft_grad = jnp.where(lane_of(slab.shape) < half, slab + pltpu.roll(slab, half, 1), 0.0)
        chosen = soft * (soft_grad - jnp.sum(soft * soft_grad, axis=-1, keepdims=True))
        logit_grad = chosen.astype(BF16)
        lg_ref[0] = logit_grad
        normed_grad = dx_ref[0, :, :width].astype(F32) + dot_nt(logit_grad, wr_ref[...])
        back, gain_grad = rms_backward(normed_grad, after_ref[0], fg_ref[...])

        @pl.when(slot == 0)
        def _():
            fgg_ref[...] = gain_grad

        @pl.when(slot > 0)
        def _():
            fgg_ref[...] += gain_grad

        after_grad = og_ref[0] + back
        ag_ref[0] = after_grad
        attn_grad = (valid * after_grad).astype(BF16)
        at_ref[0] = attn_grad
        mixed_grad = dot_nt(attn_grad, wo_ref[...]).astype(BF16)
        for t in range(mg_s.shape[0]):
            mg_s[t] = mixed_grad[:, t * 256 : (t + 1) * 256]

    dkv_ref[...] = jnp.zeros_like(dkv_ref)

    @pl.when(live)
    def _():
        q4 = stack_heads(q_ref[0], True).astype(BF16)
        do4_f = stack_heads(mg_s[tile].astype(F32) * invl_ref[0], True)
        do4 = do4_f.astype(BF16)
        product = do4_f * stack_heads(mixed_ref[0], False)
        delta = lax.dot_general(
            jnp.ones((8, LANES), F32), product, (((1,), (1,)), ((), ())),
            preferred_element_type=F32, precision=lax.Precision.HIGHEST,
        )[0:1]

        def step(index, total, masked):
            pair = kv_ref[pl.ds(2 * index, 2), 0]
            keys = pair[:, :, :LANES].reshape(chunk, LANES)
            values = pair[:, :, LANES:].reshape(chunk, LANES)
            weight = jnp.exp2(dot_nt(keys, q4) * EXP2_SCALE)
            if masked:
                at = lax.rem(lane_of(weight.shape), rows) + here * rows
                weight = jnp.where(row_of(weight.shape) + index * chunk <= at, weight, 0.0)
            pressure = dot_nt(values, do4)
            score_grad = (weight * (pressure - delta) * SCALE).astype(BF16)
            key_grad = dot(score_grad, q4)
            value_grad = dot(weight.astype(BF16), do4)
            dkv_ref[pl.ds(2 * index, 2), 0, :, :LANES] = key_grad.astype(BF16).reshape(2, rows, LANES)
            dkv_ref[pl.ds(2 * index, 2), 0, :, LANES:] = value_grad.astype(BF16).reshape(2, rows, LANES)
            return total + dot_tn(score_grad, keys)

        total = lax.fori_loop(
            0, chunks - 1, lambda i, c: step(i, c, False), jnp.zeros((4 * rows, LANES), F32)
        )
        total = step(chunks - 1, total, True)
        dq_ref[0] = unstack_heads(total).astype(BF16)

    @pl.when(jnp.logical_not(live))
    def _():
        dq_ref[...] = jnp.zeros_like(dq_ref)


def attend_backward(scalars, q, kv, mixed, invl, dx, soft, out_grad, after, ffn_gain, router, w_out):
    slots, rows, width = out_grad.shape
    group = kv.shape[0]
    qw = q.shape[2]
    tiles = qw // 256
    row = lambda lanes: pl.BlockSpec((1, rows, lanes), lambda s, b, sc: (s, 0, 0))
    tile = pl.BlockSpec((1, rows, 256), lambda s, b, sc: (s, 0, b))
    group_tile = pl.BlockSpec((group, 1, rows, 256), lambda s, b, sc: (0, s, 0, b))
    whole = lambda a: pl.BlockSpec(a.shape, lambda s, b, sc: (0, 0))
    return pl.pallas_call(
        attend_backward_kernel,
        grid_spec=pltpu.PrefetchScalarGridSpec(
            num_scalar_prefetch=1,
            grid=(slots, tiles),
            in_specs=[
                tile, group_tile, tile, tile, row(width + LANES), row(LANES), row(width), row(width),
                whole(ffn_gain), whole(router), whole(w_out),
            ],
            out_specs=(
                tile, group_tile, row(width), row(width), row(LANES),
                pl.BlockSpec((1, width), lambda s, b, sc: (0, 0)),
            ),
            scratch_shapes=[pltpu.VMEM((tiles, rows, 256), BF16)],
        ),
        out_shape=(
            jax.ShapeDtypeStruct((slots, rows, qw), BF16),
            jax.ShapeDtypeStruct(kv.shape, BF16),
            jax.ShapeDtypeStruct((slots, rows, width), F32),
            jax.ShapeDtypeStruct((slots, rows, width), BF16),
            jax.ShapeDtypeStruct((slots, rows, LANES), BF16),
            jax.ShapeDtypeStruct((1, width), F32),
        ),
        compiler_params=pltpu.CompilerParams(vmem_limit_bytes=56 * MIB),
        name="attend_backward",
    )(scalars, q, kv, mixed, invl, dx, soft, out_grad, after, ffn_gain, router, w_out)


def finish_kernel(
    dq_ref, dkv_ref, qraw_ref, kraw_ref, x_ref, ag_ref, cos_ref, sin_ref, gain_ref, qg_ref, kg_ref,
    wq_ref, wk_ref, wv_ref, h_ref, mixed_ref, at_ref, n2_ref, lg_ref,
    ig_ref, dense_ref, rt_ref, qgg_ref, kgg_ref, agg_ref, q_s, k_s, v_s,
):
    slot = pl.program_id(0)
    rows = x_ref.shape[1]
    cosine, sine = cos_ref[...], sin_ref[...]

    @pl.when(slot == 0)
    def _():
        qgg_ref[...] = jnp.zeros_like(qgg_ref)
        kgg_ref[...] = jnp.zeros_like(kgg_ref)
        agg_ref[...] = jnp.zeros_like(agg_ref)

    here = pl.ds(pl.multiple_of(slot * rows, rows), rows)
    for t in range(dq_ref.shape[2] // LANES):
        lanes = slice(t * LANES, (t + 1) * LANES)
        raw, gain = rope_backward(dq_ref[0, :, lanes].astype(F32), qraw_ref[0, :, lanes], qg_ref[...], cosine, sine)
        q_s[here, lanes] = raw.astype(BF16)
        qgg_ref[...] += gain
    for t in range(kraw_ref.shape[2] // LANES):
        lanes = slice(t * LANES, (t + 1) * LANES)
        at = 2 * t * LANES
        grad = dkv_ref[0, :, at : at + LANES].astype(BF16).astype(F32)
        raw, gain = rope_backward(grad, kraw_ref[0, :, lanes], kg_ref[...], cosine, sine)
        k_s[here, lanes] = raw.astype(BF16)
        kgg_ref[...] += gain
        v_s[here, lanes] = dkv_ref[0, :, at + LANES : at + 2 * LANES].astype(BF16)
    normed_grad = dot_nt(q_s[here], wq_ref[...]) + dot_nt(k_s[here], wk_ref[...]) + dot_nt(v_s[here], wv_ref[...])
    back, gain = rms_backward(normed_grad, x_ref[0].astype(F32), gain_ref[...])
    agg_ref[...] += gain
    ig_ref[0] = ag_ref[0] + back

    @pl.when(slot == pl.num_programs(0) - 1)
    def _():
        flat = lambda ref: ref[...].reshape(ref.shape[0] * ref.shape[1], ref.shape[2])
        shards, unused, shard_rows, width = dense_ref.shape
        h = flat(h_ref)
        half = width // 2

        def put(index, lanes, value):
            dense_ref[:, index, :, lanes] = value.astype(BF16).reshape(shards, shard_rows, value.shape[1])

        put(0, slice(0, width), dot_tn(h, q_s[...]))
        put(1, slice(0, half), dot_tn(h, k_s[...]))
        put(1, slice(half, width), dot_tn(h, v_s[...]))
        put(2, slice(0, width), dot_tn(flat(mixed_ref), flat(at_ref)))
        rt_ref[...] = dot_tn(flat(n2_ref), flat(lg_ref))


def finish(dq, dkv, qraw, kraw, x, after_grad, cosine, sine, attn_gain, qg, kg, wq, wk, wv, h, mixed, attn_grad, n2, lg):
    slots, rows, width = x.shape
    qw, kw = wq.shape[1], wk.shape[1]
    shards = 8
    row = lambda lanes: pl.BlockSpec((1, rows, lanes), lambda s: (s, 0, 0))
    whole = lambda a: pl.BlockSpec(a.shape, lambda s: (0,) * a.ndim)
    lanes_out = pl.BlockSpec((1, LANES), lambda s: (0, 0))
    return pl.pallas_call(
        finish_kernel,
        grid=(slots,),
        in_specs=[row(qw), row(2 * kw), row(qw), row(kw), row(width), row(width)]
        + [whole(a) for a in (cosine, sine, attn_gain, qg, kg, wq, wk, wv, h, mixed, attn_grad)]
        + [pl.BlockSpec((slots, rows, width), lambda s: (0, 0, 0)), whole(lg)],
        out_specs=(
            row(width),
            pl.BlockSpec((shards, 3, width // shards, width), lambda s: (0, 0, 0, 0)),
            pl.BlockSpec((width, LANES), lambda s: (0, 0)),
            lanes_out, lanes_out, pl.BlockSpec((1, width), lambda s: (0, 0)),
        ),
        out_shape=(
            jax.ShapeDtypeStruct((slots, rows, width), F32),
            jax.ShapeDtypeStruct((shards, 3, width // shards, width), BF16),
            jax.ShapeDtypeStruct((width, LANES), F32),
            jax.ShapeDtypeStruct((1, LANES), F32),
            jax.ShapeDtypeStruct((1, LANES), F32),
            jax.ShapeDtypeStruct((1, width), F32),
        ),
        scratch_shapes=[
            pltpu.VMEM((slots * rows, qw), BF16),
            pltpu.VMEM((slots * rows, kw), BF16),
            pltpu.VMEM((slots * rows, kw), BF16),
        ],
        compiler_params=pltpu.CompilerParams(vmem_limit_bytes=60 * MIB),
        name="finish",
    )(dq, dkv, qraw, kraw, x, after_grad, cosine, sine, attn_gain, qg, kg, wq, wk, wv, h, mixed, attn_grad, n2, lg)


def remote(src, dst, ss, rs, dev):
    return pltpu.make_async_remote_copy(src_ref=src, dst_ref=dst, send_sem=ss, recv_sem=rs, device_id=dev, device_id_type=MESH)

def ag_kernel(x_ref, o_ref, lsem, ss, rs):
    z = lax.axis_index("dp"); c = lax.axis_index("context"); y = lax.axis_index("experts")
    cs = c + 1 - 2 * lax.rem(c, 2)
    cx = lax.rem(c + 2, 4)
    yy = 1 - y
    sib, xn, yn = (z, cs, y), (z, cx, y), (z, c, yy)
    me = c * 2 + y
    gx = cx * 2 + y; gy = c * 2 + yy; gd = cx * 2 + yy
    bar = pltpu.get_barrier_semaphore()
    for d in (sib, xn, yn):
        pl.semaphore_signal(bar, inc=1, device_id=d, device_id_type=MESH)
    pl.semaphore_wait(bar, 3)
    n = x_ref.shape[0]
    h = n // 2
    loc = [pltpu.make_async_copy(x_ref.at[s], o_ref.at[me, s], lsem.at[s]) for s in range(n)]
    sx = [remote(x_ref.at[s], o_ref.at[me, s], ss.at[0, s], rs.at[0, s], xn) for s in range(n)]
    sy = [remote(x_ref.at[s], o_ref.at[me, s], ss.at[1, s], rs.at[1, s], yn) for s in range(n)]
    sc = [remote(x_ref.at[s], o_ref.at[me, s], ss.at[2, s], rs.at[2, s], sib) for s in range(n)]
    fx = [remote(o_ref.at[gx, s], o_ref.at[gx, s], ss.at[3, s], rs.at[3, s], sib) for s in range(n)]
    fy = [remote(o_ref.at[gy, s], o_ref.at[gy, s], ss.at[4, s], rs.at[4, s], sib) for s in range(n)]
    fd = [remote(o_ref.at[gd, s], o_ref.at[gd, s], ss.at[5, s], rs.at[5, s], sib) for s in range(n)]
    dg = [remote(o_ref.at[gx, s], o_ref.at[gx, s], ss.at[6, s], rs.at[6, s], yn) if s < h else
          remote(o_ref.at[gy, s], o_ref.at[gy, s], ss.at[6, s], rs.at[6, s], xn) for s in range(n)]
    for i in range(n):
        sx[i].start()
        sy[(i + h) % n].start()
    for s in range(n):
        sc[s].start()
        loc[s].start()
    for i in range(n):
        a = i; b = (i + h) % n
        sx[a].wait_recv()
        if a < h: dg[a].start()
        fx[a].start()
        sy[b].wait_recv()
        if b >= h: dg[b].start()
        fy[b].start()
    for i in range(h):
        for s in (i, i + h):
            dg[s].wait_recv(); fd[s].start()
    for s in range(n):
        sc[s].wait_recv(); fx[s].wait_recv(); fy[s].wait_recv(); fd[s].wait_recv()
        loc[s].wait()
        for k in (sx, sy, sc, fx, fy, fd, dg): k[s].wait_send()

def all_gather(x, cid):
    n = x.shape[0]
    return pl.pallas_call(ag_kernel,
        out_shape=jax.ShapeDtypeStruct((8,) + x.shape, x.dtype),
        in_specs=[pl.BlockSpec(memory_space=pl.ANY)], out_specs=pl.BlockSpec(memory_space=pl.ANY),
        scratch_shapes=[pltpu.SemaphoreType.DMA((n,)), pltpu.SemaphoreType.DMA((7, n)), pltpu.SemaphoreType.DMA((7, n))],
        compiler_params=pltpu.CompilerParams(collective_id=cid, has_side_effects=True), name="ag")(x)

def rs_kernel(p_ref, o_ref, own, other, sb, q, dx, dy, rx, ry, lsem, ss, rs):
    z = lax.axis_index("dp"); c = lax.axis_index("context"); y = lax.axis_index("experts")
    core = lax.rem(c, 2)
    cs = c + 1 - 2 * core
    cx = lax.rem(c + 2, 4)
    yy = 1 - y
    sib, xn, yn = (z, cs, y), (z, cx, y), (z, c, yy)
    bar = pltpu.get_barrier_semaphore()
    for d in (sib, xn, yn):
        pl.semaphore_signal(bar, inc=1, device_id=d, device_id_type=MESH)
    n = p_ref.shape[1]
    h = n // 2
    chips = [(cx, yy), (cx, y), (c, yy), (c, y)]
    idx = [a * 2 + b for a, b in chips]
    oth = [(a + 1 - 2 * core) * 2 + b for a, b in chips]
    ld = [[pltpu.make_async_copy(p_ref.at[idx[k], s], own.at[k, s], lsem.at[k, s]) for s in range(n)] for k in range(4)]
    st = [[remote(p_ref.at[oth[k], s], sb.at[k, s], ss.at[k, s], rs.at[k, s], sib) for s in range(n)] for k in range(4)]
    for k in range(4):
        for s in range(n):
            ld[k][s].start()
    pl.semaphore_wait(bar, 3)
    for k in range(4):
        for s in range(n):
            st[k][s].start()
    dgs = [remote(q.at[0, s], dx.at[s], ss.at[4, s], rs.at[4, s], xn) if s < h else
           remote(q.at[0, s], dy.at[s - h], ss.at[4, s], rs.at[4, s], yn) for s in range(n)]
    tx = [remote(q.at[1, s], rx.at[s], ss.at[5, s], rs.at[5, s], xn) for s in range(n)]
    ty = [remote(q.at[2, s], ry.at[s], ss.at[6, s], rs.at[6, s], yn) for s in range(n)]
    f32 = jnp.float32
    def pair(k, s):
        ld[k][s].wait(); st[k][s].wait_recv()
        return own[k, s].astype(f32) + sb[k, s].astype(f32)
    for i in range(h):
        for s in (i, i + h):
            q[0, s] = pair(0, s).astype(q.dtype); dgs[s].start()
    for i in range(h):
        q[1, i] = pair(1, i).astype(q.dtype); tx[i].start()
        q[2, i + h] = pair(2, i + h).astype(q.dtype); ty[i + h].start()
    for i in range(h):
        a = pair(2, i)
        dgs[i].wait_recv()
        q[2, i] = (a + dx[i].astype(f32)).astype(q.dtype); ty[i].start()
        b = pair(1, i + h)
        dgs[i + h].wait_recv()
        q[1, i + h] = (b + dy[i].astype(f32)).astype(q.dtype); tx[i + h].start()
    for i in range(h):
        for s in (i, i + h):
            a = pair(3, s)
            tx[s].wait_recv(); ty[s].wait_recv()
            o_ref[s] = (a + rx[s].astype(f32) + ry[s].astype(f32)).astype(o_ref.dtype)
    for s in range(n):
        for k in st: k[s].wait_send()
        for k in (dgs, tx, ty): k[s].wait_send()

def reduce_scatter(p, cid, dt):
    _, n, r, w = p.shape
    h = n // 2
    V = pltpu.VMEM
    return pl.pallas_call(rs_kernel,
        out_shape=jax.ShapeDtypeStruct((n, r, w), dt),
        in_specs=[pl.BlockSpec(memory_space=pl.ANY)], out_specs=pl.BlockSpec(memory_space=pltpu.VMEM),
        scratch_shapes=[V((4, n, r, w), p.dtype), V((1, 8, 128), p.dtype), V((4, n, r, w), p.dtype), V((3, n, r, w), p.dtype),
            V((h, r, w), p.dtype), V((h, r, w), p.dtype), V((n, r, w), p.dtype), V((n, r, w), p.dtype),
            pltpu.SemaphoreType.DMA((4, n)), pltpu.SemaphoreType.DMA((7, n)), pltpu.SemaphoreType.DMA((7, n))],
        compiler_params=pltpu.CompilerParams(collective_id=cid, has_side_effects=True, vmem_limit_bytes=60 * 2**20), name="rs")(p)


def plane_gather(rows, fast, number):
    if fast:
        return all_gather(rows, number)
    return lax.all_gather(rows, ("context", "experts"), axis=0, tiled=False)


def plane_scatter(parts, fast, number):
    if fast:
        return reduce_scatter(parts, number, F32)
    return lax.psum_scatter(parts, ("context", "experts"), scatter_dimension=0, tiled=False).astype(F32)


def per_device(
    fast, block_input, teacher, lengths, routes, w_query, w_key, w_value, w_out, query_gain, key_gain,
    attn_gain, ffn_gain, w_router, w_gate, w_up, w_down,
):
    slots, rows, width = block_input.shape
    expert_total = w_router.shape[1]
    group = lax.axis_size(("context", "experts"))
    here = lax.axis_index(("context", "experts"))
    span = rows * group
    slot_lengths = lax.dynamic_slice_in_dim(lengths, lax.axis_index("dp") * slots, slots)
    scalars = jnp.concatenate([slot_lengths, here[None]]).astype(jnp.int32)
    positions = here * rows + jnp.arange(rows, dtype=jnp.int32)
    valid = (positions[None, :] < slot_lengths[:, None]).astype(F32)[..., None]
    count_all = jnp.sum(lengths).astype(F32)
    positions_all = lengths.shape[0] * span

    half = HEAD // 2
    lanes = jnp.arange(LANES, dtype=jnp.int32)
    inverse = 10000.0 ** (-((lanes % half).astype(F32) * 2.0 / HEAD))
    turned = positions.astype(F32)[:, None] * inverse[None, :]
    cosine = jnp.cos(turned)
    sine = jnp.sin(turned) * jnp.where(lanes % HEAD < half, -1.0, 1.0)[None, :]
    qg = jnp.concatenate([query_gain, query_gain])[None, :]
    kg = jnp.concatenate([key_gain, key_gain])[None, :]
    ag, fg = attn_gain[None, :], ffn_gain[None, :]
    router = jnp.pad(w_router, ((0, 0), (0, LANES - expert_total)))

    h, q, kv_local, qraw, kraw = project(block_input, ag, w_query, w_key, w_value, qg, kg, cosine, sine)
    kv = plane_gather(kv_local, fast, 1)
    mixed, invl, after, xg, soft = attend(scalars, q, kv, block_input, w_out, fg, router, routes)
    tokens = plane_gather(xg, fast, 2)
    pick, xe, gate_part, up_part, hidden, part = experts_forward(scalars, tokens, w_gate, w_up, w_down)
    output = after + plane_scatter(part, fast, 3)
    difference = valid * (output - teacher.astype(F32))
    loss_part = jnp.sum(difference * difference)
    out_grad = difference * (positions_all / count_all)
    grads = plane_gather(out_grad.astype(BF16), fast, 4)
    dpart, weighted, gate_grad, up_grad = experts_backward(
        scalars, grads, tokens, pick, gate_part, up_part, hidden, w_gate, w_up, w_down
    )
    expert_grads = lax.psum(expert_weights(xe, gate_grad, up_grad, hidden, weighted), "dp")
    dx = plane_scatter(dpart, fast, 5)
    dq, dkv_parts, after_grad, attn_grad, logit_grad, ffn_gain_grad = attend_backward(
        scalars, q, kv, mixed, invl, dx, soft, out_grad, after, fg, router, w_out
    )
    dkv = plane_scatter(dkv_parts, fast, 6)
    input_grad, dense, router_grad, query_gg, key_gg, attn_gg = finish(
        dq, dkv, qraw, kraw, block_input, after_grad, cosine, sine, ag, qg, kg,
        w_query, w_key, w_value, h, mixed, attn_grad, xg, logit_grad,
    )
    if fast:
        shards, kinds, shard_rows, unused = dense.shape
        shard = reduce_scatter(dense.reshape(shards, 2 * kinds, shard_rows // 2, width), 7, F32)
        shard = lax.psum(shard, "dp").astype(BF16)
        dense = all_gather(shard, 8).reshape(shards, kinds, shard_rows, width)
    else:
        dense = lax.psum(dense, ("dp", "context", "experts"))
    dense = [dense[:, k].reshape(width, width).astype(F32) for k in range(3)]
    small = lax.psum(
        (
            query_gg[0, :HEAD] + query_gg[0, HEAD:], key_gg[0, :HEAD] + key_gg[0, HEAD:], attn_gg[0],
            ffn_gain_grad[0], router_grad[:, :expert_total], loss_part,
        ),
        ("dp", "context", "experts"),
    )
    key_width = w_key.shape[1]
    return (
        small[5] / (count_all * width),
        output.astype(BF16),
        input_grad,
        dense[0],
        dense[1][:, :key_width],
        dense[1][:, key_width:],
        dense[2],
        small[0], small[1], small[2], small[3], small[4],
        expert_grads[0].astype(F32), expert_grads[1].astype(F32), expert_grads[2].astype(F32),
    )


def solution(mesh):
    fast = mesh.shape["context"] == 4 and mesh.shape["experts"] == 2
    rows = P("dp", ("context", "experts"), None)
    owned = P(("context", "experts"), None, None)
    return jax.shard_map(
        functools.partial(per_device, fast),
        mesh=mesh,
        in_specs=(rows, rows, P(), rows) + (P(),) * 9 + (owned,) * 3,
        out_specs=(P(), rows, rows) + (P(),) * 9 + (owned,) * 3,
        check_vma=False,
    )
```

time: 1860 us -> 1090 us (0.59)
  Pallas kernels: 0 us -> 546 us
  waiting for transfers between devices: 766 us -> 353 us
  matrix products: 318 us -> 0 us
  local copies, waits for them, and re-layouts: 304 us -> 13.1 us
  blocking collectives: 285 us -> 120 us
  other arithmetic: 141 us -> 32 us
    pallas_call x0 -> x15, Pallas kernels: none -> 546 us  [the longest x4 181 us: reduce_scatter(): pl.pallas_call(rs_kernel, out_shape=jax.ShapeDtypeStruct((n, r, w), dt),...]
    dot_general x44 -> x0, matrix products: 318 us -> none  [the longest x6 41.3 us: score_block(): jnp.einsum('sqagd,sbad->sagqb', query_five, key_rows, preferred_element_t...]
    all_to_all x2 -> x0, blocking collectives: 244 us -> none  [to_owner(): lax.all_to_all(shaped, ('context', 'experts'), split_axis=0, concat_axis=...]
    psum x2, waiting for transfers between devices: 563 us -> 353 us  [the longest x1 353 us: per_device(): lax.psum(expert_weights(xe, gate_grad, up_grad, hidden, weighted), 'dp')]
    all_to_all x2 -> x0, waiting for transfers between devices: 183 us -> none  [to_source(): lax.all_to_all(owner_rows, ('context', 'experts'), split_axis=1, concat_a...]
    gather x9 -> x0, local copies, waits for them, and re-layouts: 86 us -> none  [the longest x7 33.8 us: per_device(): jnp.take_along_axis(router_logits, route_rows, axis=1)]
    psum x1 -> x2, blocking collectives: 40.8 us -> 120 us  [the longest x1 82.4 us: per_device(): shard = lax.psum(shard, 'dp').astype(BF16)]
    convert_element_type x6 -> x0, local copies, waits for them, and re-layouts: 57.4 us -> none  [the longest x1 28.2 us: experts_forward(): jnp.einsum('emf,efd->emd', hidden, w_down, preferred_element_type=jnp.flo...]
  transfers between devices with their start and end apart: 6 -> 2, of which waited for: 5 -> 1; matrix products, arithmetic and copies ran while one was open for 12% -> 1% of each run, Pallas kernels for 0% -> 8%
where the time goes in v1:
time: 1090 us; the launch traced here: 1080 us
  Pallas kernels  546 us (50%)
  waiting for transfers between devices  353 us (32%)
  blocking collectives  120 us (11%)
  other arithmetic  32 us (3%)
  between operations  17.2 us (2%)
  local copies, waits for them, and re-layouts  13.1 us (1%)
    psum x1, waiting for transfers between devices, per_device(): lax.psum(expert_weights(xe, gate_grad, up_grad, hidden, weighted), 'dp')  353 us
    pallas_call x4, Pallas kernels, reduce_scatter(): pl.pallas_call(rs_kernel, out_shape=jax.ShapeDtypeStruct((n, r, w), dt),...  181 us
    pallas_call x4, Pallas kernels, all_gather(): pl.pallas_call(ag_kernel, out_shape=jax.ShapeDtypeStruct((8,) + x.shape,...  166 us
    psum x1, blocking collectives, per_device(): shard = lax.psum(shard, 'dp').astype(BF16)  82.4 us
    pallas_call x1, Pallas kernels, experts_backward(): pl.pallas_call(experts_backward_kernel, grid_spec=pltpu.PrefetchScalarGri...  46.3 us
    pallas_call x1, Pallas kernels, experts_forward(): pl.pallas_call(experts_forward_kernel, grid_spec=pltpu.PrefetchScalarGrid...  41.6 us
    psum x1, blocking collectives, per_device(): lax.psum((query_gg[0, :HEAD] + query_gg[0, HEAD:], key_gg[0, :HEAD] + key...  38.1 us
    pallas_call x1, Pallas kernels, attend_backward(): pl.pallas_call(attend_backward_kernel, grid_spec=pltpu.PrefetchScalarGrid...  31 us
  transfers between devices with their start and end apart: 2, of which 1 were waited for; matrix products, arithmetic and copies ran while one was open for 1% of the time, Pallas kernels for 8%

profile of v1, /device:TPU:0, one launch (start us, length us, event | category | flops | bytes accessed | tf_op | source)
XLA Modules:
  0.0 1081.8 jit_solution(14927910886627223052)
XLA Ops:
  7.2 1.3 reduce_sum.19
  10.6 1.6 copy.32.routes_ref
  12.1 1.0 copy.31
  13.2 1.3 maximum_bitcast_fusion
  15.5 9.4 project.1
  24.9 41.3 %ag.4.kv_ref = bf16[8,4,128,1024]{3,2,1,0:T(8,128)(2,1)} custom-call(bf16[4,128,1024]{2,1,0:T(8,128)(2,1)} %get-tuple-element.51.x_ref), custom_call_target="tpu_custom_call" | custom-call | tf_op jit(solution)/shard_map/ag/pallas_call | solution.py:767
  67.0 22.9 %attend.1 = (bf16[4,128,1024]{2,1,0:T(8,128)(2,1)}, f32[4,128,1024]{2,1,0:T(8,128)}, f32[4,128,1024]{2,1,0:T(8,128)}, bf16[4,128,1152]{2,1,0:T(8,128)(2,1)}, f32[4,128,128]{2,1,0:T(8,128)}) custom-call(s32[5]{0:T(128)} %pad_add_fusion.sc_ref, bf16[4,128,1024]{2,1,0:T(8,128)(2,1)} %get-tuple-element.50.q_ref, bf16[8,4,128,1024]{3,2,1,0:T(8,128)(2,1)} %ag.4.kv_ref, ...), custom_call_target="tpu_custom_call" | custom-call | tf_op jit(solution)/shard_map/attend/pallas_call | solution.py:238
  89.9 55.5 %ag.5.xg_ref.slab_ref = bf16[8,4,128,1152]{3,2,1,0:T(8,128)(2,1)} custom-call(bf16[4,128,1152]{2,1,0:T(8,128)(2,1)} %get-tuple-element.53.x_ref.n2_ref), custom_call_target="tpu_custom_call" | custom-call | tf_op jit(solution)/shard_map/ag/pallas_call | solution.py:767
  145.4 41.6 %experts_forward.1 = (bf16[4,4,320,256]{3,2,1,0:T(8,128)(2,1)}, bf16[4,4,320,1024]{3,2,1,0:T(8,128)(2,1)}, f32[4,4,320,512]{3,2,1,0:T(8,128)}, f32[4,4,320,512]{...) custom-call(s32[5]{0:T(128)} %pad_add_fusion.sc_ref, ...), custom_call_target="tpu_custom_call" | custom-call | tf_op jit(solution)/shard_map/experts_forward/pallas_call | solution.py:352
  187.1 41.9 %rs.4 = f32[4,128,1024]{2,1,0:T(8,128)} custom-call(bf16[8,4,128,1024]{3,2,1,0:T(8,128)(2,1)} %get-tuple-element.54.p_ref), custom_call_target="tpu_custom_call" | custom-call | tf_op jit(solution)/shard_map/rs/pallas_call | solution.py:831
  229.0 3.1 fusion.8
  232.1 2.7 fusion
  234.9 39.0 %ag.6.dy_ref = bf16[8,4,128,1024]{3,2,1,0:T(8,128)(2,1)} custom-call(bf16[4,128,1024]{2,1,0:T(8,128)(2,1)} %get-tuple-element.116.x_ref), custom_call_target="tpu_custom_call" | custom-call | tf_op jit(solution)/shard_map/ag/pallas_call | solution.py:767
  273.9 46.3 %experts_backward.1 = (bf16[8,4,128,1152]{3,2,1,0:T(8,128)(2,1)}, bf16[4,4,320,1024]{3,2,1,0:T(8,128)(2,1)}, bf16[4,4,320,512]{3,2,1,0:T(8,128)(2,1)}, bf16[4,4,320,512]{3,2,1,0:T(8,128)(2,1)}) custom-call(s32[5]{0:T(128)} %pad_add_fusion.sc_ref, bf16[8,4,128,1024]{3,2,1,0:T(8,128)(2,1)} %ag.6.dy_ref, bf16[8,4,128,1152]{3,2,1,0:T(8,128)(2,1)} %ag.5.xg_ref.slab_ref, ...), custom_call_target="tpu_custom_call" | custom-call | tf_op jit(solution)/shard_map/experts_backward/pallas_call | solution.py:429
  320.2 46.0 %rs.5.dx_ref = f32[4,128,1152]{2,1,0:T(8,128)} custom-call(bf16[8,4,128,1152]{3,2,1,0:T(8,128)(2,1)} %get-tuple-element.61.p_ref), custom_call_target="tpu_custom_call" | custom-call | tf_op jit(solution)/shard_map/rs/pallas_call | solution.py:831
  366.2 31.0 %attend_backward.1 = (bf16[4,128,1024]{2,1,0:T(8,128)(2,1)}, bf16[8,4,128,1024]{3,2,1,0:T(8,128)(2,1)}, f32[4,128,1024]{2,1,0:T(8,128)}, bf16[4,128,1024]{2,1,0:...) custom-call(s32[5]{0:T(128)} %pad_add_fusion.sc_ref, bf16[4,128,1024]{2,1,0:T(8,128)(2,1)} %get-tuple-element.50.q_ref, ...), custom_call_target="tpu_custom_call" | custom-call | tf_op jit(solution)/shard_map/attend_backward/pallas_call | solution.py:601
  397.1 59.4 %rs.6.dkv_ref = f32[4,128,1024]{2,1,0:T(8,128)} custom-call(bf16[8,4,128,1024]{3,2,1,0:T(8,128)(2,1)} %get-tuple-element.64.p_ref), custom_call_target="tpu_custom_call" | custom-call | tf_op jit(solution)/shard_map/rs/pallas_call | solution.py:831
  456.5 24.1 %finish.1 = (f32[4,128,1024]{2,1,0:T(8,128)}, bf16[8,3,128,1024]{3,2,1,0:T(8,128)(2,1)}, f32[1024,128]{1,0:T(8,128)}, f32[1,128]{1,0:T(1,128)}, f32[1,128]{1,0:T(1,128)}, /*index=5*/f32[1,1024]{1,0:T(1,128)}) custom-call(bf16[4,128,1024]{2,1,0:T(8,128)(2,1)} %get-tuple-element.63.dq_ref, f32[4,128,1024]{2,1,0:T(8,128)} %rs.6.dkv_ref, ...), custom_call_target="tpu_custom_call" | custom-call | tf_op jit(solution)/shard_map/finish/pallas_call | solution.py:687
  480.7 22.7 %expert_weights.1 = (bf16[4,1024,512]{2,1,0:T(8,128)(2,1)}, bf16[4,1024,512]{2,1,0:T(8,128)(2,1)}, bf16[4,512,1024]{2,1,0:T(8,128)(2,1)}) custom-call(bf16[4,4,320,1024]{3,2,1,0:T(8,128)(2,1)} %get-tuple-element.78.xe_ref, bf16[4,4,320,512]{3,2,1,0:T(8,128)(2,1)} %get-tuple-element.79.gg_ref, bf16[4,4,320,512]{3,2,1,0:T(8,128)(2,1)} %get-tuple-element.80.ug_ref, ...), custom_call_target="tpu_custom_call" | custom-call | tf_op jit(solution)/shard_map/expert_weights/pallas_call | solution.py:493
  504.2 38.1 %all-reduce.1 = (f32[]{:T(128)}, f32[64]{0:T(128)}, f32[64]{0:T(128)}, f32[1024]{0:T(1024)}, f32[1024]{0:T(1024)}) all-reduce(f32[]{:T(128)} %get-tuple-element.117, f32[64]{0:T(128)S(1)} %add_bitcast_fusion.1, f32[64]{0:T(128)S(1)} %add_bitcast_fusion, ...), channel_id=1, replica_groups=mesh['dp'=4,'context'=4,'experts'=2] {'dp','context','experts'}, use_global_device_ids=true, to_apply=%region_1.2 | all-reduce | flops 2177 | bytes 17416 | tf_op jit(solution)/shard_map/psum | solution.py:910
  542.3 34.1 %rs.7 = f32[6,64,1024]{2,1,0:T(8,128)} custom-call(bf16[8,6,64,1024]{3,2,1,0:T(8,128)(2,1)} %bitcast.26), custom_call_target="tpu_custom_call" | custom-call | tf_op jit(solution)/shard_map/rs/pallas_call | solution.py:831
  576.5 82.4 %all-reduce.10.x_ref = bf16[6,64,1024]{2,1,0:T(8,128)(2,1)} all-reduce(f32[6,64,1024]{2,1,0:T(8,128)} %rs.7), channel_id=1, replica_groups=mesh['dp'=4,'context'=4,'experts'=2] {'dp'}, use_global_device_ids=true, to_apply=%region_3.4 | all-reduce | flops 393216 | bytes 2359296 | tf_op jit(solution)/shard_map/psum | solution.py:905
  658.9 30.3 %ag.7 = bf16[8,6,64,1024]{3,2,1,0:T(8,128)(2,1)} custom-call(bf16[6,64,1024]{2,1,0:T(8,128)(2,1)} %all-reduce.10.x_ref), custom_call_target="tpu_custom_call" | custom-call | tf_op jit(solution)/shard_map/ag/pallas_call | solution.py:767
  689.8 3.9 fusion.9
  693.7 2.6 bitcast_convert_fusion
  696.9 2.6 fusion.10
  699.5 2.6 bitcast_convert_fusion.1
  702.1 1.9 copy.33
  704.0 353.5 %all-reduce.9.cloned.1.call-done = (bf16[4,1024,512]{2,1,0:T(8,128)(2,1)}, bf16[4,1024,512]{2,1,0:T(8,128)(2,1)}, bf16[4,512,1024]{2,1,0:T(8,128)(2,1)}) async-done(((bf16[4,1024,512]{2,1,0:T(8,128)(2,1)}, bf16[4,1024,512]{2,1,0:T(8,128)(2,1)}, bf16[4,512,1024]{2,1,0:T(8,128)(2,1)}), (bf16[4,1024,512]{2,1,0:T(8,128)(2,1)}, bf16[4,1024,512]{2,1,0:T(8,128)(2,1)}, ...) | async-done | bytes 12582928 | tf_op jit(solution)/shard_map/psum | solution.py:892
  1057.4 6.9 convert_element_type.79
  1064.4 4.6 convert_element_type.80
  1069.0 4.4 convert_element_type.81
  (31 shorter events, 4.6 us)
Async XLA Ops:
  7.2 694.9 %all-reduce.7.cloned.1.call-start = ((), (), s32[]{:S(2)}) async-start(), calls=%async_computation | async-start | bytes 1048576 | tf_op jit(solution)/shard_map/psum | solution.py:910
  187.0 41.9 %copy-start = (f32[4,128,1024]{2,1,0:T(8,128)S(1)}, f32[4,128,1024]{2,1,0:T(8,128)}, u32[]{:S(2)}) copy-start(f32[4,128,1024]{2,1,0:T(8,128)} %get-tuple-element.52.after_ref) | copy-start | bytes 6291460
  229.0 3.2 copy-start.3
  480.7 576.8 %all-reduce.9.cloned.1.call-start = ((), (), s32[]{:S(2)}) async-start(), calls=%async_computation.1 | async-start | bytes 25165824 | tf_op jit(solution)/shard_map/psum | solution.py:892
  503.4 0.7 copy-start.7
  503.4 0.7 copy-start.6
  503.4 0.8 copy-start.4
  503.4 0.8 copy-start.5
  1057.4 6.9 copy-start.2
  1064.4 4.6 copy-start.1
Sparse Core Ops, SparseCore 0:
  480.8 128.7 all-reduce.6
  612.7 444.7 all-reduce.8

commit v2 on v1

--- a/solution.py
+++ b/solution.py
@@ -837,6 +837,764 @@
         compiler_params=pltpu.CompilerParams(collective_id=cid, has_side_effects=True, vmem_limit_bytes=60 * 2**20), name="rs")(p)
 
 
+def add_to(ref, value):
+    ref[...] = (ref[...].astype(F32) + value).astype(ref.dtype)
+
+
+class Plane:
+    def __init__(self):
+        z, c, y = lax.axis_index("dp"), lax.axis_index("context"), lax.axis_index("experts")
+        core = lax.rem(c, 2)
+        cx, yy = lax.rem(c + 2, 4), 1 - y
+        self.me = c * 2 + y
+        self.sib, self.xn, self.yn = (z, c + 1 - 2 * core, y), (z, cx, y), (z, c, yy)
+        chips = [(cx, yy), (cx, y), (c, yy), (c, y)]
+        self.own = [a * 2 + b for a, b in chips]
+        self.other = [(a + 1 - 2 * core) * 2 + b for a, b in chips]
+        self.inner_plane = (z == 1) | (z == 2)
+        self.outer_plane = (z == 0) | (z == 3)
+        self.inner = (1 + z // 2, c, y)
+        self.across = (3 - z, c, y)
+        self.outer = ((z - 1) * 3, c, y)
+
+    def barrier(self, line):
+        bar = pltpu.get_barrier_semaphore()
+        tell = lambda who: pl.semaphore_signal(bar, inc=1, device_id=who, device_id_type=MESH)
+        for who in (self.sib, self.xn, self.yn):
+            tell(who)
+        if not line:
+            pl.semaphore_wait(bar, 3)
+            return
+
+        @pl.when(self.outer_plane)
+        def _():
+            tell(self.inner)
+            pl.semaphore_wait(bar, 4)
+
+        @pl.when(self.inner_plane)
+        def _():
+            tell(self.across)
+            tell(self.outer)
+            pl.semaphore_wait(bar, 5)
+
+
+class Scatter:
+    def __init__(self, plane, own, other, buffers, sems):
+        self.plane, self.own, self.other = plane, own, other
+        self.sb, self.da, self.db, self.rx, self.ry = buffers
+        self.sent, self.got = sems
+        self.rows = self.sb.shape[2]
+        self.top, self.low = pl.ds(0, self.rows // 2), pl.ds(self.rows // 2, self.rows // 2)
+
+    def core(self, k, s):
+        return remote(self.other(k, s), self.sb.at[k, s], self.sent.at[k, s], self.got.at[k, s], self.plane.sib)
+
+    def diag(self, s):
+        mine = self.own(0, s)
+        return (
+            remote(mine.at[self.top], self.da.at[s], self.sent.at[4, s], self.got.at[4, s], self.plane.xn),
+            remote(mine.at[self.low], self.db.at[s], self.sent.at[5, s], self.got.at[5, s], self.plane.yn),
+        )
+
+    def side(self, number, s):
+        axis, half = number // 2, (self.top, self.low)[number % 2]
+        there = (self.rx, self.ry)[axis]
+        who = (self.plane.xn, self.plane.yn)[axis]
+        return remote(
+            self.own(1 + axis, s).at[half], there.at[s, half], self.sent.at[6 + number, s], self.got.at[6 + number, s], who
+        )
+
+    def pair(self, k, s, half):
+        return self.own(k, s)[half].astype(F32) + self.sb[k, s, half].astype(F32)
+
+    def start(self, s):
+        for k in range(4):
+            self.core(k, s).start()
+
+    def first(self, s):
+        self.core(0, s).wait_recv()
+        mine = self.own(0, s)
+        add_to(mine, self.sb[0, s].astype(F32))
+        for copy in self.diag(s):
+            copy.start()
+
+    def second(self, s):
+        self.core(1, s).wait_recv()
+        self.own(1, s)[self.top] = self.pair(1, s, self.top).astype(BF16)
+        self.side(0, s).start()
+        self.core(2, s).wait_recv()
+        self.own(2, s)[self.low] = self.pair(2, s, self.low).astype(BF16)
+        self.side(3, s).start()
+
+    def third(self, s):
+        by_x, by_y = self.diag(s)
+        by_x.wait_recv()
+        self.own(2, s)[self.top] = (self.pair(2, s, self.top) + self.da[s].astype(F32)).astype(BF16)
+        self.side(2, s).start()
+        by_y.wait_recv()
+        self.own(1, s)[self.low] = (self.pair(1, s, self.low) + self.db[s].astype(F32)).astype(BF16)
+        self.side(1, s).start()
+
+    def result(self, s):
+        self.core(3, s).wait_recv()
+        for number in range(4):
+            self.side(number, s).wait_recv()
+        return (
+            self.own(3, s)[...].astype(F32)
+            + self.sb[3, s].astype(F32)
+            + self.rx[s].astype(F32)
+            + self.ry[s].astype(F32)
+        )
+
+    def drain(self, s):
+        for k in range(4):
+            self.core(k, s).wait_send()
+        for copy in self.diag(s):
+            copy.wait_send()
+        for number in range(4):
+            self.side(number, s).wait_send()
+
+
+class Line:
+    ring, back = 4, 2
+
+    def __init__(self, plane, held, first, second, total, buffers, sems):
+        self.plane, self.held, self.r1, self.r2, self.total = plane, held, first, second, total
+        self.l1, self.va, self.vt = buffers
+        self.sent, self.got, self.local = sems
+        self.count = held.shape[0]
+
+    def inward(self, i):
+        return remote(self.held.at[i], self.r1.at[i], self.sent.at[0, i], self.got.at[0, i], self.plane.inner)
+
+    def across(self, i):
+        return remote(self.va.at[i % self.ring], self.r2.at[i], self.sent.at[1, i], self.got.at[1, i], self.plane.across)
+
+    def outward(self, i):
+        return remote(self.vt.at[i % self.back], self.total.at[i], self.sent.at[2, i], self.got.at[2, i], self.plane.outer)
+
+    def keep(self, i):
+        return pltpu.make_async_copy(self.vt.at[i % self.back], self.total.at[i], self.local.at[i % self.back])
+
+    def load(self, number, i):
+        source, there = (
+            (self.r1, self.l1.at[i % 2]), (self.held, self.va.at[i % self.ring]), (self.r2, self.vt.at[i % self.back])
+        )[number]
+        return pltpu.make_async_copy(source.at[i], there, self.local.at[self.ring + 2 * number + i % 2])
+
+    def advance(self, j):
+        steps = self.count // 2
+        ahead = [2 * j, 2 * j + 1] if j < steps else []
+        behind = [2 * j - 2, 2 * j - 1] if j >= 1 else []
+
+        @pl.when(self.plane.inner_plane)
+        def _():
+            for i in ahead:
+                if i >= self.ring:
+                    self.across(i - self.ring).wait_send()
+                self.load(1, i).start()
+            for i in ahead:
+                self.inward(i).wait_recv()
+                self.load(0, i).start()
+            for i in ahead:
+                self.load(1, i).wait()
+                self.load(0, i).wait()
+                add_to(self.va.at[i % self.ring], self.l1[i % 2].astype(F32))
+                self.across(i).start()
+            for i in behind:
+                if i >= self.back:
+                    self.outward(i - self.back).wait_send()
+                    self.keep(i - self.back).wait()
+                self.across(i).wait_recv()
+                self.load(2, i).start()
+            for i in behind:
+                self.load(2, i).wait()
+                add_to(self.vt.at[i % self.back], self.va[i % self.ring].astype(F32))
+                self.outward(i).start()
+                self.keep(i).start()
+
+    def finish(self):
+        @pl.when(self.plane.inner_plane)
+        def _():
+            for i in range(self.count - self.ring, self.count):
+                self.across(i).wait_send()
+            for i in range(self.count - self.back, self.count):
+                self.outward(i).wait_send()
+                self.keep(i).wait()
+
+        @pl.when(self.plane.outer_plane)
+        def _():
+            def one(i, carry):
+                self.inward(i).wait_send()
+                remote(
+                    self.held.at[i], self.total.at[i], self.sent.at[2, i], self.got.at[2, i], self.plane.inner
+                ).wait_recv()
+                return carry
+
+            lax.fori_loop(0, self.count, one, 0)
+
+
+HELD_BACK = 14
+
+
+def tail_kernel(
+    sc_ref, dpart, xe, gg, ug, hid, dyw, q_in, kv_in, mixed_in, invl_in, soft_in, og_in, after_in, qraw_in, kraw_in,
+    x_in, h_in, n2_in, wo_in, wq_in, wk_in, wv_in, fg_ref, wr_ref, cos_ref, sin_ref, gain_ref, qg_ref, kg_ref, loss_ref,
+    total, ig_out, dense_out, small_out, held, r1, r2,
+    dx_own, dx_sb, dx_da, dx_db, dx_rx, dx_ry, kv_sb, kv_da, kv_db, kv_rx, kv_ry,
+    l1, va, vt, dsh, dr1, dr2, dfin, sm_mine, sm_got,
+    sent_dx, got_dx, sent_kv, got_kv, sent_de, got_de, sent_z, got_z, local_z, sent_ag, got_ag, sent_sm, got_sm, local,
+):
+    plane = Plane()
+    slots, rows = x_in.shape[0], x_in.shape[1]
+    width = x_in.shape[2]
+    group = dpart.shape[0]
+    owned = xe.shape[1]
+    eff = gg.shape[3]
+    each = lambda body, count=slots: lax.fori_loop(0, count, lambda s, c: (body(s), c)[1], 0)
+    line = Line(plane, held, r1, r2, total, (l1, va, vt), (sent_z, got_z, local_z))
+    scat_dx = Scatter(
+        plane, lambda k, s: dx_own.at[k, s], lambda k, s: dpart.at[plane.other[k], s],
+        (dx_sb, dx_da, dx_db, dx_rx, dx_ry), (sent_dx, got_dx),
+    )
+    own_load = lambda k, s: pltpu.make_async_copy(dpart.at[plane.own[k], s], dx_own.at[k, s], local.at[0])
+    for k in range(4):
+        each(lambda s: own_load(k, s).start())
+    plane.barrier(True)
+    each(scat_dx.start)
+
+    def expert_phase(xeb, ggb, ugb, hidb, dywb, gb, sems, out_sem):
+        def loads(e):
+            slot = e % 2
+            return [
+                pltpu.make_async_copy(source.at[:, e], there.at[slot], sems.at[slot, n])
+                for n, (source, there) in enumerate(((xe, xeb), (gg, ggb), (ug, ugb), (hid, hidb), (dyw, dywb)))
+            ]
+
+        def store(e):
+            return pltpu.make_async_copy(gb.at[e % 2], held.at[pl.ds(6 * e, 6)], out_sem.at[e % 2])
+
+        def send(e):
+            store(e).wait()
+            todo = [6 * e + n for n in range(6) if 6 * e + n < HELD_BACK]
+            if todo:
+                @pl.when(plane.outer_plane)
+                def _():
+                    for i in todo:
+                        line.inward(i).start()
+
+        flat = lambda ref, slot: ref[slot].reshape(ref.shape[1] * ref.shape[2], ref.shape[3])
+        for copy in loads(0):
+            copy.start()
+        for e in range(owned):
+            slot = e % 2
+            if e + 1 < owned:
+                for copy in loads(e + 1):
+                    copy.start()
+            for copy in loads(e):
+                copy.wait()
+            half = width // 2
+            for n, (left, right) in enumerate(((xeb, ggb), (xeb, ugb))):
+                part = dot_tn(flat(left, slot), flat(right, slot)).astype(BF16)
+                gb[slot, 2 * n] = part[:half]
+                gb[slot, 2 * n + 1] = part[half:]
+            part = dot_tn(flat(hidb, slot), flat(dywb, slot)).astype(BF16)
+            gb[slot, 4] = part[:, :half]
+            gb[slot, 5] = part[:, half:]
+            store(e).start()
+            if e >= 1:
+                send(e - 1)
+            if e == 1:
+                for k in range(4):
+                    each(lambda s: own_load(k, s).wait())
+                each(scat_dx.first)
+            if e == 2:
+                each(scat_dx.second)
+        send(owned - 1)
+        each(scat_dx.third)
+
+    held_rows = (xe.shape[0], xe.shape[2])
+    pl.run_scoped(
+        expert_phase,
+        pltpu.VMEM((2,) + held_rows + (width,), BF16),
+        pltpu.VMEM((2,) + held_rows + (eff,), BF16),
+        pltpu.VMEM((2,) + held_rows + (eff,), BF16),
+        pltpu.VMEM((2,) + held_rows + (eff,), BF16),
+        pltpu.VMEM((2,) + held_rows + (width,), BF16),
+        pltpu.VMEM((2, 6, eff, width // 2), BF16),
+        pltpu.SemaphoreType.DMA((2, 5)),
+        pltpu.SemaphoreType.DMA((2,)),
+    )
+    line.advance(0)
+    here = plane.me
+    chunk = 2 * rows
+    chunks = (here + 2) // 2
+    qw = q_in.shape[2]
+    kw = kraw_in.shape[2]
+    tiles = qw // 256
+
+    def rest(dkv, ag_s, at_s, lg_s, mixed_s, q_s, qgg, kgg, agg, fgg, mg_s):
+        scat_kv = Scatter(
+            plane, lambda k, s: dkv.at[plane.own[k], s], lambda k, s: dkv.at[plane.other[k], s],
+            (kv_sb, kv_da, kv_db, kv_rx, kv_ry), (sent_kv, got_kv),
+        )
+        for ref in (qgg, kgg, agg, fgg):
+            ref[...] = jnp.zeros_like(ref)
+        mixed_load = pltpu.make_async_copy(mixed_in, mixed_s, local.at[1])
+        mixed_load.start()
+
+        def attention_phase(wo, qb, kvb, invlb, softb, ogb, afterb, qrawb, sems):
+            wo_load = pltpu.make_async_copy(wo_in, wo, local.at[2])
+            wo_load.start()
+
+            def loads(s):
+                slot = lax.rem(s, 2)
+                out = [pltpu.make_async_copy(kv_in.at[:, s], kvb.at[slot], sems.at[slot, 0])]
+                for n, (source, there) in enumerate(
+                    ((q_in, qb), (invl_in, invlb), (soft_in, softb), (og_in, ogb), (after_in, afterb), (qraw_in, qrawb))
+                ):
+                    out.append(pltpu.make_async_copy(source.at[s], there.at[slot], sems.at[slot, n + 1]))
+                return out
+
+            for s in range(2):
+                for copy in loads(s):
+                    copy.start()
+            wo_load.wait()
+            mixed_load.wait()
+
+            def one_slot(s):
+                slot = lax.rem(s, 2)
+                for copy in loads(s):
+                    copy.wait()
+                dx = scat_dx.result(s)
+                valid = (row_of((rows, 1)) + here * rows < sc_ref[s]).astype(F32)
+                slab = dx[:, width:]
+                half = slab.shape[1] // 2
+                soft = softb[slot]
+                soft_grad = jnp.where(lane_of(slab.shape) < half, slab + pltpu.roll(slab, half, 1), 0.0)
+                chosen = soft * (soft_grad - jnp.sum(soft * soft_grad, axis=-1, keepdims=True))
+                logit_grad = chosen.astype(BF16)
+                lg_s[s] = logit_grad
+                normed_grad = dx[:, :width] + dot_nt(logit_grad, wr_ref[...])
+                back, gain_grad = rms_backward(normed_grad, afterb[slot], fg_ref[...])
+                fgg[...] += gain_grad
+                after_grad = ogb[slot] + back
+                ag_s[s] = after_grad
+                attn_grad = (valid * after_grad).astype(BF16)
+                at_s[s] = attn_grad
+                mixed_grad = dot_nt(attn_grad, wo[...]).astype(BF16)
+                for t in range(tiles):
+                    mg_s[t] = mixed_grad[:, t * 256 : (t + 1) * 256]
+
+                def one_tile(t, carry):
+                    lanes = pl.ds(pl.multiple_of(t * 256, 256), 256)
+                    key_lanes = pl.ds(pl.multiple_of(t * 256, 256), LANES)
+                    value_lanes = pl.ds(pl.multiple_of(t * 256 + LANES, LANES), LANES)
+                    q4 = stack_heads(qb[slot, :, lanes], True).astype(BF16)
+                    do4_f = stack_heads(mg_s[t].astype(F32) * invlb[slot, :, lanes], True)
+                    do4 = do4_f.astype(BF16)
+                    product = do4_f * stack_heads(mixed_s[s, :, lanes], False)
+                    delta = lax.dot_general(
+                        jnp.ones((8, LANES), F32), product, (((1,), (1,)), ((), ())),
+                        preferred_element_type=F32, precision=lax.Precision.HIGHEST,
+                    )[0:1]
+
+                    def step(index, sum_q, masked):
+                        two = pl.ds(2 * index, 2)
+                        keys = kvb[slot, two, :, key_lanes].reshape(chunk, LANES)
+                        values = kvb[slot, two, :, value_lanes].reshape(chunk, LANES)
+                        weight = jnp.exp2(dot_nt(keys, q4) * EXP2_SCALE)
+                        if masked:
+                            at = lax.rem(lane_of(weight.shape), rows) + here * rows
+                            weight = jnp.where(row_of(weight.shape) + index * chunk <= at, weight, 0.0)
+                        pressure = dot_nt(values, do4)
+                        score_grad = (weight * (pressure - delta) * SCALE).astype(BF16)
+                        key_grad = dot(score_grad, q4).astype(BF16)
+                        value_grad = dot(weight.astype(BF16), do4).astype(BF16)
+                        dkv[two, s, :, key_lanes] = key_grad.reshape(2, rows, LANES)
+                        dkv[two, s, :, value_lanes] = value_grad.reshape(2, rows, LANES)
+                        return sum_q + dot_tn(score_grad, keys)
+
+                    total_q = lax.fori_loop(
+                        0, chunks - 1, lambda i, c: step(i, c, False), jnp.zeros((4 * rows, LANES), F32)
+                    )
+                    total_q = step(chunks - 1, total_q, True)
+
+                    def blank(index, carry):
+                        dkv[pl.ds(2 * index, 2), s, :, lanes] = jnp.zeros((2, rows, 256), BF16)
+                        return carry
+
+                    lax.fori_loop(chunks, group // 2, blank, 0)
+                    dq = unstack_heads(total_q).astype(BF16).astype(F32)
+                    for n in range(2):
+                        part = slice(n * LANES, (n + 1) * LANES)
+                        here_lanes = pl.ds(pl.multiple_of(t * 256 + n * LANES, LANES), LANES)
+                        raw, gain = rope_backward(
+                            dq[:, part], qrawb[slot, :, here_lanes], qg_ref[...], cos_ref[...], sin_ref[...]
+                        )
+                        q_s[s, :, here_lanes] = raw.astype(BF16)
+                        qgg[...] += gain
+                    return carry
+
+                lax.fori_loop(0, tiles, one_tile, 0)
+
+                @pl.when(s + 2 < slots)
+                def _():
+                    for copy in loads(s + 2):
+                        copy.start()
+
+                scat_kv.start(s)
+
+                @pl.when(s >= 1)
+                def _():
+                    scat_kv.first(s - 1)
+                    scat_kv.second(s - 1)
+
+                @pl.when(s >= 2)
+                def _():
+                    scat_kv.third(s - 2)
+
+            lax.fori_loop(0, 2, lambda s, c: (one_slot(s), c)[1], 0)
+            line.advance(1)
+            lax.fori_loop(2, slots, lambda s, c: (one_slot(s), c)[1], 0)
+            line.advance(2)
+
+        pl.run_scoped(
+            attention_phase,
+            pltpu.VMEM(wo_in.shape, BF16),
+            pltpu.VMEM((2, rows, qw), BF16),
+            pltpu.VMEM((2, group, rows, 2 * kw), BF16),
+            pltpu.VMEM((2, rows, qw), F32),
+            pltpu.VMEM((2, rows, LANES), F32),
+            pltpu.VMEM((2, rows, width), F32),
+            pltpu.VMEM((2, rows, width), F32),
+            pltpu.VMEM((2, rows, qw), F32),
+            pltpu.SemaphoreType.DMA((2, 7)),
+        )
+        each(scat_dx.drain)
+
+        def last_phase(wq, wk, wv, xb, krawb, hb, n2b, k_s, v_s):
+            loads = [
+                pltpu.make_async_copy(source, there, local.at[2 + n])
+                for n, (source, there) in enumerate(
+                    ((wq_in, wq), (wk_in, wk), (wv_in, wv), (x_in, xb), (kraw_in, krawb), (h_in, hb),
+                     (n2_in.at[:, :, pl.ds(0, width)], n2b))
+                )
+            ]
+            for copy in loads:
+                copy.start()
+            scat_kv.first(slots - 1)
+            scat_kv.second(slots - 1)
+            scat_kv.third(slots - 2)
+            flat = lambda ref: ref[...].reshape(slots * rows, ref.shape[2])
+            for copy in loads:
+                copy.wait()
+            shards, shard_rows = group, width // group
+
+            def product(left, right, place):
+                def one(n, carry):
+                    lanes = pl.ds(pl.multiple_of(n * 256, 256), 256)
+                    column = right[:, :, lanes].reshape(slots * rows, 256)
+                    place(n, dot_tn(flat(left), column).astype(BF16).reshape(shards, shard_rows, 256))
+                    return carry
+
+                lax.fori_loop(0, right.shape[2] // 256, one, 0)
+
+            def aside(k):
+                def place(n, value):
+                    lanes = pl.ds(pl.multiple_of(n * 256, 256), 256)
+                    for shard in range(shards):
+                        dx_own[k + shard // slots, shard % slots, :, lanes] = value[shard]
+
+                return place
+
+            product(mixed_s, at_s, aside(0))
+            scat_kv.third(slots - 1)
+            product(hb, q_s, aside(2))
+            router = dot_tn(flat(lg_s), flat(n2b))
+            experts = small_out.shape[0] - 8
+            sm_mine[0] = jnp.zeros(sm_mine.shape[1:], F32)
+            sm_mine[0, :experts] = router[:experts]
+            sm_mine[0, experts + 1 : experts + 2] = fgg[...]
+            sm_mine[0, experts + 2 : experts + 3, :LANES] = qgg[...]
+            sm_mine[0, experts + 4 : experts + 5, :LANES] = loss_ref[...]
+            line.advance(3)
+
+            def one_slot(s):
+                grads = scat_kv.result(s)
+                for t in range(kw // LANES):
+                    lanes = slice(t * LANES, (t + 1) * LANES)
+                    at = 2 * t * LANES
+                    grad = grads[:, at : at + LANES].astype(BF16).astype(F32)
+                    raw, gain = rope_backward(grad, krawb[s, :, lanes], kg_ref[...], cos_ref[...], sin_ref[...])
+                    k_s[s, :, lanes] = raw.astype(BF16)
+                    kgg[...] += gain
+                    v_s[s, :, lanes] = grads[:, at + LANES : at + 2 * LANES].astype(BF16)
+                normed_grad = dot_nt(q_s[s], wq[...]) + dot_nt(k_s[s], wk[...]) + dot_nt(v_s[s], wv[...])
+                back, gain = rms_backward(normed_grad, xb[s].astype(F32), gain_ref[...])
+                agg[...] += gain
+                ag_s[s] += back
+                pltpu.make_async_copy(ag_s.at[s], ig_out.at[s], local.at[0]).start()
+
+            each(one_slot)
+            each(scat_kv.drain)
+            line.advance(4)
+            sm_mine[0, experts : experts + 1] = agg[...]
+            sm_mine[0, experts + 3 : experts + 4, :LANES] = kgg[...]
+            for shard in range(shards):
+                dkv[shard, 2] = dx_own[shard // slots, shard % slots, :, :width]
+                dkv[shard, 0] = dx_own[2 + shard // slots, shard % slots, :, :width]
+
+            def beside(first):
+                def place(n, value):
+                    dkv[:, 1, :, pl.ds(pl.multiple_of(first + n * 256, 256), 256)] = value
+
+                return place
+
+            product(hb, k_s, beside(0))
+            product(hb, v_s, beside(kw))
+
+        pl.run_scoped(
+            last_phase,
+            pltpu.VMEM(wq_in.shape, BF16),
+            pltpu.VMEM(wk_in.shape, BF16),
+            pltpu.VMEM(wv_in.shape, BF16),
+            pltpu.VMEM(x_in.shape, BF16),
+            pltpu.VMEM(kraw_in.shape, F32),
+            pltpu.VMEM(h_in.shape, BF16),
+            pltpu.VMEM((slots, rows, width), BF16),
+            pltpu.VMEM((slots, rows, kw), BF16),
+            pltpu.VMEM((slots, rows, kw), BF16),
+        )
+        kinds = 3
+        narrow = pl.ds(0, width)
+        again = [dx_sb.at[:, :, :, narrow]] + [r.at[:, :, narrow] for r in (dx_da, dx_db, dx_rx, dx_ry)]
+        scat_de = Scatter(
+            plane, lambda k, s: dkv.at[plane.own[k], s], lambda k, s: dkv.at[plane.other[k], s],
+            again, (sent_de, got_de),
+        )
+        by_kind = lambda body: each(body, kinds)
+        by_kind(scat_de.start)
+        small = lambda n, who: remote(sm_mine.at[n], sm_got.at[n], sent_sm.at[n], got_sm.at[n], who)
+
+        def small_step(n, who):
+            small(n, who).wait_recv()
+            sm_mine[n + 1] = sm_mine[n] + sm_got[n]
+
+        small(0, plane.sib).start()
+        by_kind(scat_de.first)
+        small_step(0, plane.sib)
+        small(1, plane.xn).start()
+        by_kind(scat_de.second)
+        small_step(1, plane.xn)
+        small(2, plane.yn).start()
+        by_kind(scat_de.third)
+        small_step(2, plane.yn)
+        line.advance(5)
+
+        def one_kind(s):
+            dsh[s] = scat_de.result(s).astype(BF16)
+
+        by_kind(one_kind)
+        by_kind(scat_de.drain)
+        each(lambda s: pltpu.make_async_copy(ag_s.at[s], ig_out.at[s], local.at[0]).wait())
+
+    pl.run_scoped(
+        rest,
+        pltpu.VMEM((group, slots, rows, 2 * kw), BF16),
+        pltpu.VMEM((slots, rows, width), F32),
+        pltpu.VMEM((slots, rows, width), BF16),
+        pltpu.VMEM((slots, rows, LANES), BF16),
+        pltpu.VMEM((slots, rows, qw), BF16),
+        pltpu.VMEM((slots, rows, qw), BF16),
+        pltpu.VMEM((1, LANES), F32),
+        pltpu.VMEM((1, LANES), F32),
+        pltpu.VMEM((1, width), F32),
+        pltpu.VMEM((1, width), F32),
+        pltpu.VMEM((tiles, rows, 256), BF16),
+    )
+
+    small_in = remote(sm_mine.at[3], sm_got.at[3], sent_sm.at[3], got_sm.at[3], plane.inner)
+    small_across = remote(sm_mine.at[4], sm_got.at[4], sent_sm.at[4], got_sm.at[4], plane.across)
+    small_back = remote(sm_mine.at[5], sm_got.at[5], sent_sm.at[5], got_sm.at[5], plane.outer)
+    dense_in = remote(dsh, dr1, sent_sm.at[6], got_sm.at[6], plane.inner)
+    dense_across = remote(dsh, dr2, sent_sm.at[7], got_sm.at[7], plane.across)
+    dense_back = remote(dfin, dfin, sent_sm.at[8], got_sm.at[8], plane.outer)
+
+    @pl.when(plane.outer_plane)
+    def _():
+        small_in.start()
+        dense_in.start()
+
+        def one(i, carry):
+            line.inward(i).start()
+            return carry
+
+        lax.fori_loop(HELD_BACK, line.count, one, 0)
+
+    line.advance(6)
+
+    @pl.when(plane.inner_plane)
+    def _():
+        small_in.wait_recv()
+        sm_mine[4] = sm_mine[3] + sm_got[3]
+        small_across.start()
+        dense_in.wait_recv()
+        add_to(dsh, dr1[...].astype(F32))
+        dense_across.start()
+
+    line.advance(7)
+
+    @pl.when(plane.inner_plane)
+    def _():
+        small_across.wait_recv()
+        sm_mine[5] = sm_mine[4] + sm_got[4]
+        small_back.start()
+        dense_across.wait_recv()
+        dfin[...] = (dsh[...].astype(F32) + dr2[...].astype(F32)).astype(BF16)
+        dense_back.start()
+        small_out[...] = sm_mine[5]
+
+    line.advance(8)
+
+    @pl.when(plane.outer_plane)
+    def _():
+        small_back.wait_recv()
+        dense_back.wait_recv()
+        small_out[...] = sm_got[5]
+
+    gather = Gather(plane, dfin, dense_out, sent_ag, got_ag, local)
+    gather.start()
+    line.advance(9)
+    gather.forward()
+    line.advance(10)
+    gather.finish()
+    line.advance(11)
+    line.advance(12)
+    line.finish()
+    for n, who in ((0, plane.sib), (1, plane.xn), (2, plane.yn)):
+        remote(sm_mine.at[n], sm_got.at[n], sent_sm.at[n], got_sm.at[n], who).wait_send()
+
+    @pl.when(plane.outer_plane)
+    def _():
+        small_in.wait_send()
+        dense_in.wait_send()
+
+    @pl.when(plane.inner_plane)
+    def _():
+        small_across.wait_send()
+        small_back.wait_send()
+        dense_across.wait_send()
+        dense_back.wait_send()
+
+
+class Gather:
+    def __init__(self, plane, mine, out, sent, got, local):
+        self.plane, self.mine, self.out, self.sent, self.got, self.local = plane, mine, out, sent, got, local
+        self.n = mine.shape[0]
+        rows = mine.shape[1]
+        self.halves = (pl.ds(0, rows // 2), pl.ds(rows // 2, rows // 2))
+        self.at_x, self.at_y, self.at_d = plane.own[1], plane.own[2], plane.own[0]
+
+    def own(self, number, s):
+        who = (self.plane.xn, self.plane.yn, self.plane.sib)[number]
+        return remote(self.mine.at[s], self.out.at[self.plane.me, s], self.sent.at[number, s], self.got.at[number, s], who)
+
+    def keep(self, s):
+        return pltpu.make_async_copy(self.mine.at[s], self.out.at[self.plane.me, s], self.local.at[s])
+
+    def pass_on(self, number, s):
+        at = (self.at_x, self.at_y, self.at_d)[number]
+        view = self.out.at[at, s]
+        return remote(view, view, self.sent.at[3 + number, s], self.got.at[3 + number, s], self.plane.sib)
+
+    def far(self, number, s):
+        at, who = ((self.at_x, self.plane.yn), (self.at_y, self.plane.xn))[number]
+        view = self.out.at[at, s, self.halves[number]]
+        return remote(view, view, self.sent.at[6 + number, s], self.got.at[6 + number, s], who)
+
+    def start(self):
+        for s in range(self.n):
+            for number in range(3):
+                self.own(number, s).start()
+            self.keep(s).start()
+
+    def forward(self):
+        for s in range(self.n):
+            for number in range(2):
+                self.own(number, s).wait_recv()
+                self.far(number, s).start()
+                self.pass_on(number, s).start()
+
+    def finish(self):
+        for s in range(self.n):
+            for number in range(2):
+                self.far(number, s).wait_recv()
+            self.pass_on(2, s).start()
+        for s in range(self.n):
+            self.keep(s).wait()
+            self.own(2, s).wait_recv()
+            for number in range(3):
+                self.pass_on(number, s).wait_recv()
+                self.pass_on(number, s).wait_send()
+                self.own(number, s).wait_send()
+            for number in range(2):
+                self.far(number, s).wait_send()
+
+
+def tail(
+    slot_lengths, dpart, xe, gate_grad, up_grad, hidden, weighted, q, kv, mixed, invl, soft, out_grad, after, qraw, kraw,
+    x, h, n2, w_out, w_query, w_key, w_value, ffn_gain, router, cosine, sine, attn_gain, qg, kg, loss, experts, number,
+):
+    slots, rows, width = x.shape
+    group, unused, unused_rows, wide = dpart.shape
+    owned, eff = xe.shape[1], gate_grad.shape[3]
+    kw = kraw.shape[2]
+    chunks = 6 * owned
+    piece = (eff, width // 2)
+    kinds = 3
+    hbm = pl.BlockSpec(memory_space=pl.ANY)
+    vmem = pl.BlockSpec(memory_space=pltpu.VMEM)
+    smem = pl.BlockSpec(memory_space=pltpu.SMEM)
+    V, D = pltpu.VMEM, pltpu.SemaphoreType.DMA
+    half = rows // 2
+
+    def landing(n, lanes):
+        return [
+            V((4, n, rows, lanes), BF16), V((n, half, lanes), BF16), V((n, half, lanes), BF16),
+            V((n, rows, lanes), BF16), V((n, rows, lanes), BF16),
+        ]
+
+    small_rows = experts + 8
+    return pl.pallas_call(
+        tail_kernel,
+        in_specs=[smem] + [hbm] * 22 + [vmem] * 8,
+        out_specs=(hbm, hbm, hbm, vmem, hbm, hbm, hbm),
+        out_shape=(
+            jax.ShapeDtypeStruct((chunks,) + piece, BF16),
+            jax.ShapeDtypeStruct((slots, rows, width), F32),
+            jax.ShapeDtypeStruct((group, kinds, width // group, width), BF16),
+            jax.ShapeDtypeStruct((small_rows, width), F32),
+            jax.ShapeDtypeStruct((chunks,) + piece, BF16),
+            jax.ShapeDtypeStruct((chunks,) + piece, BF16),
+            jax.ShapeDtypeStruct((chunks,) + piece, BF16),
+        ),
+        scratch_shapes=[V((4, slots, rows, wide), BF16)]
+        + landing(slots, wide) + landing(slots, 2 * kw)
+        + [V((2,) + piece, BF16), V((4,) + piece, BF16), V((2,) + piece, BF16)]
+        + [V((kinds, rows, width), BF16)] * 4
+        + [V((6, small_rows, width), F32)] * 2
+        + [D((10, slots))] * 4 + [D((10, kinds))] * 2
+        + [D((3, chunks))] * 2 + [D((10,))]
+        + [D((8, kinds))] * 2 + [D((9,))] * 2 + [D((9,))],
+        compiler_params=pltpu.CompilerParams(collective_id=number, has_side_effects=True, vmem_limit_bytes=63 * MIB),
+        name="tail",
+    )(
+        slot_lengths, dpart, xe, gate_grad, up_grad, hidden, weighted, q, kv, mixed, invl, soft, out_grad, after, qraw,
+        kraw, x, h, n2, w_out, w_query, w_key, w_value, ffn_gain, router, cosine, sine, attn_gain, qg, kg, loss,
+    )
+
+
 def plane_gather(rows, fast, number):
     if fast:
         return all_gather(rows, number)
@@ -889,31 +1647,46 @@
     dpart, weighted, gate_grad, up_grad = experts_backward(
         scalars, grads, tokens, pick, gate_part, up_part, hidden, w_gate, w_up, w_down
     )
-    expert_grads = lax.psum(expert_weights(xe, gate_grad, up_grad, hidden, weighted), "dp")
-    dx = plane_scatter(dpart, fast, 5)
-    dq, dkv_parts, after_grad, attn_grad, logit_grad, ffn_gain_grad = attend_backward(
-        scalars, q, kv, mixed, invl, dx, soft, out_grad, after, fg, router, w_out
-    )
-    dkv = plane_scatter(dkv_parts, fast, 6)
-    input_grad, dense, router_grad, query_gg, key_gg, attn_gg = finish(
-        dq, dkv, qraw, kraw, block_input, after_grad, cosine, sine, ag, qg, kg,
-        w_query, w_key, w_value, h, mixed, attn_grad, xg, logit_grad,
-    )
     if fast:
-        shards, kinds, shard_rows, unused = dense.shape
-        shard = reduce_scatter(dense.reshape(shards, 2 * kinds, shard_rows // 2, width), 7, F32)
-        shard = lax.psum(shard, "dp").astype(BF16)
-        dense = all_gather(shard, 8).reshape(shards, kinds, shard_rows, width)
+        eff = w_gate.shape[2]
+        owned = w_gate.shape[0]
+        total, input_grad, dense, sums = tail(
+            slot_lengths, dpart, xe, gate_grad, up_grad, hidden, weighted, q, kv, mixed, invl, soft, out_grad, after,
+            qraw, kraw, block_input, h, xg, w_out, w_query, w_key, w_value, fg, router, cosine, sine, ag, qg, kg,
+            jnp.broadcast_to(loss_part[None, None], (1, LANES)), expert_total, 5,
+        )[:4]
+        total = total.reshape(owned, 6, eff, width // 2)
+        expert_grads = (
+            total[:, 0:2].reshape(owned, width, eff),
+            total[:, 2:4].reshape(owned, width, eff),
+            jnp.concatenate([total[:, 4], total[:, 5]], axis=2),
+        )
+        dense = [dense[:, k].reshape(width, width).astype(F32) for k in range(3)]
+        tops = sums[expert_total : expert_total + 5]
+        small = (
+            tops[2, :HEAD] + tops[2, HEAD : 2 * HEAD], tops[3, :HEAD] + tops[3, HEAD : 2 * HEAD], tops[0], tops[1],
+            sums[:expert_total].T, tops[4, 0],
+        )
     else:
+        expert_grads = lax.psum(expert_weights(xe, gate_grad, up_grad, hidden, weighted), "dp")
+        dx = plane_scatter(dpart, fast, 5)
+        dq, dkv_parts, after_grad, attn_grad, logit_grad, ffn_gain_grad = attend_backward(
+            scalars, q, kv, mixed, invl, dx, soft, out_grad, after, fg, router, w_out
+        )
+        dkv = plane_scatter(dkv_parts, fast, 6)
+        input_grad, dense, router_grad, query_gg, key_gg, attn_gg = finish(
+            dq, dkv, qraw, kraw, block_input, after_grad, cosine, sine, ag, qg, kg,
+            w_query, w_key, w_value, h, mixed, attn_grad, xg, logit_grad,
+        )
         dense = lax.psum(dense, ("dp", "context", "experts"))
-    dense = [dense[:, k].reshape(width, width).astype(F32) for k in range(3)]
-    small = lax.psum(
-        (
-            query_gg[0, :HEAD] + query_gg[0, HEAD:], key_gg[0, :HEAD] + key_gg[0, HEAD:], attn_gg[0],
-            ffn_gain_grad[0], router_grad[:, :expert_total], loss_part,
-        ),
-        ("dp", "context", "experts"),
-    )
+        dense = [dense[:, k].reshape(width, width).astype(F32) for k in range(3)]
+        small = lax.psum(
+            (
+                query_gg[0, :HEAD] + query_gg[0, HEAD:], key_gg[0, :HEAD] + key_gg[0, HEAD:], attn_gg[0],
+                ffn_gain_grad[0], router_grad[:, :expert_total], loss_part,
+            ),
+            ("dp", "context", "experts"),
+        )
     key_width = w_key.shape[1]
     return (
         small[5] / (count_all * width),

time: 1090 us -> 749 us (0.69)
  waiting for transfers between devices: 353 us -> 0 us
  Pallas kernels: 546 us -> 682 us
  blocking collectives: 120 us -> 0 us
  between operations: 17.2 us -> 3.78 us
    psum x2 -> x0, waiting for transfers between devices: 353 us -> none  [the longest x1 353 us: per_device(): lax.psum(expert_weights(xe, gate_grad, up_grad, hidden, weighted), 'dp')]
    pallas_call x3 -> x1, Pallas kernels: 77.8 us -> 386 us  [tail(): pl.pallas_call(tail_kernel, in_specs=[smem] + [hbm] * 22 + [vmem] * 8, ou...]
    pallas_call x4 -> x1, Pallas kernels: 181 us -> 41.9 us  [reduce_scatter(): pl.pallas_call(rs_kernel, out_shape=jax.ShapeDtypeStruct((n, r, w), dt),...]
    psum x2 -> x0, blocking collectives: 120 us -> none  [the longest x1 82.4 us: per_device(): shard = lax.psum(shard, 'dp').astype(BF16)]
    pallas_call x4 -> x3, Pallas kernels: 166 us -> 134 us  [all_gather(): pl.pallas_call(ag_kernel, out_shape=jax.ShapeDtypeStruct((8,) + x.shape,...]
  transfers between devices with their start and end apart: 2 -> 0, of which waited for: 1 -> 0; matrix products, arithmetic and copies ran while one was open for 1% -> 0% of each run, Pallas kernels for 8% -> 0%
where the time goes in v2:
time: 749 us; the launch traced here: 738 us
  Pallas kernels  682 us (91%)
  other arithmetic  31.6 us (4%)
  local copies, waits for them, and re-layouts  20.9 us (3%)
    pallas_call x1, Pallas kernels, tail(): pl.pallas_call(tail_kernel, in_specs=[smem] + [hbm] * 22 + [vmem] * 8, ou...  386 us
    pallas_call x3, Pallas kernels, all_gather(): pl.pallas_call(ag_kernel, out_shape=jax.ShapeDtypeStruct((8,) + x.shape,...  134 us
    pallas_call x1, Pallas kernels, experts_backward(): pl.pallas_call(experts_backward_kernel, grid_spec=pltpu.PrefetchScalarGri...  46.3 us
    pallas_call x1, Pallas kernels, experts_forward(): pl.pallas_call(experts_forward_kernel, grid_spec=pltpu.PrefetchScalarGrid...  42 us
    pallas_call x1, Pallas kernels, reduce_scatter(): pl.pallas_call(rs_kernel, out_shape=jax.ShapeDtypeStruct((n, r, w), dt),...  41.9 us
    pallas_call x1, Pallas kernels, attend(): pl.pallas_call(attend_kernel, grid_spec=pltpu.PrefetchScalarGridSpec(num_...  22.9 us

profile of v2, /device:TPU:0, one launch (start us, length us, event | category | flops | bytes accessed | tf_op | source)
XLA Modules:
  0.0 738.5 jit_solution(5680292361991800410)
XLA Ops:
  0.7 1.3 reduce_sum.18
  4.0 1.3 maximum_bitcast_fusion
  5.4 1.0 fusion.1
  6.3 1.6 copy.32.routes_ref
  7.9 1.0 copy.31
  8.9 0.7 pad.4.wr_ref
  9.7 9.4 %project.1 = (bf16[4,128,1024]{2,1,0:T(8,128)(2,1)}, bf16[4,128,1024]{2,1,0:T(8,128)(2,1)}, bf16[4,128,1024]{2,1,0:T(8,128)(2,1)}, f32[4,128,1024]{2,1,0:T(8,128)}, f32[4,128,512]{2,1,0:T(8,128)}) custom-call(bf16[4,128,1024]{2,1,0:T(8,128)(2,1)} %x_in.1, f32[1,1024]{1,0:T(1,128)} %bitcast.44, bf16[1024,1024]{1,0:T(8,128)(2,1)} %wq_in.1, ...), custom_call_target="tpu_custom_call" | custom-call | tf_op jit(solution)/shard_map/project/pallas_call | solution.py:141
  19.1 41.4 %ag.3.kv_ref.kv_in = bf16[8,4,128,1024]{3,2,1,0:T(8,128)(2,1)} custom-call(bf16[4,128,1024]{2,1,0:T(8,128)(2,1)} %get-tuple-element.40.x_ref), custom_call_target="tpu_custom_call" | custom-call | tf_op jit(solution)/shard_map/ag/pallas_call | solution.py:767
  60.4 22.9 %attend.1 = (bf16[4,128,1024]{2,1,0:T(8,128)(2,1)}, f32[4,128,1024]{2,1,0:T(8,128)}, f32[4,128,1024]{2,1,0:T(8,128)}, bf16[4,128,1152]{2,1,0:T(8,128)(2,1)}, f32[4,128,128]{2,1,0:T(8,128)}) custom-call(s32[5]{0:T(128)} %pad_add_fusion.sc_ref, bf16[4,128,1024]{2,1,0:T(8,128)(2,1)} %get-tuple-element.39.q_ref.q_in, bf16[8,4,128,1024]{3,2,1,0:T(8,128)(2,1)} %ag.3.kv_ref.kv_in, ...), custom_call_target="tpu_custom_call" | custom-call | tf_op jit(solution)/shard_map/attend/pallas_call | solution.py:238
  83.4 53.9 %ag.4.xg_ref.slab_ref = bf16[8,4,128,1152]{3,2,1,0:T(8,128)(2,1)} custom-call(bf16[4,128,1152]{2,1,0:T(8,128)(2,1)} %get-tuple-element.42.x_ref.n2_in), custom_call_target="tpu_custom_call" | custom-call | tf_op jit(solution)/shard_map/ag/pallas_call | solution.py:767
  137.3 42.0 %experts_forward.1 = (bf16[4,4,320,256]{3,2,1,0:T(8,128)(2,1)}, bf16[4,4,320,1024]{3,2,1,0:T(8,128)(2,1)}, f32[4,4,320,512]{3,2,1,0:T(8,128)}, f32[4,4,320,512]{...) custom-call(s32[5]{0:T(128)} %pad_add_fusion.sc_ref, ...), custom_call_target="tpu_custom_call" | custom-call | tf_op jit(solution)/shard_map/experts_forward/pallas_call | solution.py:352
  179.3 41.9 %rs.1 = f32[4,128,1024]{2,1,0:T(8,128)} custom-call(bf16[8,4,128,1024]{3,2,1,0:T(8,128)(2,1)} %get-tuple-element.43.p_ref), custom_call_target="tpu_custom_call" | custom-call | tf_op jit(solution)/shard_map/rs/pallas_call | solution.py:831
  221.2 3.2 fusion.8
  224.4 2.7 multiply_reduce_fusion
  227.1 1.2 broadcast_in_dim.42.loss_ref
  228.2 38.9 %ag.5.dy_ref = bf16[8,4,128,1024]{3,2,1,0:T(8,128)(2,1)} custom-call(bf16[4,128,1024]{2,1,0:T(8,128)(2,1)} %get-tuple-element.75.x_ref), custom_call_target="tpu_custom_call" | custom-call | tf_op jit(solution)/shard_map/ag/pallas_call | solution.py:767
  267.1 46.3 %experts_backward.1 = (bf16[8,4,128,1152]{3,2,1,0:T(8,128)(2,1)}, bf16[4,4,320,1024]{3,2,1,0:T(8,128)(2,1)}, bf16[4,4,320,512]{3,2,1,0:T(8,128)(2,1)}, bf16[4,4,320,512]{3,2,1,0:T(8,128)(2,1)}) custom-call(s32[5]{0:T(128)} %pad_add_fusion.sc_ref, bf16[8,4,128,1024]{3,2,1,0:T(8,128)(2,1)} %ag.5.dy_ref, bf16[8,4,128,1152]{3,2,1,0:T(8,128)(2,1)} %ag.4.xg_ref.slab_ref, ...), custom_call_target="tpu_custom_call" | custom-call | tf_op jit(solution)/shard_map/experts_backward/pallas_call | solution.py:429
  313.5 385.5 %tail.1 = (bf16[24,512,512]{2,1,0:T(8,128)(2,1)}, f32[4,128,1024]{2,1,0:T(8,128)}, bf16[8,3,128,1024]{3,2,1,0:T(8,128)(2,1)}, f32[40,1024]{1,0:T(8,128)}, bf16[2...) custom-call(s32[4]{0:T(128)} %copy-done.3, ...), custom_call_target="tpu_custom_call" | custom-call | tf_op jit(solution)/shard_map/tail/pallas_call | solution.py:1569
  699.0 1.2 slice.59
  700.8 1.4 add_bitcast_fusion
  702.2 1.4 fusion.12
  703.7 1.6 slice_bitcast_fusion.2
  705.3 2.5 slice_bitcast_fusion.1
  707.8 4.0 fusion.9
  711.8 4.6 maximum_convert_fusion
  716.4 4.9 bitcast_convert_fusion
  721.2 1.1 fusion.10
  722.3 2.6 bitcast_convert_fusion.2
  725.5 2.6 fusion.11
  728.1 2.6 bitcast_convert_fusion.3
  730.7 4.9 bitcast_convert_fusion.1
  735.5 1.3 copy.38
  (19 shorter events, 2.0 us)
Async XLA Ops:
  3.4 57.1 %copy-start.3 = (s32[4]{0:T(128)}, s32[4]{0:T(128)S(1)}, u32[]{:S(2)}) copy-start(s32[4]{0:T(128)S(1)} %dynamic_slice.3.sc_ref) | copy-start | bytes 52
  179.3 41.9 %copy-start = (f32[4,128,1024]{2,1,0:T(8,128)S(1)}, f32[4,128,1024]{2,1,0:T(8,128)}, u32[]{:S(2)}) copy-start(f32[4,128,1024]{2,1,0:T(8,128)} %get-tuple-element.41.after_in) | copy-start | bytes 6291460
  221.2 3.2 copy-start.2
  711.8 9.5 %slice-start = ((s8[6291456]{0:T(1024)(128)(4,1)}), s8[2097152]{0:T(1024)(128)(4,1)S(1)}, s32[]{:S(2)}) async-start(s8[6291456]{0:T(1024)(128)(4,1)} %bitcast.42), calls=%async_computation | async-start | bytes 4194304
  716.4 4.9 slice-start.1
  730.7 4.9 copy-start.1

commit v3 on v2

--- a/solution.py
+++ b/solution.py
@@ -717,124 +717,437 @@
 def remote(src, dst, ss, rs, dev):
     return pltpu.make_async_remote_copy(src_ref=src, dst_ref=dst, send_sem=ss, recv_sem=rs, device_id=dev, device_id_type=MESH)
 
-def ag_kernel(x_ref, o_ref, lsem, ss, rs):
-    z = lax.axis_index("dp"); c = lax.axis_index("context"); y = lax.axis_index("experts")
-    cs = c + 1 - 2 * lax.rem(c, 2)
-    cx = lax.rem(c + 2, 4)
-    yy = 1 - y
-    sib, xn, yn = (z, cs, y), (z, cx, y), (z, c, yy)
-    me = c * 2 + y
-    gx = cx * 2 + y; gy = c * 2 + yy; gd = cx * 2 + yy
-    bar = pltpu.get_barrier_semaphore()
-    for d in (sib, xn, yn):
-        pl.semaphore_signal(bar, inc=1, device_id=d, device_id_type=MESH)
-    pl.semaphore_wait(bar, 3)
-    n = x_ref.shape[0]
-    h = n // 2
-    loc = [pltpu.make_async_copy(x_ref.at[s], o_ref.at[me, s], lsem.at[s]) for s in range(n)]
-    sx = [remote(x_ref.at[s], o_ref.at[me, s], ss.at[0, s], rs.at[0, s], xn) for s in range(n)]
-    sy = [remote(x_ref.at[s], o_ref.at[me, s], ss.at[1, s], rs.at[1, s], yn) for s in range(n)]
-    sc = [remote(x_ref.at[s], o_ref.at[me, s], ss.at[2, s], rs.at[2, s], sib) for s in range(n)]
-    fx = [remote(o_ref.at[gx, s], o_ref.at[gx, s], ss.at[3, s], rs.at[3, s], sib) for s in range(n)]
-    fy = [remote(o_ref.at[gy, s], o_ref.at[gy, s], ss.at[4, s], rs.at[4, s], sib) for s in range(n)]
-    fd = [remote(o_ref.at[gd, s], o_ref.at[gd, s], ss.at[5, s], rs.at[5, s], sib) for s in range(n)]
-    dg = [remote(o_ref.at[gx, s], o_ref.at[gx, s], ss.at[6, s], rs.at[6, s], yn) if s < h else
-          remote(o_ref.at[gy, s], o_ref.at[gy, s], ss.at[6, s], rs.at[6, s], xn) for s in range(n)]
-    for i in range(n):
-        sx[i].start()
-        sy[(i + h) % n].start()
-    for s in range(n):
-        sc[s].start()
-        loc[s].start()
-    for i in range(n):
-        a = i; b = (i + h) % n
-        sx[a].wait_recv()
-        if a < h: dg[a].start()
-        fx[a].start()
-        sy[b].wait_recv()
-        if b >= h: dg[b].start()
-        fy[b].start()
-    for i in range(h):
-        for s in (i, i + h):
-            dg[s].wait_recv(); fd[s].start()
-    for s in range(n):
-        sc[s].wait_recv(); fx[s].wait_recv(); fy[s].wait_recv(); fd[s].wait_recv()
-        loc[s].wait()
-        for k in (sx, sy, sc, fx, fy, fd, dg): k[s].wait_send()
-
-def all_gather(x, cid):
-    n = x.shape[0]
-    return pl.pallas_call(ag_kernel,
-        out_shape=jax.ShapeDtypeStruct((8,) + x.shape, x.dtype),
-        in_specs=[pl.BlockSpec(memory_space=pl.ANY)], out_specs=pl.BlockSpec(memory_space=pl.ANY),
-        scratch_shapes=[pltpu.SemaphoreType.DMA((n,)), pltpu.SemaphoreType.DMA((7, n)), pltpu.SemaphoreType.DMA((7, n))],
-        compiler_params=pltpu.CompilerParams(collective_id=cid, has_side_effects=True), name="ag")(x)
-
-def rs_kernel(p_ref, o_ref, own, other, sb, q, dx, dy, rx, ry, lsem, ss, rs):
-    z = lax.axis_index("dp"); c = lax.axis_index("context"); y = lax.axis_index("experts")
-    core = lax.rem(c, 2)
-    cs = c + 1 - 2 * core
-    cx = lax.rem(c + 2, 4)
-    yy = 1 - y
-    sib, xn, yn = (z, cs, y), (z, cx, y), (z, c, yy)
-    bar = pltpu.get_barrier_semaphore()
-    for d in (sib, xn, yn):
-        pl.semaphore_signal(bar, inc=1, device_id=d, device_id_type=MESH)
-    n = p_ref.shape[1]
-    h = n // 2
-    chips = [(cx, yy), (cx, y), (c, yy), (c, y)]
-    idx = [a * 2 + b for a, b in chips]
-    oth = [(a + 1 - 2 * core) * 2 + b for a, b in chips]
-    ld = [[pltpu.make_async_copy(p_ref.at[idx[k], s], own.at[k, s], lsem.at[k, s]) for s in range(n)] for k in range(4)]
-    st = [[remote(p_ref.at[oth[k], s], sb.at[k, s], ss.at[k, s], rs.at[k, s], sib) for s in range(n)] for k in range(4)]
-    for k in range(4):
-        for s in range(n):
-            ld[k][s].start()
-    pl.semaphore_wait(bar, 3)
-    for k in range(4):
-        for s in range(n):
-            st[k][s].start()
-    dgs = [remote(q.at[0, s], dx.at[s], ss.at[4, s], rs.at[4, s], xn) if s < h else
-           remote(q.at[0, s], dy.at[s - h], ss.at[4, s], rs.at[4, s], yn) for s in range(n)]
-    tx = [remote(q.at[1, s], rx.at[s], ss.at[5, s], rs.at[5, s], xn) for s in range(n)]
-    ty = [remote(q.at[2, s], ry.at[s], ss.at[6, s], rs.at[6, s], yn) for s in range(n)]
-    f32 = jnp.float32
-    def pair(k, s):
-        ld[k][s].wait(); st[k][s].wait_recv()
-        return own[k, s].astype(f32) + sb[k, s].astype(f32)
-    for i in range(h):
-        for s in (i, i + h):
-            q[0, s] = pair(0, s).astype(q.dtype); dgs[s].start()
-    for i in range(h):
-        q[1, i] = pair(1, i).astype(q.dtype); tx[i].start()
-        q[2, i + h] = pair(2, i + h).astype(q.dtype); ty[i + h].start()
-    for i in range(h):
-        a = pair(2, i)
-        dgs[i].wait_recv()
-        q[2, i] = (a + dx[i].astype(f32)).astype(q.dtype); ty[i].start()
-        b = pair(1, i + h)
-        dgs[i + h].wait_recv()
-        q[1, i + h] = (b + dy[i].astype(f32)).astype(q.dtype); tx[i + h].start()
-    for i in range(h):
-        for s in (i, i + h):
-            a = pair(3, s)
-            tx[s].wait_recv(); ty[s].wait_recv()
-            o_ref[s] = (a + rx[s].astype(f32) + ry[s].astype(f32)).astype(o_ref.dtype)
-    for s in range(n):
-        for k in st: k[s].wait_send()
-        for k in (dgs, tx, ty): k[s].wait_send()
-
-def reduce_scatter(p, cid, dt):
-    _, n, r, w = p.shape
-    h = n // 2
-    V = pltpu.VMEM
-    return pl.pallas_call(rs_kernel,
-        out_shape=jax.ShapeDtypeStruct((n, r, w), dt),
-        in_specs=[pl.BlockSpec(memory_space=pl.ANY)], out_specs=pl.BlockSpec(memory_space=pltpu.VMEM),
-        scratch_shapes=[V((4, n, r, w), p.dtype), V((1, 8, 128), p.dtype), V((4, n, r, w), p.dtype), V((3, n, r, w), p.dtype),
-            V((h, r, w), p.dtype), V((h, r, w), p.dtype), V((n, r, w), p.dtype), V((n, r, w), p.dtype),
-            pltpu.SemaphoreType.DMA((4, n)), pltpu.SemaphoreType.DMA((7, n)), pltpu.SemaphoreType.DMA((7, n))],
-        compiler_params=pltpu.CompilerParams(collective_id=cid, has_side_effects=True, vmem_limit_bytes=60 * 2**20), name="rs")(p)
+
+class Slots:
+    def __init__(self, plane, mine, out, sent, got, local):
+        self.plane, self.mine, self.out, self.sent, self.got, self.local = plane, mine, out, sent, got, local
+        rows = mine.shape[1]
+        self.halves = (pl.ds(0, rows // 2), pl.ds(rows // 2, rows // 2))
+        self.at = (plane.own[1], plane.own[2], plane.own[0])
+
+    def own(self, number, s):
+        who = (self.plane.xn, self.plane.yn, self.plane.sib)[number]
+        return remote(self.mine.at[s], self.out.at[self.plane.me, s], self.sent.at[number, s], self.got.at[number, s], who)
+
+    def keep(self, s):
+        return pltpu.make_async_copy(self.mine.at[s], self.out.at[self.plane.me, s], self.local.at[s])
+
+    def pass_on(self, number, s):
+        view = self.out.at[self.at[number], s]
+        return remote(view, view, self.sent.at[3 + number, s], self.got.at[3 + number, s], self.plane.sib)
+
+    def far(self, number, s):
+        at, who = ((self.at[0], self.plane.yn), (self.at[1], self.plane.xn))[number]
+        view = self.out.at[at, s, self.halves[number]]
+        return remote(view, view, self.sent.at[6 + number, s], self.got.at[6 + number, s], who)
+
+    def start(self, s):
+        for number in range(3):
+            self.own(number, s).start()
+        self.keep(s).start()
+
+    def forward(self, s):
+        for number in range(2):
+            self.own(number, s).wait_recv()
+            self.far(number, s).start()
+            self.pass_on(number, s).start()
+
+    def settle(self, s):
+        for number in range(2):
+            self.far(number, s).wait_recv()
+        self.pass_on(2, s).start()
+
+    def arrive(self, s):
+        self.keep(s).wait()
+        self.own(2, s).wait_recv()
+        for number in range(3):
+            self.pass_on(number, s).wait_recv()
+
+    def drain(self, s):
+        for number in range(3):
+            self.own(number, s).wait_send()
+            self.pass_on(number, s).wait_send()
+        for number in range(2):
+            self.far(number, s).wait_send()
+
+
+def front_kernel(
+    sc_ref, x_in, teacher_in, routes_ref, wq_in, wk_in, wv_in, wo_in, wg_in, wu_in, wd_in,
+    gain_ref, fg_ref, qg_ref, kg_ref, cos_ref, sin_ref, wr_ref, scale_ref,
+    h_out, q_out, qraw_out, kraw_out, kv_out, mixed_out, invl_out, after_out, soft_out, tokens_out,
+    pick_out, xe_out, gp_out, up_out, hid_out, y_out, og_out, loss_out, grads_out,
+    sb, da, db, rx, ry, parts, wg, wu, wd, after_s, xg_s, dy_s,
+    sent_kv, got_kv, loc_kv, sent_xg, got_xg, loc_xg, sent_dy, got_dy, loc_dy, sent_rs, got_rs, wsem, local,
+):
+    plane = Plane()
+    slots, rows, width = x_in.shape
+    group = kv_out.shape[0]
+    qw, kw = wq_in.shape[1], wk_in.shape[1]
+    tiles = qw // 256
+    here = plane.me
+    owned = wg_in.shape[0]
+    first = here * owned
+    wide = xg_s.shape[2]
+    each = lambda body, start=0, stop=slots: lax.fori_loop(start, stop, lambda s, c: (body(s), c)[1], 0)
+    row_gather = Slots(plane, xg_s, tokens_out, sent_xg, got_xg, loc_xg)
+    grad_gather = Slots(plane, dy_s, grads_out, sent_dy, got_dy, loc_dy)
+    scatter = Scatter(
+        plane, lambda k, s: parts.at[plane.own[k], s], lambda k, s: parts.at[plane.other[k], s],
+        (sb, da, db, rx, ry), (sent_rs, got_rs),
+    )
+    expert_loads = [
+        pltpu.make_async_copy(source, there, wsem.at[n])
+        for n, (source, there) in enumerate(((wg_in, wg), (wu_in, wu), (wd_in, wd)))
+    ]
+
+    def first_phase(wq, wk, wv, wo, xb, kvl, q_s, h_s, qraw_s, kraw_s, kvb, mixed_s, invl_s, soft_s, acc, sems, out_sems):
+        loads = [
+            pltpu.make_async_copy(source, there, sems.at[n])
+            for n, (source, there) in enumerate(((x_in, xb), (wk_in, wk), (wv_in, wv), (wq_in, wq), (wo_in, wo)))
+        ]
+        for copy in loads:
+            copy.start()
+        for copy in expert_loads:
+            copy.start()
+        kv_gather = Slots(plane, kvl, kv_out, sent_kv, got_kv, loc_kv)
+        plane.barrier(False)
+        for copy in loads[:4]:
+            copy.wait()
+
+        def project_two(s):
+            two = pl.ds(s, 2)
+            x = xb[two].astype(F32).reshape(2 * rows, width)
+            unit, unused = rms_parts(x)
+            normed = (unit * gain_ref[...]).astype(BF16)
+            h_s[two] = normed.reshape(2, rows, width)
+            cosine = jnp.concatenate([cos_ref[...]] * 2, axis=0)
+            sine = jnp.concatenate([sin_ref[...]] * 2, axis=0)
+            k_raw = dot(normed, wk[...])
+            kraw_s[two] = k_raw.reshape(2, rows, kw)
+            value = dot(normed, wv[...]).astype(BF16)
+            for tile in range(kw // LANES):
+                lanes = slice(tile * LANES, (tile + 1) * LANES)
+                turned = rope_forward(k_raw[:, lanes], kg_ref[...], cosine, sine)
+                at = 2 * tile * LANES
+                kvl[two, :, at : at + LANES] = turned.astype(BF16).reshape(2, rows, LANES)
+                kvl[two, :, at + LANES : at + 2 * LANES] = value[:, lanes].reshape(2, rows, LANES)
+            kv_gather.start(s)
+            kv_gather.start(s + 1)
+            q_raw = dot(normed, wq[...])
+            qraw_s[two] = q_raw.reshape(2, rows, qw)
+            for tile in range(qw // LANES):
+                lanes = slice(tile * LANES, (tile + 1) * LANES)
+                turned = rope_forward(q_raw[:, lanes], qg_ref[...], cosine, sine)
+                q_s[two, :, lanes] = turned.astype(BF16).reshape(2, rows, LANES)
+
+        lax.fori_loop(0, slots // 2, lambda n, c: (project_two(2 * n), c)[1], 0)
+        keeps = [
+            pltpu.make_async_copy(source, there, out_sems.at[n])
+            for n, (source, there) in enumerate(((h_s, h_out), (q_s, q_out), (qraw_s, qraw_out), (kraw_s, kraw_out)))
+        ]
+        for copy in keeps:
+            copy.start()
+        kv_gather.forward(0)
+        kv_gather.forward(1)
+        kv_gather.settle(0)
+        loads[4].wait()
+
+        def attend_slot(s):
+            load = pltpu.make_async_copy(kv_out.at[:, s], kvb, sems.at[5])
+            load.start()
+            load.wait()
+            chunk = 2 * rows
+            chunks = (here + 2) // 2
+            acc[...] = jnp.zeros_like(acc)
+
+            def one_tile(t, carry):
+                lanes = pl.ds(pl.multiple_of(t * 256, 256), 256)
+                key_lanes = pl.ds(pl.multiple_of(t * 256, 256), LANES)
+                value_lanes = pl.ds(pl.multiple_of(t * 256 + LANES, LANES), LANES)
+                q4 = stack_heads(q_s[s, :, lanes], True).astype(BF16)
+
+                def step(index, carry, masked):
+                    mass, total = carry
+                    two = pl.ds(2 * index, 2)
+                    keys = kvb[two, :, key_lanes].reshape(chunk, LANES)
+                    values = kvb[two, :, value_lanes].reshape(chunk, LANES)
+                    weight = jnp.exp2(dot_nt(q4, keys) * EXP2_SCALE)
+                    if masked:
+                        at = lax.rem(row_of(weight.shape), rows) + here * rows
+                        weight = jnp.where(lane_of(weight.shape) + index * chunk <= at, weight, 0.0)
+                    for part in range(chunk // LANES):
+                        mass = mass + weight[:, part * LANES : (part + 1) * LANES]
+                    return mass, total + dot(weight.astype(BF16), values)
+
+                blank = jnp.zeros((4 * rows, LANES), F32)
+                state = lax.fori_loop(0, chunks - 1, lambda i, c: step(i, c, False), (blank, blank))
+                mass, total = step(chunks - 1, state, True)
+                inverse = 1.0 / jnp.sum(mass, axis=-1, keepdims=True)
+                mixed = unstack_heads(total * inverse).astype(BF16)
+                mixed_s[s, :, lanes] = mixed
+                invl_s[s, :, lanes] = unstack_heads(jnp.broadcast_to(inverse, total.shape))
+                acc[...] += dot(mixed, wo[pl.ds(pl.multiple_of(t * 256, 256), 256)])
+                return carry
+
+            lax.fori_loop(0, tiles, one_tile, 0)
+            valid = (row_of((rows, 1)) + here * rows < sc_ref[s]).astype(F32)
+            after = xb[s].astype(F32) + valid * acc[...]
+            after_s[s] = after
+            unit, unused = rms_parts(after)
+            normed = (unit * fg_ref[...]).astype(BF16)
+            xg_s[s, :, :width] = normed
+            logits = dot(normed, wr_ref[...])
+            lanes = lane_of(logits.shape)
+            routes = routes_ref[s]
+            chosen = lanes == routes[:, 0:1]
+            for k in range(1, routes.shape[1]):
+                chosen = chosen | (lanes == routes[:, k : k + 1])
+            top = jnp.max(jnp.where(chosen, logits, -1e30), axis=-1, keepdims=True)
+            weight = jnp.where(chosen, jnp.exp(jnp.minimum(logits - top, 0.0)), 0.0)
+            soft = weight / jnp.sum(weight, axis=-1, keepdims=True)
+            soft_s[s] = soft
+            gates = soft * valid
+            high = gates.astype(BF16).astype(F32)
+            xg_s[s, :, width:] = (high + pltpu.roll(gates - high, LANES // 2, 1)).astype(BF16)
+
+        def one(t):
+            kv_gather.arrive(t)
+            attend_slot(t)
+            row_gather.start(t)
+
+            @pl.when(t <= slots - 3)
+            def _():
+                kv_gather.forward(t + 2)
+
+            @pl.when(t <= slots - 2)
+            def _():
+                kv_gather.settle(t + 1)
+
+            @pl.when(t >= 1)
+            def _():
+                row_gather.forward(t - 1)
+
+            @pl.when(t >= 2)
+            def _():
+                row_gather.settle(t - 2)
+
+        each(one)
+        keeps += [
+            pltpu.make_async_copy(source, there, out_sems.at[4 + n])
+            for n, (source, there) in enumerate(
+                ((mixed_s, mixed_out), (invl_s, invl_out), (after_s, after_out), (soft_s, soft_out))
+            )
+        ]
+        for copy in keeps[4:]:
+            copy.start()
+        each(kv_gather.drain)
+        for copy in keeps:
+            copy.wait()
+
+    V, D = pltpu.VMEM, pltpu.SemaphoreType.DMA
+    full = lambda lanes, kind: V((slots, rows, lanes), kind)
+    pl.run_scoped(
+        first_phase,
+        V(wq_in.shape, BF16), V(wk_in.shape, BF16), V(wv_in.shape, BF16), V(wo_in.shape, BF16),
+        full(width, BF16), full(2 * kw, BF16), full(qw, BF16), full(width, BF16), full(qw, F32), full(kw, F32),
+        V((group, rows, 2 * kw), BF16), full(qw, BF16), full(qw, F32), full(LANES, F32), V((rows, width), F32),
+        D((6,)), D((8,)),
+    )
+    sources, double, pairs, held = group, 2 * rows, group // 2, group // 2 * PAIR
+
+    def second_phase(tok, pick_s, xe_s, gp_s, up_s, hid_s, gates, ybuf, teach, y_s, og_s, sems, out_sems):
+        teacher_load = pltpu.make_async_copy(teacher_in, teach, sems.at[1])
+        teacher_load.start()
+        for copy in expert_loads:
+            copy.wait()
+        teacher_load.wait()
+        loss_out[...] = jnp.zeros_like(loss_out)
+        keeps = lambda s: [
+            pltpu.make_async_copy(source, there.at[s], out_sems.at[n])
+            for n, (source, there) in enumerate(
+                ((pick_s, pick_out), (xe_s, xe_out), (gp_s, gp_out), (up_s, up_out), (hid_s, hid_out))
+            )
+        ]
+
+        def experts_slot(s, between):
+            load = pltpu.make_async_copy(tokens_out.at[:, s], tok, sems.at[0])
+            load.start()
+
+            @pl.when(s >= 1)
+            def _():
+                for copy in keeps(s - 1):
+                    copy.wait()
+
+            load.wait()
+            slab = tok[:, :, width:].reshape(sources * rows, LANES)
+            chosen = (lane_of((8, LANES)) == row_of((8, LANES)) + first).astype(BF16)
+            routed = dot_nt(chosen, slab) > 0.0
+            before, after = row_of((double, double)), lane_of((double, double))
+            count = ((before < after) & (before // rows == after // rows)).astype(BF16)
+            place = lax.broadcasted_iota(jnp.int32, (PAIR, double), 0)
+            offset = (lane_of((8, double)) // rows) * MOST
+            for p in range(pairs):
+                mask = routed[:, p * double : (p + 1) * double]
+                rank = dot(mask.astype(F32).astype(BF16), count).astype(jnp.int32) + offset
+                rank = jnp.where(mask, rank, -1)
+                pick = jnp.concatenate(
+                    [(place == rank[e : e + 1, :]).astype(F32).astype(BF16) for e in range(owned)], axis=0
+                )
+                pick_s[p] = pick
+                picked = dot(pick, tok[2 * p : 2 * p + 2, :, :width].reshape(double, width)).astype(BF16)
+                scale = row_gates(dot(pick, slab[p * double : (p + 1) * double]), first, owned)
+                for e in range(owned):
+                    xe_s[e, p * PAIR : (p + 1) * PAIR] = picked[e * PAIR : (e + 1) * PAIR]
+                    gates[e, p * PAIR : (p + 1) * PAIR] = jnp.broadcast_to(
+                        scale[e * PAIR : (e + 1) * PAIR], (PAIR, LANES)
+                    )
+
+            def one_expert(e, carry):
+                rows_in = xe_s[e]
+                gate_part = dot(rows_in, wg[e])
+                up_part = dot(rows_in, wu[e])
+                gp_s[e] = gate_part
+                up_s[e] = up_part
+                hidden = (gate_part * jax.nn.sigmoid(gate_part) * up_part).astype(BF16)
+                hid_s[e] = hidden
+                result = (dot(hidden, wd[e]) * gates[e][:, 0:1]).astype(BF16)
+                for p in range(pairs):
+                    ybuf[p, e] = result[p * PAIR : (p + 1) * PAIR]
+                return carry
+
+            lax.fori_loop(0, owned // 2, one_expert, 0)
+            between()
+            lax.fori_loop(owned // 2, owned, one_expert, 0)
+            for p in range(pairs):
+                back = dot_tn(pick_s[p], ybuf[p].reshape(owned * PAIR, width))
+                parts[2 * p : 2 * p + 2, s] = back.astype(BF16).reshape(2, rows, width)
+            for copy in keeps(s):
+                copy.start()
+
+        def loss_slot(s):
+            output = after_s[s] + scatter.result(s)
+            y_s[s] = output.astype(BF16)
+            valid = (row_of((rows, 1)) + here * rows < sc_ref[s]).astype(F32)
+            difference = valid * (output - teach[s].astype(F32))
+            square = jnp.sum(difference * difference, axis=0, keepdims=True)
+            loss_out[...] += square
+            grad = difference * scale_ref[0]
+            og_s[s] = grad
+            dy_s[s] = grad.astype(BF16)
+            grad_gather.start(s)
+
+        def one(t):
+            row_gather.arrive(t)
+
+            def between():
+                @pl.when(t == 0)
+                def _():
+                    row_gather.settle(slots - 2)
+                    row_gather.forward(slots - 1)
+
+                @pl.when(t == 1)
+                def _():
+                    row_gather.settle(slots - 1)
+
+                @pl.when(t >= 1)
+                def _():
+                    scatter.first(t - 1)
+                    scatter.second(t - 1)
+
+                @pl.when(t == slots - 1)
+                def _():
+                    grad_gather.forward(0)
+
+            experts_slot(t, between)
+            scatter.start(t)
+
+            @pl.when(t >= 1)
+            def _():
+                scatter.third(t - 1)
+
+            @pl.when(t >= 2)
+            def _():
+                loss_slot(t - 2)
+
+        each(one)
+        last = slots - 1
+        scatter.first(last)
+        scatter.second(last)
+        loss_slot(last - 1)
+        grad_gather.settle(0)
+        grad_gather.forward(1)
+        scatter.third(last)
+        grad_gather.settle(1)
+        loss_slot(last)
+        outs = [
+            pltpu.make_async_copy(source, there, sems.at[n]) for n, (source, there) in enumerate(((y_s, y_out), (og_s, og_out)))
+        ]
+        for copy in outs:
+            copy.start()
+        for s in range(2, slots):
+            grad_gather.forward(s)
+            grad_gather.settle(s)
+        each(grad_gather.arrive)
+        each(grad_gather.drain)
+        each(row_gather.drain)
+        each(scatter.drain)
+        for copy in keeps(last) + outs:
+            copy.wait()
+
+    eff = wg_in.shape[2]
+    pl.run_scoped(
+        second_phase,
+        V((group, rows, wide), BF16), V((pairs, owned * PAIR, double), BF16), V((owned, held, width), BF16),
+        V((owned, held, eff), F32), V((owned, held, eff), F32), V((owned, held, eff), BF16), V((owned, held, LANES), F32),
+        V((pairs, owned, PAIR, width), BF16), full(width, BF16), full(width, BF16), full(width, F32), D((2,)), D((5,)),
+    )
+
+
+def front(
+    slot_lengths, x, teacher, routes, w_query, w_key, w_value, w_out, w_gate, w_up, w_down,
+    attn_gain, ffn_gain, qg, kg, cosine, sine, router, scale, group, number,
+):
+    slots, rows, width = x.shape
+    qw, kw = w_query.shape[1], w_key.shape[1]
+    owned, unused, eff = w_gate.shape
+    wide = width + LANES
+    pairs = group // 2
+    held = pairs * PAIR
+    hbm = pl.BlockSpec(memory_space=pl.ANY)
+    vmem = pl.BlockSpec(memory_space=pltpu.VMEM)
+    smem = pl.BlockSpec(memory_space=pltpu.SMEM)
+    V, D = pltpu.VMEM, pltpu.SemaphoreType.DMA
+    half = rows // 2
+    mine = lambda lanes, kind: jax.ShapeDtypeStruct((slots, rows, lanes), kind)
+    all_of = lambda lanes: jax.ShapeDtypeStruct((group, slots, rows, lanes), BF16)
+    saved = lambda *dims: jax.ShapeDtypeStruct((slots,) + dims, BF16)
+    outs = (
+        mine(width, BF16), mine(qw, BF16), mine(qw, F32), mine(kw, F32), all_of(2 * kw), mine(qw, BF16), mine(qw, F32),
+        mine(width, F32), mine(LANES, F32), all_of(wide),
+        saved(pairs, owned * PAIR, 2 * rows), saved(owned, held, width),
+        jax.ShapeDtypeStruct((slots, owned, held, eff), F32), jax.ShapeDtypeStruct((slots, owned, held, eff), F32),
+        saved(owned, held, eff), mine(width, BF16), mine(width, F32), jax.ShapeDtypeStruct((1, width), F32), all_of(width),
+    )
+    return pl.pallas_call(
+        front_kernel,
+        in_specs=[smem, hbm, hbm, vmem] + [hbm] * 7 + [vmem] * 7 + [smem],
+        out_specs=(hbm,) * 17 + (vmem, hbm),
+        out_shape=outs,
+        scratch_shapes=[
+            V((4, slots, rows, width), BF16), V((slots, half, width), BF16), V((slots, half, width), BF16),
+            V((slots, rows, width), BF16), V((slots, rows, width), BF16),
+            V((group, slots, rows, width), BF16),
+            V(w_gate.shape, BF16), V(w_up.shape, BF16), V(w_down.shape, BF16),
+            V((slots, rows, width), F32), V((slots, rows, wide), BF16), V((slots, rows, width), BF16),
+        ]
+        + [D((8, slots)), D((8, slots)), D((slots,))] * 3
+        + [D((10, slots)), D((10, slots)), D((3,)), D((1,))],
+        compiler_params=pltpu.CompilerParams(collective_id=number, has_side_effects=True, vmem_limit_bytes=63 * MIB),
+        name="front",
+    )(
+        slot_lengths, x, teacher, routes, w_query, w_key, w_value, w_out, w_gate, w_up, w_down,
+        attn_gain, ffn_gain, qg, kg, cosine, sine, router, scale,
+    )
 
 
 def add_to(ref, value):
@@ -982,36 +1295,61 @@
         )[number]
         return pltpu.make_async_copy(source.at[i], there, self.local.at[self.ring + 2 * number + i % 2])
 
-    def advance(self, j):
-        steps = self.count // 2
-        ahead = [2 * j, 2 * j + 1] if j < steps else []
-        behind = [2 * j - 2, 2 * j - 1] if j >= 1 else []
-
+    def when(self, fact, body):
+        if isinstance(fact, bool):
+            if fact:
+                body()
+        else:
+            pl.when(fact)(body)
+
+    def take(self, i):
+        def wait():
+            self.across(i - self.ring).wait_send()
+
+        self.when(i >= self.ring, wait)
+        self.load(1, i).start()
+        self.inward(i).wait_recv()
+        self.load(0, i).start()
+
+    def give(self, i):
+        self.load(1, i).wait()
+        self.load(0, i).wait()
+        add_to(self.va.at[i % self.ring], self.l1[i % 2].astype(F32))
+        self.across(i).start()
+
+    def fetch(self, i):
+        def wait():
+            self.outward(i - self.back).wait_send()
+            self.keep(i - self.back).wait()
+
+        self.when(i >= self.back, wait)
+        self.across(i).wait_recv()
+        self.load(2, i).start()
+
+    def settle(self, i):
+        self.load(2, i).wait()
+        add_to(self.vt.at[i % self.back], self.va[i % self.ring].astype(F32))
+        self.outward(i).start()
+        self.keep(i).start()
+
+    def move(self, i, lag=2):
         @pl.when(self.plane.inner_plane)
         def _():
-            for i in ahead:
-                if i >= self.ring:
-                    self.across(i - self.ring).wait_send()
-                self.load(1, i).start()
-            for i in ahead:
-                self.inward(i).wait_recv()
-                self.load(0, i).start()
-            for i in ahead:
-                self.load(1, i).wait()
-                self.load(0, i).wait()
-                add_to(self.va.at[i % self.ring], self.l1[i % 2].astype(F32))
-                self.across(i).start()
-            for i in behind:
-                if i >= self.back:
-                    self.outward(i - self.back).wait_send()
-                    self.keep(i - self.back).wait()
-                self.across(i).wait_recv()
-                self.load(2, i).start()
-            for i in behind:
-                self.load(2, i).wait()
-                add_to(self.vt.at[i % self.back], self.va[i % self.ring].astype(F32))
-                self.outward(i).start()
-                self.keep(i).start()
+            self.take(i)
+            self.when(i >= lag, lambda: self.fetch(i - lag))
+            self.give(i)
+            self.when(i >= lag, lambda: self.settle(i - lag))
+
+    def wind_up(self, start):
+        @pl.when(self.plane.inner_plane)
+        def _():
+            for i in range(start, self.count + 1):
+                if i < self.count:
+                    self.take(i)
+                    self.give(i)
+                for n in ([start - 2] if i == start else []) + [i - 1]:
+                    self.fetch(n)
+                    self.settle(n)
 
     def finish(self):
         @pl.when(self.plane.inner_plane)
@@ -1049,6 +1387,7 @@
     slots, rows = x_in.shape[0], x_in.shape[1]
     width = x_in.shape[2]
     group = dpart.shape[0]
+    kinds = dsh.shape[0]
     owned = xe.shape[1]
     eff = gg.shape[3]
     each = lambda body, count=slots: lax.fori_loop(0, count, lambda s, c: (body(s), c)[1], 0)
@@ -1060,9 +1399,6 @@
     own_load = lambda k, s: pltpu.make_async_copy(dpart.at[plane.own[k], s], dx_own.at[k, s], local.at[0])
     for k in range(4):
         each(lambda s: own_load(k, s).start())
-    plane.barrier(True)
-    each(scat_dx.start)
-
     def expert_phase(xeb, ggb, ugb, hidb, dywb, gb, sems, out_sem):
         def loads(e):
             slot = e % 2
@@ -1071,12 +1407,12 @@
                 for n, (source, there) in enumerate(((xe, xeb), (gg, ggb), (ug, ugb), (hid, hidb), (dyw, dywb)))
             ]
 
-        def store(e):
-            return pltpu.make_async_copy(gb.at[e % 2], held.at[pl.ds(6 * e, 6)], out_sem.at[e % 2])
-
-        def send(e):
-            store(e).wait()
-            todo = [6 * e + n for n in range(6) if 6 * e + n < HELD_BACK]
+        def store(number):
+            return pltpu.make_async_copy(gb.at[number % 4], held.at[pl.ds(2 * number, 2)], out_sem.at[number % 4])
+
+        def send(number):
+            store(number).wait()
+            todo = [2 * number + n for n in range(2) if 2 * number + n < HELD_BACK]
             if todo:
                 @pl.when(plane.outer_plane)
                 def _():
@@ -1084,8 +1420,11 @@
                         line.inward(i).start()
 
         flat = lambda ref, slot: ref[slot].reshape(ref.shape[1] * ref.shape[2], ref.shape[3])
+        half = width // 2
         for copy in loads(0):
             copy.start()
+        plane.barrier(True)
+        each(scat_dx.start)
         for e in range(owned):
             slot = e % 2
             if e + 1 < owned:
@@ -1093,24 +1432,23 @@
                     copy.start()
             for copy in loads(e):
                 copy.wait()
-            half = width // 2
-            for n, (left, right) in enumerate(((xeb, ggb), (xeb, ugb))):
+            for n, (left, right) in enumerate(((xeb, ggb), (xeb, ugb), (hidb, dywb))):
+                number = 3 * e + n
                 part = dot_tn(flat(left, slot), flat(right, slot)).astype(BF16)
-                gb[slot, 2 * n] = part[:half]
-                gb[slot, 2 * n + 1] = part[half:]
-            part = dot_tn(flat(hidb, slot), flat(dywb, slot)).astype(BF16)
-            gb[slot, 4] = part[:, :half]
-            gb[slot, 5] = part[:, half:]
-            store(e).start()
-            if e >= 1:
-                send(e - 1)
+                gb[number % 4, 0] = part[:half] if n < 2 else part[:, :half]
+                gb[number % 4, 1] = part[half:] if n < 2 else part[:, half:]
+                store(number).start()
+                if number >= 1:
+                    send(number - 1)
             if e == 1:
                 for k in range(4):
                     each(lambda s: own_load(k, s).wait())
                 each(scat_dx.first)
             if e == 2:
                 each(scat_dx.second)
-        send(owned - 1)
+                line.move(0)
+        send(3 * owned - 1)
+        line.move(1)
         each(scat_dx.third)
 
     held_rows = (xe.shape[0], xe.shape[2])
@@ -1121,11 +1459,11 @@
         pltpu.VMEM((2,) + held_rows + (eff,), BF16),
         pltpu.VMEM((2,) + held_rows + (eff,), BF16),
         pltpu.VMEM((2,) + held_rows + (width,), BF16),
-        pltpu.VMEM((2, 6, eff, width // 2), BF16),
+        pltpu.VMEM((4, 2, eff, width // 2), BF16),
         pltpu.SemaphoreType.DMA((2, 5)),
-        pltpu.SemaphoreType.DMA((2,)),
+        pltpu.SemaphoreType.DMA((4,)),
     )
-    line.advance(0)
+    line.move(2)
     here = plane.me
     chunk = 2 * rows
     chunks = (here + 2) // 2
@@ -1254,10 +1592,11 @@
                 def _():
                     scat_kv.third(s - 2)
 
-            lax.fori_loop(0, 2, lambda s, c: (one_slot(s), c)[1], 0)
-            line.advance(1)
-            lax.fori_loop(2, slots, lambda s, c: (one_slot(s), c)[1], 0)
-            line.advance(2)
+            def slot_and_move(s):
+                one_slot(s)
+                line.move(s + 3)
+
+            each(slot_and_move)
 
         pl.run_scoped(
             attention_phase,
@@ -1278,7 +1617,7 @@
                 pltpu.make_async_copy(source, there, local.at[2 + n])
                 for n, (source, there) in enumerate(
                     ((wq_in, wq), (wk_in, wk), (wv_in, wv), (x_in, xb), (kraw_in, krawb), (h_in, hb),
-                     (n2_in.at[:, :, pl.ds(0, width)], n2b))
+                     (n2_in.at[plane.me, :, :, pl.ds(0, width)], n2b))
                 )
             ]
             for copy in loads:
@@ -1286,6 +1625,7 @@
             scat_kv.first(slots - 1)
             scat_kv.second(slots - 1)
             scat_kv.third(slots - 2)
+            line.move(slots + 3)
             flat = lambda ref: ref[...].reshape(slots * rows, ref.shape[2])
             for copy in loads:
                 copy.wait()
@@ -1310,6 +1650,7 @@
 
             product(mixed_s, at_s, aside(0))
             scat_kv.third(slots - 1)
+            line.move(slots + 4)
             product(hb, q_s, aside(2))
             router = dot_tn(flat(lg_s), flat(n2b))
             experts = small_out.shape[0] - 8
@@ -1317,8 +1658,8 @@
             sm_mine[0, :experts] = router[:experts]
             sm_mine[0, experts + 1 : experts + 2] = fgg[...]
             sm_mine[0, experts + 2 : experts + 3, :LANES] = qgg[...]
-            sm_mine[0, experts + 4 : experts + 5, :LANES] = loss_ref[...]
-            line.advance(3)
+            sm_mine[0, experts + 4 : experts + 5] = loss_ref[...]
+            line.move(slots + 5)
 
             def one_slot(s):
                 grads = scat_kv.result(s)
@@ -1338,7 +1679,7 @@
 
             each(one_slot)
             each(scat_kv.drain)
-            line.advance(4)
+            line.move(slots + 6)
             sm_mine[0, experts : experts + 1] = agg[...]
             sm_mine[0, experts + 3 : experts + 4, :LANES] = kgg[...]
             for shard in range(shards):
@@ -1353,6 +1694,7 @@
 
             product(hb, k_s, beside(0))
             product(hb, v_s, beside(kw))
+            line.move(slots + 7)
 
         pl.run_scoped(
             last_phase,
@@ -1366,7 +1708,6 @@
             pltpu.VMEM((slots, rows, kw), BF16),
             pltpu.VMEM((slots, rows, kw), BF16),
         )
-        kinds = 3
         narrow = pl.ds(0, width)
         again = [dx_sb.at[:, :, :, narrow]] + [r.at[:, :, narrow] for r in (dx_da, dx_db, dx_rx, dx_ry)]
         scat_de = Scatter(
@@ -1390,13 +1731,14 @@
         small(2, plane.yn).start()
         by_kind(scat_de.third)
         small_step(2, plane.yn)
-        line.advance(5)
+        line.move(slots + 8)
 
         def one_kind(s):
             dsh[s] = scat_de.result(s).astype(BF16)
 
         by_kind(one_kind)
         by_kind(scat_de.drain)
+        line.move(slots + 9)
         each(lambda s: pltpu.make_async_copy(ag_s.at[s], ig_out.at[s], local.at[0]).wait())
 
     pl.run_scoped(
@@ -1432,8 +1774,6 @@
 
         lax.fori_loop(HELD_BACK, line.count, one, 0)
 
-    line.advance(6)
-
     @pl.when(plane.inner_plane)
     def _():
         small_in.wait_recv()
@@ -1443,34 +1783,43 @@
         add_to(dsh, dr1[...].astype(F32))
         dense_across.start()
 
-    line.advance(7)
+    line.move(14)
 
     @pl.when(plane.inner_plane)
     def _():
         small_across.wait_recv()
         sm_mine[5] = sm_mine[4] + sm_got[4]
         small_back.start()
+        small_out[...] = sm_mine[5]
+
+    line.move(15)
+
+    @pl.when(plane.inner_plane)
+    def _():
         dense_across.wait_recv()
         dfin[...] = (dsh[...].astype(F32) + dr2[...].astype(F32)).astype(BF16)
         dense_back.start()
-        small_out[...] = sm_mine[5]
-
-    line.advance(8)
 
     @pl.when(plane.outer_plane)
     def _():
         small_back.wait_recv()
+        small_out[...] = sm_got[5]
         dense_back.wait_recv()
-        small_out[...] = sm_got[5]
-
-    gather = Gather(plane, dfin, dense_out, sent_ag, got_ag, local)
-    gather.start()
-    line.advance(9)
-    gather.forward()
-    line.advance(10)
-    gather.finish()
-    line.advance(11)
-    line.advance(12)
+
+    gather = Slots(plane, dfin, dense_out, sent_ag, got_ag, local)
+    for s in range(kinds):
+        gather.start(s)
+    line.move(16)
+    for s in range(kinds):
+        gather.forward(s)
+    line.move(17)
+    for s in range(kinds):
+        gather.settle(s)
+    line.move(18)
+    for s in range(kinds):
+        gather.arrive(s)
+        gather.drain(s)
+    line.wind_up(19)
     line.finish()
     for n, who in ((0, plane.sib), (1, plane.xn), (2, plane.yn)):
         remote(sm_mine.at[n], sm_got.at[n], sent_sm.at[n], got_sm.at[n], who).wait_send()
@@ -1486,60 +1835,6 @@
         small_back.wait_send()
         dense_across.wait_send()
         dense_back.wait_send()
-
-
-class Gather:
-    def __init__(self, plane, mine, out, sent, got, local):
-        self.plane, self.mine, self.out, self.sent, self.got, self.local = plane, mine, out, sent, got, local
-        self.n = mine.shape[0]
-        rows = mine.shape[1]
-        self.halves = (pl.ds(0, rows // 2), pl.ds(rows // 2, rows // 2))
-        self.at_x, self.at_y, self.at_d = plane.own[1], plane.own[2], plane.own[0]
-
-    def own(self, number, s):
-        who = (self.plane.xn, self.plane.yn, self.plane.sib)[number]
-        return remote(self.mine.at[s], self.out.at[self.plane.me, s], self.sent.at[number, s], self.got.at[number, s], who)
-
-    def keep(self, s):
-        return pltpu.make_async_copy(self.mine.at[s], self.out.at[self.plane.me, s], self.local.at[s])
-
-    def pass_on(self, number, s):
-        at = (self.at_x, self.at_y, self.at_d)[number]
-        view = self.out.at[at, s]
-        return remote(view, view, self.sent.at[3 + number, s], self.got.at[3 + number, s], self.plane.sib)
-
-    def far(self, number, s):
-        at, who = ((self.at_x, self.plane.yn), (self.at_y, self.plane.xn))[number]
-        view = self.out.at[at, s, self.halves[number]]
-        return remote(view, view, self.sent.at[6 + number, s], self.got.at[6 + number, s], who)
-
-    def start(self):
-        for s in range(self.n):
-            for number in range(3):
-                self.own(number, s).start()
-            self.keep(s).start()
-
-    def forward(self):
-        for s in range(self.n):
-            for number in range(2):
-                self.own(number, s).wait_recv()
-                self.far(number, s).start()
-                self.pass_on(number, s).start()
-
-    def finish(self):
-        for s in range(self.n):
-            for number in range(2):
-                self.far(number, s).wait_recv()
-            self.pass_on(2, s).start()
-        for s in range(self.n):
-            self.keep(s).wait()
-            self.own(2, s).wait_recv()
-            for number in range(3):
-                self.pass_on(number, s).wait_recv()
-                self.pass_on(number, s).wait_send()
-                self.own(number, s).wait_send()
-            for number in range(2):
-                self.far(number, s).wait_send()
 
 
 def tail(
@@ -1595,16 +1890,50 @@
     )
 
 
-def plane_gather(rows, fast, number):
-    if fast:
-        return all_gather(rows, number)
+def plane_gather(rows):
     return lax.all_gather(rows, ("context", "experts"), axis=0, tiled=False)
 
 
-def plane_scatter(parts, fast, number):
-    if fast:
-        return reduce_scatter(parts, number, F32)
+def plane_scatter(parts):
     return lax.psum_scatter(parts, ("context", "experts"), scatter_dimension=0, tiled=False).astype(F32)
+
+
+def unpack_kernel(gate_ref, up_ref, down_ref, dense_ref, dg_ref, du_ref, dd_ref, dq_ref, dk_ref, dv_ref, do_ref):
+    dg_ref[0] = gate_ref[0].astype(F32)
+    du_ref[0] = up_ref[0].astype(F32)
+    dd_ref[0] = down_ref[0].astype(F32)
+    half = dk_ref.shape[1]
+    dq_ref[...] = dense_ref[0, 0].astype(F32)
+    dk_ref[...] = dense_ref[0, 1, :, :half].astype(F32)
+    dv_ref[...] = dense_ref[0, 1, :, half:].astype(F32)
+    do_ref[...] = dense_ref[0, 2].astype(F32)
+
+
+def unpack(total, dense, key_width):
+    chunks, eff, half = total.shape
+    shards, kinds, shard_rows, width = dense.shape
+    owned = chunks // 6
+    steps = 2 * owned
+    piece = lambda kind: pl.BlockSpec((1, eff, half), lambda i: (i // 2 * 6 + 2 * kind + i % 2, 0, 0))
+    row = lambda lanes: pl.BlockSpec((shard_rows * shards // steps, lanes), lambda i: (i, 0))
+    shape = lambda *dims: jax.ShapeDtypeStruct(dims, F32)
+    return pl.pallas_call(
+        unpack_kernel,
+        grid=(steps,),
+        in_specs=[piece(0), piece(1), piece(2), pl.BlockSpec((1, kinds, shard_rows, width), lambda i: (i, 0, 0, 0))],
+        out_specs=(
+            pl.BlockSpec((1, eff, half), lambda i: (i // 2, i % 2, 0)),
+            pl.BlockSpec((1, eff, half), lambda i: (i // 2, i % 2, 0)),
+            pl.BlockSpec((1, eff, half), lambda i: (i // 2, 0, i % 2)),
+            row(width), row(key_width), row(key_width), row(width),
+        ),
+        out_shape=(
+            shape(owned, width, eff), shape(owned, width, eff), shape(owned, eff, width),
+            shape(width, width), shape(width, key_width), shape(width, key_width), shape(width, width),
+        ),
+        compiler_params=pltpu.CompilerParams(vmem_limit_bytes=48 * MIB),
+        name="unpack",
+    )(total, total, total, dense)
 
 
 def per_device(
@@ -1634,46 +1963,50 @@
     ag, fg = attn_gain[None, :], ffn_gain[None, :]
     router = jnp.pad(w_router, ((0, 0), (0, LANES - expert_total)))
 
-    h, q, kv_local, qraw, kraw = project(block_input, ag, w_query, w_key, w_value, qg, kg, cosine, sine)
-    kv = plane_gather(kv_local, fast, 1)
-    mixed, invl, after, xg, soft = attend(scalars, q, kv, block_input, w_out, fg, router, routes)
-    tokens = plane_gather(xg, fast, 2)
-    pick, xe, gate_part, up_part, hidden, part = experts_forward(scalars, tokens, w_gate, w_up, w_down)
-    output = after + plane_scatter(part, fast, 3)
-    difference = valid * (output - teacher.astype(F32))
-    loss_part = jnp.sum(difference * difference)
-    out_grad = difference * (positions_all / count_all)
-    grads = plane_gather(out_grad.astype(BF16), fast, 4)
-    dpart, weighted, gate_grad, up_grad = experts_backward(
-        scalars, grads, tokens, pick, gate_part, up_part, hidden, w_gate, w_up, w_down
-    )
     if fast:
-        eff = w_gate.shape[2]
-        owned = w_gate.shape[0]
+        scale = (positions_all / count_all)[None]
+        (
+            h, q, qraw, kraw, kv, mixed, invl, after, soft, tokens, pick, xe, gate_part, up_part, hidden,
+            block_output, out_grad, loss_row, grads,
+        ) = front(
+            slot_lengths, block_input, teacher, routes, w_query, w_key, w_value, w_out, w_gate, w_up, w_down,
+            ag, fg, qg, kg, cosine, sine, router, scale, group, 1,
+        )
+        dpart, weighted, gate_grad, up_grad = experts_backward(
+            scalars, grads, tokens, pick, gate_part, up_part, hidden, w_gate, w_up, w_down
+        )
         total, input_grad, dense, sums = tail(
             slot_lengths, dpart, xe, gate_grad, up_grad, hidden, weighted, q, kv, mixed, invl, soft, out_grad, after,
-            qraw, kraw, block_input, h, xg, w_out, w_query, w_key, w_value, fg, router, cosine, sine, ag, qg, kg,
-            jnp.broadcast_to(loss_part[None, None], (1, LANES)), expert_total, 5,
+            qraw, kraw, block_input, h, tokens, w_out, w_query, w_key, w_value, fg, router, cosine, sine, ag, qg, kg,
+            loss_row, expert_total, 2,
         )[:4]
-        total = total.reshape(owned, 6, eff, width // 2)
-        expert_grads = (
-            total[:, 0:2].reshape(owned, width, eff),
-            total[:, 2:4].reshape(owned, width, eff),
-            jnp.concatenate([total[:, 4], total[:, 5]], axis=2),
-        )
-        dense = [dense[:, k].reshape(width, width).astype(F32) for k in range(3)]
+        unpacked = unpack(total, dense, w_key.shape[1])
+        expert_grads, dense = unpacked[:3], unpacked[3:]
         tops = sums[expert_total : expert_total + 5]
         small = (
             tops[2, :HEAD] + tops[2, HEAD : 2 * HEAD], tops[3, :HEAD] + tops[3, HEAD : 2 * HEAD], tops[0], tops[1],
-            sums[:expert_total].T, tops[4, 0],
+            sums[:expert_total].T, jnp.sum(tops[4]),
         )
     else:
+        h, q, kv_local, qraw, kraw = project(block_input, ag, w_query, w_key, w_value, qg, kg, cosine, sine)
+        kv = plane_gather(kv_local)
+        mixed, invl, after, xg, soft = attend(scalars, q, kv, block_input, w_out, fg, router, routes)
+        tokens = plane_gather(xg)
+        pick, xe, gate_part, up_part, hidden, part = experts_forward(scalars, tokens, w_gate, w_up, w_down)
+        output = after + plane_scatter(part)
+        difference = valid * (output - teacher.astype(F32))
+        loss_part = jnp.sum(difference * difference)
+        out_grad = difference * (positions_all / count_all)
+        grads = plane_gather(out_grad.astype(BF16))
+        dpart, weighted, gate_grad, up_grad = experts_backward(
+            scalars, grads, tokens, pick, gate_part, up_part, hidden, w_gate, w_up, w_down
+        )
         expert_grads = lax.psum(expert_weights(xe, gate_grad, up_grad, hidden, weighted), "dp")
-        dx = plane_scatter(dpart, fast, 5)
+        dx = plane_scatter(dpart)
         dq, dkv_parts, after_grad, attn_grad, logit_grad, ffn_gain_grad = attend_backward(
             scalars, q, kv, mixed, invl, dx, soft, out_grad, after, fg, router, w_out
         )
-        dkv = plane_scatter(dkv_parts, fast, 6)
+        dkv = plane_scatter(dkv_parts)
         input_grad, dense, router_grad, query_gg, key_gg, attn_gg = finish(
             dq, dkv, qraw, kraw, block_input, after_grad, cosine, sine, ag, qg, kg,
             w_query, w_key, w_value, h, mixed, attn_grad, xg, logit_grad,
@@ -1687,17 +2020,13 @@
             ),
             ("dp", "context", "experts"),
         )
-    key_width = w_key.shape[1]
+        key_width = w_key.shape[1]
+        expert_grads = [grad.astype(F32) for grad in expert_grads]
+        dense = [dense[0], dense[1][:, :key_width], dense[1][:, key_width:], dense[2]]
+        block_output = output.astype(BF16)
     return (
-        small[5] / (count_all * width),
-        output.astype(BF16),
-        input_grad,
-        dense[0],
-        dense[1][:, :key_width],
-        dense[1][:, key_width:],
-        dense[2],
-        small[0], small[1], small[2], small[3], small[4],
-        expert_grads[0].astype(F32), expert_grads[1].astype(F32), expert_grads[2].astype(F32),
+        small[5] / (count_all * width), block_output, input_grad, dense[0], dense[1], dense[2], dense[3],
+        small[0], small[1], small[2], small[3], small[4], expert_grads[0], expert_grads[1], expert_grads[2],
     )
 
 

time: 749 us -> 654 us (0.87)
  Pallas kernels: 682 us -> 624 us
  other arithmetic: 31.6 us -> 7.66 us
  local copies, waits for them, and re-layouts: 20.9 us -> 7.93 us
    pallas_call x7 -> x2, Pallas kernels: 250 us -> 208 us  [the longest x1 188 us: front(): pl.pallas_call(front_kernel, in_specs=[smem, hbm, hbm, vmem] + [hbm] * 7...]
    convert_element_type x8 -> x1, other arithmetic: 23.4 us -> 0.01 us  [per_device(): turned = positions.astype(F32)[:, None] * inverse[None, :]]
    pallas_call x1, Pallas kernels: 386 us -> 369 us  [tail(): pl.pallas_call(tail_kernel, in_specs=[smem] + [hbm] * 22 + [vmem] * 8, ou...]
    slice x5 -> x0, local copies, waits for them, and re-layouts: 10.2 us -> none  [the longest x1 4 us: per_device(): total[:, 2:4].reshape(owned, width, eff)]
where the time goes in v3:
time: 654 us; the launch traced here: 643 us
  Pallas kernels  624 us (95%)
  local copies, waits for them, and re-layouts  7.93 us (1%)
  other arithmetic  7.66 us (1%)
    pallas_call x1, Pallas kernels, tail(): pl.pallas_call(tail_kernel, in_specs=[smem] + [hbm] * 22 + [vmem] * 8, ou...  369 us
    pallas_call x1, Pallas kernels, front(): pl.pallas_call(front_kernel, in_specs=[smem, hbm, hbm, vmem] + [hbm] * 7...  188 us
    pallas_call x1, Pallas kernels, experts_backward(): pl.pallas_call(experts_backward_kernel, grid_spec=pltpu.PrefetchScalarGri...  46.6 us
    pallas_call x1, Pallas kernels, unpack(): pl.pallas_call(unpack_kernel, grid=(steps,), in_specs=[piece(0), piece(1)...  20.6 us

profile of v3, /device:TPU:0, one launch (start us, length us, event | category | flops | bytes accessed | tf_op | source)
XLA Modules:
  0.0 643.4 jit_solution(4373724060483588802)
XLA Ops:
  0.7 1.3 reduce_sum.18
  2.6 0.7 dynamic_slice.3.sc_ref
  3.4 0.0 copy-start.2
  3.4 0.6 pad_add_fusion.sc_ref
  4.0 1.3 maximum_bitcast_fusion
  5.3 1.0 fusion
  6.3 1.6 copy.32.routes_ref
  7.8 1.0 copy.31
  8.8 0.8 pad.4.wr_ref
  9.6 0.0 copy-done.2
  9.6 187.8 %front.1 = (bf16[4,128,1024]{2,1,0:T(8,128)(2,1)}, bf16[4,128,1024]{2,1,0:T(8,128)(2,1)}, f32[4,128,1024]{2,1,0:T(8,128)}, f32[4,128,512]{2,1,0:T(8,128)}, bf16[...) custom-call(s32[4]{0:T(128)} %copy-done.2, ...), custom_call_target="tpu_custom_call" | custom-call | tf_op jit(solution)/shard_map/front/pallas_call | solution.py:1131
  197.4 46.6 %experts_backward.1 = (bf16[8,4,128,1152]{3,2,1,0:T(8,128)(2,1)}, bf16[4,4,320,1024]{3,2,1,0:T(8,128)(2,1)}, bf16[4,4,320,512]{3,2,1,0:T(8,128)(2,1)}, bf16[4,4,320,512]{3,2,1,0:T(8,128)(2,1)}) custom-call(s32[5]{0:T(128)} %pad_add_fusion.sc_ref, bf16[8,4,128,1024]{3,2,1,0:T(8,128)(2,1)} %get-tuple-element.49.dy_ref, ...), custom_call_target="tpu_custom_call" | custom-call | tf_op jit(solution)/shard_map/experts_backward/pallas_call | solution.py:429
  243.9 369.5 %tail.1 = (bf16[24,512,512]{2,1,0:T(8,128)(2,1)}, f32[4,128,1024]{2,1,0:T(8,128)}, bf16[8,3,128,1024]{3,2,1,0:T(8,128)(2,1)}, f32[40,1024]{1,0:T(8,128)}, bf16[2...) custom-call(s32[4]{0:T(128)} %copy-done.2, ...), custom_call_target="tpu_custom_call" | custom-call | tf_op jit(solution)/shard_map/tail/pallas_call | solution.py:1864
  613.4 1.4 add_bitcast_fusion
  614.8 2.1 fusion.5
  617.6 1.6 slice_bitcast_fusion
  619.1 0.0 copy-start.1
  619.1 0.0 copy-start
  619.1 20.6 %unpack.1 = (f32[4,1024,512]{2,1,0:T(8,128)}, f32[4,1024,512]{2,1,0:T(8,128)}, f32[4,512,1024]{2,1,0:T(8,128)}, f32[1024,1024]{1,0:T(8,128)}, f32[1024,512]{1,0:...) custom-call(bf16[24,512,512]{2,1,0:T(8,128)(2,1)} %get-tuple-element.74.gate_ref.up_ref.down_ref, ...), custom_call_target="tpu_custom_call" | custom-call | tf_op jit(solution)/shard_map/unpack/pallas_call | solution.py:1920
  639.7 0.0 copy-done.1
  639.7 1.0 copy.35
  640.7 0.0 copy-done
  640.7 1.3 copy.36
  (2 shorter events, 0.0 us)
Async XLA Ops:
  3.4 6.2 copy-start.2
  619.1 20.6 %copy-start.1 = (bf16[4,128,1024]{2,1,0:T(8,128)(2,1)S(1)}, bf16[4,128,1024]{2,1,0:T(8,128)(2,1)}, u32[]{:S(2)}) copy-start(bf16[4,128,1024]{2,1,0:T(8,128)(2,1)} %get-tuple-element.110) | copy-start | bytes 3145732
  619.1 21.6 %copy-start = (f32[4,128,1024]{2,1,0:T(8,128)S(1)}, f32[4,128,1024]{2,1,0:T(8,128)}, u32[]{:S(2)}) copy-start(f32[4,128,1024]{2,1,0:T(8,128)} %get-tuple-element.111) | copy-start | bytes 6291460

commit v4 on v3

--- a/solution.py
+++ b/solution.py
@@ -775,7 +775,7 @@
     sc_ref, x_in, teacher_in, routes_ref, wq_in, wk_in, wv_in, wo_in, wg_in, wu_in, wd_in,
     gain_ref, fg_ref, qg_ref, kg_ref, cos_ref, sin_ref, wr_ref, scale_ref,
     h_out, q_out, qraw_out, kraw_out, kv_out, mixed_out, invl_out, after_out, soft_out, tokens_out,
-    pick_out, xe_out, gp_out, up_out, hid_out, y_out, og_out, loss_out, grads_out,
+    pick_out, xe_out, gp_out, up_out, hid_out, y_out, og_out, loss_out, grads_out, dpart_out, dyw_out, gg_out, ug_out,
     sb, da, db, rx, ry, parts, wg, wu, wd, after_s, xg_s, dy_s,
     sent_kv, got_kv, loc_kv, sent_xg, got_xg, loc_xg, sent_dy, got_dy, loc_dy, sent_rs, got_rs, wsem, local,
 ):
@@ -831,8 +831,12 @@
                 at = 2 * tile * LANES
                 kvl[two, :, at : at + LANES] = turned.astype(BF16).reshape(2, rows, LANES)
                 kvl[two, :, at + LANES : at + 2 * LANES] = value[:, lanes].reshape(2, rows, LANES)
-            kv_gather.start(s)
-            kv_gather.start(s + 1)
+
+            @pl.when(s == 0)
+            def _():
+                kv_gather.start(0)
+                kv_gather.start(1)
+
             q_raw = dot(normed, wq[...])
             qraw_s[two] = q_raw.reshape(2, rows, qw)
             for tile in range(qw // LANES):
@@ -848,8 +852,10 @@
         for copy in keeps:
             copy.start()
         kv_gather.forward(0)
+        kv_gather.start(2)
         kv_gather.forward(1)
         kv_gather.settle(0)
+        kv_gather.start(3)
         loads[4].wait()
 
         def attend_slot(s):
@@ -955,151 +961,279 @@
     )
     sources, double, pairs, held = group, 2 * rows, group // 2, group // 2 * PAIR
 
-    def second_phase(tok, pick_s, xe_s, gp_s, up_s, hid_s, gates, ybuf, teach, y_s, og_s, sems, out_sems):
-        teacher_load = pltpu.make_async_copy(teacher_in, teach, sems.at[1])
+    eff = wg_in.shape[2]
+
+    def late_phases(teach, y_s, og_s, late_sems):
+        teacher_load = pltpu.make_async_copy(teacher_in, teach, late_sems.at[0])
         teacher_load.start()
-        for copy in expert_loads:
-            copy.wait()
-        teacher_load.wait()
         loss_out[...] = jnp.zeros_like(loss_out)
-        keeps = lambda s: [
-            pltpu.make_async_copy(source, there.at[s], out_sems.at[n])
-            for n, (source, there) in enumerate(
-                ((pick_s, pick_out), (xe_s, xe_out), (gp_s, gp_out), (up_s, up_out), (hid_s, hid_out))
-            )
+        outs = lambda s: [
+            pltpu.make_async_copy(source.at[lax.rem(s, 2)], there.at[s], late_sems.at[1 + 2 * n + lax.rem(s, 2)])
+            for n, (source, there) in enumerate(((y_s, y_out), (og_s, og_out)))
         ]
 
-        def experts_slot(s, between):
-            load = pltpu.make_async_copy(tokens_out.at[:, s], tok, sems.at[0])
-            load.start()
-
-            @pl.when(s >= 1)
-            def _():
-                for copy in keeps(s - 1):
+        def loss_slot(s):
+            slot = lax.rem(s, 2)
+
+            def wait():
+                for copy in outs(s - 2):
                     copy.wait()
 
-            load.wait()
-            slab = tok[:, :, width:].reshape(sources * rows, LANES)
-            chosen = (lane_of((8, LANES)) == row_of((8, LANES)) + first).astype(BF16)
-            routed = dot_nt(chosen, slab) > 0.0
-            before, after = row_of((double, double)), lane_of((double, double))
-            count = ((before < after) & (before // rows == after // rows)).astype(BF16)
-            place = lax.broadcasted_iota(jnp.int32, (PAIR, double), 0)
-            offset = (lane_of((8, double)) // rows) * MOST
-            for p in range(pairs):
-                mask = routed[:, p * double : (p + 1) * double]
-                rank = dot(mask.astype(F32).astype(BF16), count).astype(jnp.int32) + offset
-                rank = jnp.where(mask, rank, -1)
-                pick = jnp.concatenate(
-                    [(place == rank[e : e + 1, :]).astype(F32).astype(BF16) for e in range(owned)], axis=0
-                )
-                pick_s[p] = pick
-                picked = dot(pick, tok[2 * p : 2 * p + 2, :, :width].reshape(double, width)).astype(BF16)
-                scale = row_gates(dot(pick, slab[p * double : (p + 1) * double]), first, owned)
-                for e in range(owned):
-                    xe_s[e, p * PAIR : (p + 1) * PAIR] = picked[e * PAIR : (e + 1) * PAIR]
-                    gates[e, p * PAIR : (p + 1) * PAIR] = jnp.broadcast_to(
-                        scale[e * PAIR : (e + 1) * PAIR], (PAIR, LANES)
-                    )
-
-            def one_expert(e, carry):
-                rows_in = xe_s[e]
-                gate_part = dot(rows_in, wg[e])
-                up_part = dot(rows_in, wu[e])
-                gp_s[e] = gate_part
-                up_s[e] = up_part
-                hidden = (gate_part * jax.nn.sigmoid(gate_part) * up_part).astype(BF16)
-                hid_s[e] = hidden
-                result = (dot(hidden, wd[e]) * gates[e][:, 0:1]).astype(BF16)
-                for p in range(pairs):
-                    ybuf[p, e] = result[p * PAIR : (p + 1) * PAIR]
-                return carry
-
-            lax.fori_loop(0, owned // 2, one_expert, 0)
-            between()
-            lax.fori_loop(owned // 2, owned, one_expert, 0)
-            for p in range(pairs):
-                back = dot_tn(pick_s[p], ybuf[p].reshape(owned * PAIR, width))
-                parts[2 * p : 2 * p + 2, s] = back.astype(BF16).reshape(2, rows, width)
-            for copy in keeps(s):
-                copy.start()
-
-        def loss_slot(s):
+            if isinstance(s, int):
+                if s >= 2:
+                    wait()
+            else:
+                pl.when(s >= 2)(wait)
             output = after_s[s] + scatter.result(s)
-            y_s[s] = output.astype(BF16)
+            y_s[slot] = output.astype(BF16)
             valid = (row_of((rows, 1)) + here * rows < sc_ref[s]).astype(F32)
             difference = valid * (output - teach[s].astype(F32))
-            square = jnp.sum(difference * difference, axis=0, keepdims=True)
-            loss_out[...] += square
+            loss_out[...] += jnp.sum(difference * difference, axis=0, keepdims=True)
             grad = difference * scale_ref[0]
-            og_s[s] = grad
+            og_s[slot] = grad
             dy_s[s] = grad.astype(BF16)
+            for copy in outs(s):
+                copy.start()
             grad_gather.start(s)
 
-        def one(t):
-            row_gather.arrive(t)
-
-            def between():
-                @pl.when(t == 0)
+        teacher_load.wait()
+
+        def second_phase(tok, pick_s, xe_s, gp_s, up_s, hid_s, gates, ybuf, sems, out_sems):
+            for copy in expert_loads:
+                copy.wait()
+            keeps = lambda s: [
+                pltpu.make_async_copy(source, there.at[s], out_sems.at[n])
+                for n, (source, there) in enumerate(
+                    ((pick_s, pick_out), (xe_s, xe_out), (gp_s, gp_out), (up_s, up_out), (hid_s, hid_out))
+                )
+            ]
+
+            def experts_slot(s, between):
+                load = pltpu.make_async_copy(tokens_out.at[:, s], tok, sems.at[0])
+                load.start()
+
+                @pl.when(s >= 1)
                 def _():
-                    row_gather.settle(slots - 2)
-                    row_gather.forward(slots - 1)
-
-                @pl.when(t == 1)
-                def _():
-                    row_gather.settle(slots - 1)
+                    for copy in keeps(s - 1):
+                        copy.wait()
+
+                load.wait()
+                slab = tok[:, :, width:].reshape(sources * rows, LANES)
+                chosen = (lane_of((8, LANES)) == row_of((8, LANES)) + first).astype(BF16)
+                routed = dot_nt(chosen, slab) > 0.0
+                before, after = row_of((double, double)), lane_of((double, double))
+                count = ((before < after) & (before // rows == after // rows)).astype(BF16)
+                place = lax.broadcasted_iota(jnp.int32, (PAIR, double), 0)
+                offset = (lane_of((8, double)) // rows) * MOST
+                for p in range(pairs):
+                    mask = routed[:, p * double : (p + 1) * double]
+                    rank = dot(mask.astype(F32).astype(BF16), count).astype(jnp.int32) + offset
+                    rank = jnp.where(mask, rank, -1)
+                    pick = jnp.concatenate(
+                        [(place == rank[e : e + 1, :]).astype(F32).astype(BF16) for e in range(owned)], axis=0
+                    )
+                    pick_s[p] = pick
+                    picked = dot(pick, tok[2 * p : 2 * p + 2, :, :width].reshape(double, width)).astype(BF16)
+                    scale = row_gates(dot(pick, slab[p * double : (p + 1) * double]), first, owned)
+                    for e in range(owned):
+                        xe_s[e, p * PAIR : (p + 1) * PAIR] = picked[e * PAIR : (e + 1) * PAIR]
+                        gates[e, p * PAIR : (p + 1) * PAIR] = jnp.broadcast_to(
+                            scale[e * PAIR : (e + 1) * PAIR], (PAIR, LANES)
+                        )
+
+                def one_expert(e, carry):
+                    rows_in = xe_s[e]
+                    gate_part = dot(rows_in, wg[e])
+                    up_part = dot(rows_in, wu[e])
+                    gp_s[e] = gate_part.astype(BF16)
+                    up_s[e] = up_part.astype(BF16)
+                    hidden = (gate_part * jax.nn.sigmoid(gate_part) * up_part).astype(BF16)
+                    hid_s[e] = hidden
+                    result = (dot(hidden, wd[e]) * gates[e][:, 0:1]).astype(BF16)
+                    for p in range(pairs):
+                        ybuf[p, e] = result[p * PAIR : (p + 1) * PAIR]
+                    return carry
+
+                for e in range(owned // 2):
+                    one_expert(e, 0)
+                between()
+                for e in range(owned // 2, owned):
+                    one_expert(e, 0)
+                for p in range(pairs):
+                    back = dot_tn(pick_s[p], ybuf[p].reshape(owned * PAIR, width))
+                    parts[2 * p : 2 * p + 2, s] = back.astype(BF16).reshape(2, rows, width)
+                for copy in keeps(s):
+                    copy.start()
+
+            def one(t):
+                row_gather.arrive(t)
+
+                def between():
+                    @pl.when(t == 0)
+                    def _():
+                        row_gather.settle(slots - 2)
+                        row_gather.forward(slots - 1)
+
+                    @pl.when(t == 1)
+                    def _():
+                        row_gather.settle(slots - 1)
+
+                    @pl.when(t >= 1)
+                    def _():
+                        scatter.first(t - 1)
+                        scatter.second(t - 1)
+
+                    @pl.when(t == slots - 1)
+                    def _():
+                        grad_gather.forward(0)
+
+                experts_slot(t, between)
+                scatter.start(t)
 
                 @pl.when(t >= 1)
                 def _():
-                    scatter.first(t - 1)
-                    scatter.second(t - 1)
-
-                @pl.when(t == slots - 1)
+                    scatter.third(t - 1)
+
+                @pl.when(t >= 2)
                 def _():
-                    grad_gather.forward(0)
-
-            experts_slot(t, between)
-            scatter.start(t)
-
-            @pl.when(t >= 1)
-            def _():
-                scatter.third(t - 1)
-
-            @pl.when(t >= 2)
-            def _():
-                loss_slot(t - 2)
-
-        each(one)
-        last = slots - 1
-        scatter.first(last)
-        scatter.second(last)
-        loss_slot(last - 1)
-        grad_gather.settle(0)
-        grad_gather.forward(1)
-        scatter.third(last)
-        grad_gather.settle(1)
-        loss_slot(last)
-        outs = [
-            pltpu.make_async_copy(source, there, sems.at[n]) for n, (source, there) in enumerate(((y_s, y_out), (og_s, og_out)))
-        ]
-        for copy in outs:
-            copy.start()
-        for s in range(2, slots):
-            grad_gather.forward(s)
-            grad_gather.settle(s)
-        each(grad_gather.arrive)
-        each(grad_gather.drain)
-        each(row_gather.drain)
-        each(scatter.drain)
-        for copy in keeps(last) + outs:
-            copy.wait()
-
-    eff = wg_in.shape[2]
+                    loss_slot(t - 2)
+
+            each(one)
+            each(row_gather.drain)
+            for copy in keeps(slots - 1):
+                copy.wait()
+
+        pl.run_scoped(
+            second_phase,
+            V((group, rows, wide), BF16), V((pairs, owned * PAIR, double), BF16), V((owned, held, width), BF16),
+            V((owned, held, eff), BF16), V((owned, held, eff), BF16), V((owned, held, eff), BF16), V((owned, held, LANES), F32),
+            V((pairs, owned, PAIR, width), BF16), D((2,)), D((5,)),
+        )
+
+        def third_phase(dyb, slabb, pickb, gpb, upb, hidb, gates, dye, dxb, dp_s, dyw_s, gg_s, ug_s, sems, out_sems):
+            saved = lambda s: [
+                pltpu.make_async_copy(source, there, sems.at[n])
+                for n, (source, there) in enumerate(
+                    ((tokens_out.at[:, s, :, pl.ds(width, LANES)], slabb), (pick_out.at[s], pickb), (gp_out.at[s], gpb),
+                     (up_out.at[s], upb), (hid_out.at[s], hidb))
+                )
+            ]
+            keeps = lambda s: [
+                pltpu.make_async_copy(source, there, out_sems.at[n])
+                for n, (source, there) in enumerate(
+                    ((dp_s, dpart_out.at[:, s]), (dyw_s, dyw_out.at[s]), (gg_s, gg_out.at[s]), (ug_s, ug_out.at[s]))
+                )
+            ]
+            for copy in saved(0):
+                copy.start()
+            last = slots - 1
+            scatter.first(last)
+            scatter.second(last)
+            loss_slot(last - 1)
+            grad_gather.settle(0)
+            grad_gather.forward(1)
+
+            def one(s):
+                grad_gather.arrive(s)
+                load = pltpu.make_async_copy(grads_out.at[:, s], dyb, sems.at[5])
+                load.start()
+
+                @pl.when(s >= 1)
+                def _():
+                    for copy in keeps(s - 1):
+                        copy.wait()
+
+                for copy in saved(s):
+                    copy.wait()
+                load.wait()
+                for p in range(pairs):
+                    pick = pickb[p]
+                    picked = dot(pick, dyb[2 * p : 2 * p + 2].reshape(double, width)).astype(BF16)
+                    scale = row_gates(dot(pick, slabb[2 * p : 2 * p + 2].reshape(double, LANES)), first, owned)
+                    for e in range(owned):
+                        dye[e, p * PAIR : (p + 1) * PAIR] = picked[e * PAIR : (e + 1) * PAIR]
+                        gates[e, p * PAIR : (p + 1) * PAIR] = jnp.broadcast_to(
+                            scale[e * PAIR : (e + 1) * PAIR], (PAIR, LANES)
+                        )
+
+                def one_expert(e, carry):
+                    grad_rows = dye[e]
+                    scale = gates[e][:, 0:1]
+                    plain = dot_nt(grad_rows, wd[e])
+                    gate_part, up_part = gpb[e].astype(F32), upb[e].astype(F32)
+                    soft_grad = jnp.sum(plain * hidb[e].astype(F32), axis=-1, keepdims=True)
+                    hidden_grad = plain * scale
+                    sigma = jax.nn.sigmoid(gate_part)
+                    gate_grad = (hidden_grad * up_part * sigma * (1.0 + gate_part * (1.0 - sigma))).astype(BF16)
+                    up_grad = (hidden_grad * gate_part * sigma).astype(BF16)
+                    gg_s[e] = gate_grad
+                    ug_s[e] = up_grad
+                    dyw_s[e] = (grad_rows.astype(F32) * scale).astype(BF16)
+                    input_grad = (dot_nt(gate_grad, wg[e]) + dot_nt(up_grad, wu[e])).astype(BF16)
+                    lanes = lane_of((held, LANES))
+                    high = soft_grad.astype(BF16).astype(F32)
+                    spot = jnp.where(
+                        lanes == first + e, high, jnp.where(lanes == first + e + LANES // 2, soft_grad - high, 0.0)
+                    ).astype(BF16)
+                    for p in range(pairs):
+                        dxb[p, e, :, :width] = input_grad[p * PAIR : (p + 1) * PAIR]
+                        dxb[p, e, :, width:] = spot[p * PAIR : (p + 1) * PAIR]
+                    return carry
+
+                for e in range(owned // 2):
+                    one_expert(e, 0)
+
+                @pl.when(s == 0)
+                def _():
+                    scatter.third(last)
+                    grad_gather.settle(1)
+                    grad_gather.forward(2)
+
+                @pl.when(s == 1)
+                def _():
+                    grad_gather.settle(2)
+                    grad_gather.forward(3)
+
+                @pl.when(s == 2)
+                def _():
+                    grad_gather.settle(3)
+
+                for e in range(owned // 2, owned):
+                    one_expert(e, 0)
+                for p in range(pairs):
+                    back = dot_tn(pickb[p], dxb[p].reshape(owned * PAIR, wide))
+                    dp_s[2 * p : 2 * p + 2] = back.astype(BF16).reshape(2, rows, wide)
+                for copy in keeps(s):
+                    copy.start()
+
+                @pl.when(s + 1 < slots)
+                def _():
+                    for copy in saved(s + 1):
+                        copy.start()
+
+                @pl.when(s == 0)
+                def _():
+                    loss_slot(last)
+
+            each(one)
+            each(scatter.drain)
+            each(grad_gather.drain)
+            for copy in keeps(slots - 1):
+                copy.wait()
+
+        pl.run_scoped(
+            third_phase,
+            V((group, rows, width), BF16), V((group, rows, LANES), BF16), V((pairs, owned * PAIR, double), BF16),
+            V((owned, held, eff), BF16), V((owned, held, eff), BF16), V((owned, held, eff), BF16), V((owned, held, LANES), F32),
+            V((owned, held, width), BF16), V((pairs, owned, PAIR, wide), BF16), V((group, rows, wide), BF16),
+            V((owned, held, width), BF16), V((owned, held, eff), BF16), V((owned, held, eff), BF16), D((6,)), D((4,)),
+        )
+        for s in range(slots - 2, slots):
+            for copy in outs(s):
+                copy.wait()
+
     pl.run_scoped(
-        second_phase,
-        V((group, rows, wide), BF16), V((pairs, owned * PAIR, double), BF16), V((owned, held, width), BF16),
-        V((owned, held, eff), F32), V((owned, held, eff), F32), V((owned, held, eff), BF16), V((owned, held, LANES), F32),
-        V((pairs, owned, PAIR, width), BF16), full(width, BF16), full(width, BF16), full(width, F32), D((2,)), D((5,)),
+        late_phases, full(width, BF16), V((2, rows, width), BF16), V((2, rows, width), F32), D((5,)),
     )
 
 
@@ -1125,13 +1259,13 @@
         mine(width, BF16), mine(qw, BF16), mine(qw, F32), mine(kw, F32), all_of(2 * kw), mine(qw, BF16), mine(qw, F32),
         mine(width, F32), mine(LANES, F32), all_of(wide),
         saved(pairs, owned * PAIR, 2 * rows), saved(owned, held, width),
-        jax.ShapeDtypeStruct((slots, owned, held, eff), F32), jax.ShapeDtypeStruct((slots, owned, held, eff), F32),
-        saved(owned, held, eff), mine(width, BF16), mine(width, F32), jax.ShapeDtypeStruct((1, width), F32), all_of(width),
+        saved(owned, held, eff), saved(owned, held, eff), saved(owned, held, eff), mine(width, BF16), mine(width, F32), jax.ShapeDtypeStruct((1, width), F32), all_of(width),
+        all_of(wide), saved(owned, held, width), saved(owned, held, eff), saved(owned, held, eff),
     )
     return pl.pallas_call(
         front_kernel,
         in_specs=[smem, hbm, hbm, vmem] + [hbm] * 7 + [vmem] * 7 + [smem],
-        out_specs=(hbm,) * 17 + (vmem, hbm),
+        out_specs=(hbm,) * 17 + (vmem,) + (hbm,) * 5,
         out_shape=outs,
         scratch_shapes=[
             V((4, slots, rows, width), BF16), V((slots, half, width), BF16), V((slots, half, width), BF16),
@@ -1594,7 +1728,12 @@
 
             def slot_and_move(s):
                 one_slot(s)
-                line.move(s + 3)
+                ahead = s + 3 + s // 2
+                line.move(ahead)
+
+                @pl.when(lax.rem(s, 2) == 1)
+                def _():
+                    line.move(ahead + 1)
 
             each(slot_and_move)
 
@@ -1625,7 +1764,7 @@
             scat_kv.first(slots - 1)
             scat_kv.second(slots - 1)
             scat_kv.third(slots - 2)
-            line.move(slots + 3)
+            line.move(9)
             flat = lambda ref: ref[...].reshape(slots * rows, ref.shape[2])
             for copy in loads:
                 copy.wait()
@@ -1650,8 +1789,8 @@
 
             product(mixed_s, at_s, aside(0))
             scat_kv.third(slots - 1)
-            line.move(slots + 4)
             product(hb, q_s, aside(2))
+            line.move(10)
             router = dot_tn(flat(lg_s), flat(n2b))
             experts = small_out.shape[0] - 8
             sm_mine[0] = jnp.zeros(sm_mine.shape[1:], F32)
@@ -1659,7 +1798,6 @@
             sm_mine[0, experts + 1 : experts + 2] = fgg[...]
             sm_mine[0, experts + 2 : experts + 3, :LANES] = qgg[...]
             sm_mine[0, experts + 4 : experts + 5] = loss_ref[...]
-            line.move(slots + 5)
 
             def one_slot(s):
                 grads = scat_kv.result(s)
@@ -1679,7 +1817,7 @@
 
             each(one_slot)
             each(scat_kv.drain)
-            line.move(slots + 6)
+            line.move(11)
             sm_mine[0, experts : experts + 1] = agg[...]
             sm_mine[0, experts + 3 : experts + 4, :LANES] = kgg[...]
             for shard in range(shards):
@@ -1694,7 +1832,7 @@
 
             product(hb, k_s, beside(0))
             product(hb, v_s, beside(kw))
-            line.move(slots + 7)
+            line.move(12)
 
         pl.run_scoped(
             last_phase,
@@ -1731,14 +1869,13 @@
         small(2, plane.yn).start()
         by_kind(scat_de.third)
         small_step(2, plane.yn)
-        line.move(slots + 8)
+        line.move(13)
 
         def one_kind(s):
             dsh[s] = scat_de.result(s).astype(BF16)
 
         by_kind(one_kind)
         by_kind(scat_de.drain)
-        line.move(slots + 9)
         each(lambda s: pltpu.make_async_copy(ag_s.at[s], ig_out.at[s], local.at[0]).wait())
 
     pl.run_scoped(
@@ -1967,13 +2104,10 @@
         scale = (positions_all / count_all)[None]
         (
             h, q, qraw, kraw, kv, mixed, invl, after, soft, tokens, pick, xe, gate_part, up_part, hidden,
-            block_output, out_grad, loss_row, grads,
+            block_output, out_grad, loss_row, unused_grads, dpart, weighted, gate_grad, up_grad,
         ) = front(
             slot_lengths, block_input, teacher, routes, w_query, w_key, w_value, w_out, w_gate, w_up, w_down,
             ag, fg, qg, kg, cosine, sine, router, scale, group, 1,
-        )
-        dpart, weighted, gate_grad, up_grad = experts_backward(
-            scalars, grads, tokens, pick, gate_part, up_part, hidden, w_gate, w_up, w_down
         )
         total, input_grad, dense, sums = tail(
             slot_lengths, dpart, xe, gate_grad, up_grad, hidden, weighted, q, kv, mixed, invl, soft, out_grad, after,

time: 654 us -> 614 us (0.939)
  Pallas kernels: 624 us -> 584 us
    pallas_call x1 -> x0, Pallas kernels: 46.6 us -> none  [experts_backward(): pl.pallas_call(experts_backward_kernel, grid_spec=pltpu.PrefetchScalarGri...]
    pallas_call x1, Pallas kernels: 188 us -> 205 us  [front(): pl.pallas_call(front_kernel, in_specs=[smem, hbm, hbm, vmem] + [hbm] * 7...]
    pallas_call x1, Pallas kernels: 369 us -> 359 us  [tail(): pl.pallas_call(tail_kernel, in_specs=[smem] + [hbm] * 22 + [vmem] * 8, ou...]
where the time goes in v4:
time: 614 us; the launch traced here: 603 us
  Pallas kernels  584 us (95%)
  local copies, waits for them, and re-layouts  8.43 us (1%)
  other arithmetic  7.08 us (1%)
    pallas_call x1, Pallas kernels, tail(): pl.pallas_call(tail_kernel, in_specs=[smem] + [hbm] * 22 + [vmem] * 8, ou...  359 us
    pallas_call x1, Pallas kernels, front(): pl.pallas_call(front_kernel, in_specs=[smem, hbm, hbm, vmem] + [hbm] * 7...  205 us
    pallas_call x1, Pallas kernels, unpack(): pl.pallas_call(unpack_kernel, grid=(steps,), in_specs=[piece(0), piece(1)...  20.6 us

profile of v4, /device:TPU:0, one launch (start us, length us, event | category | flops | bytes accessed | tf_op | source)
XLA Modules:
  0.0 603.0 jit_solution(9307230897621175300)
XLA Ops:
  0.7 1.3 reduce_sum.18
  2.6 1.2 dynamic_slice.3.sc_ref
  3.9 1.3 maximum_bitcast_fusion
  5.2 1.0 fusion
  6.2 1.6 copy.32.routes_ref
  7.7 1.0 copy.31
  8.8 0.8 pad.4.wr_ref
  9.5 204.8 %front.1 = (bf16[4,128,1024]{2,1,0:T(8,128)(2,1)}, bf16[4,128,1024]{2,1,0:T(8,128)(2,1)}, f32[4,128,1024]{2,1,0:T(8,128)}, f32[4,128,512]{2,1,0:T(8,128)}, bf16[...) custom-call(s32[4]{0:T(128)} %dynamic_slice.3.sc_ref, ...), custom_call_target="tpu_custom_call" | custom-call | tf_op jit(solution)/shard_map/front/pallas_call | solution.py:1265
  214.3 358.7 %tail.1 = (bf16[24,512,512]{2,1,0:T(8,128)(2,1)}, f32[4,128,1024]{2,1,0:T(8,128)}, bf16[8,3,128,1024]{3,2,1,0:T(8,128)(2,1)}, f32[40,1024]{1,0:T(8,128)}, bf16[2...) custom-call(s32[4]{0:T(128)} %dynamic_slice.3.sc_ref, ...), custom_call_target="tpu_custom_call" | custom-call | tf_op jit(solution)/shard_map/tail/pallas_call | solution.py:2001
  573.0 1.4 add_bitcast_fusion
  574.4 2.1 fusion.5
  577.1 1.6 slice_bitcast_fusion
  578.7 0.0 copy-start.1
  578.7 0.0 copy-start
  578.7 20.6 %unpack.1 = (f32[4,1024,512]{2,1,0:T(8,128)}, f32[4,1024,512]{2,1,0:T(8,128)}, f32[4,512,1024]{2,1,0:T(8,128)}, f32[1024,1024]{1,0:T(8,128)}, f32[1024,512]{1,0:...) custom-call(bf16[24,512,512]{2,1,0:T(8,128)(2,1)} %get-tuple-element.66.gate_ref.up_ref.down_ref, ...), custom_call_target="tpu_custom_call" | custom-call | tf_op jit(solution)/shard_map/unpack/pallas_call | solution.py:2057
  599.3 0.0 copy-done.1
  599.3 1.0 copy.35
  600.3 0.0 copy-done
  600.3 1.3 copy.36
  (2 shorter events, 0.0 us)
Async XLA Ops:
  578.7 20.6 %copy-start.1 = (bf16[4,128,1024]{2,1,0:T(8,128)(2,1)S(1)}, bf16[4,128,1024]{2,1,0:T(8,128)(2,1)}, u32[]{:S(2)}) copy-start(bf16[4,128,1024]{2,1,0:T(8,128)(2,1)} %get-tuple-element.102) | copy-start | bytes 3145732
  578.7 21.6 %copy-start = (f32[4,128,1024]{2,1,0:T(8,128)S(1)}, f32[4,128,1024]{2,1,0:T(8,128)}, u32[]{:S(2)}) copy-start(f32[4,128,1024]{2,1,0:T(8,128)} %get-tuple-element.103) | copy-start | bytes 6291460

commit v5 on v4

--- a/solution.py
+++ b/solution.py
@@ -718,6 +718,10 @@
     return pltpu.make_async_remote_copy(src_ref=src, dst_ref=dst, send_sem=ss, recv_sem=rs, device_id=dev, device_id_type=MESH)
 
 
+def padded_rows(rows):
+    return jnp.concatenate([rows, jnp.zeros((LANES - rows.shape[0], rows.shape[1]), rows.dtype)], axis=0)
+
+
 class Slots:
     def __init__(self, plane, mine, out, sent, got, local):
         self.plane, self.mine, self.out, self.sent, self.got, self.local = plane, mine, out, sent, got, local
@@ -902,12 +906,13 @@
             unit, unused = rms_parts(after)
             normed = (unit * fg_ref[...]).astype(BF16)
             xg_s[s, :, :width] = normed
-            logits = dot(normed, wr_ref[...])
+            logits = dot_nt(normed, padded_rows(wr_ref[...]))
             lanes = lane_of(logits.shape)
-            routes = routes_ref[s]
-            chosen = lanes == routes[:, 0:1]
+            routes = routes_ref[s].astype(F32).T
+            number = lanes.astype(F32)
+            chosen = number == routes[:, 0:1]
             for k in range(1, routes.shape[1]):
-                chosen = chosen | (lanes == routes[:, k : k + 1])
+                chosen = chosen | (number == routes[:, k : k + 1])
             top = jnp.max(jnp.where(chosen, logits, -1e30), axis=-1, keepdims=True)
             weight = jnp.where(chosen, jnp.exp(jnp.minimum(logits - top, 0.0)), 0.0)
             soft = weight / jnp.sum(weight, axis=-1, keepdims=True)
@@ -1647,7 +1652,7 @@
                 chosen = soft * (soft_grad - jnp.sum(soft * soft_grad, axis=-1, keepdims=True))
                 logit_grad = chosen.astype(BF16)
                 lg_s[s] = logit_grad
-                normed_grad = dx[:, :width] + dot_nt(logit_grad, wr_ref[...])
+                normed_grad = dx[:, :width] + dot(logit_grad, padded_rows(wr_ref[...]))
                 back, gain_grad = rms_backward(normed_grad, afterb[slot], fg_ref[...])
                 fgg[...] += gain_grad
                 after_grad = ogb[slot] + back
@@ -2035,7 +2040,22 @@
     return lax.psum_scatter(parts, ("context", "experts"), scatter_dimension=0, tiled=False).astype(F32)
 
 
-def unpack_kernel(gate_ref, up_ref, down_ref, dense_ref, dg_ref, du_ref, dd_ref, dq_ref, dk_ref, dv_ref, do_ref):
+def unpack_kernel(
+    gate_ref, up_ref, down_ref, dense_ref, sums_ref, scale_ref, dg_ref, du_ref, dd_ref, dq_ref, dk_ref, dv_ref, do_ref,
+    router_ref, attn_ref, ffn_ref, query_ref, key_ref, loss_ref,
+):
+    @pl.when(pl.program_id(0) == 0)
+    def _():
+        experts = router_ref.shape[0]
+        line = lambda n: sums_ref[experts + n : experts + n + 1, :]
+        router_ref[...] = sums_ref[:experts, :]
+        attn_ref[...] = line(0)
+        ffn_ref[...] = line(1)
+        for ref, n in ((query_ref, 2), (key_ref, 3)):
+            tile = line(n)[:, :LANES]
+            ref[...] = (tile + pltpu.roll(tile, HEAD, 1))[:, :HEAD]
+        loss_ref[...] = jnp.sum(line(4), axis=-1, keepdims=True) * scale_ref[0]
+
     dg_ref[0] = gate_ref[0].astype(F32)
     du_ref[0] = up_ref[0].astype(F32)
     dd_ref[0] = down_ref[0].astype(F32)
@@ -2046,7 +2066,7 @@
     do_ref[...] = dense_ref[0, 2].astype(F32)
 
 
-def unpack(total, dense, key_width):
+def unpack(total, dense, sums, scale, key_width):
     chunks, eff, half = total.shape
     shards, kinds, shard_rows, width = dense.shape
     owned = chunks // 6
@@ -2054,23 +2074,29 @@
     piece = lambda kind: pl.BlockSpec((1, eff, half), lambda i: (i // 2 * 6 + 2 * kind + i % 2, 0, 0))
     row = lambda lanes: pl.BlockSpec((shard_rows * shards // steps, lanes), lambda i: (i, 0))
     shape = lambda *dims: jax.ShapeDtypeStruct(dims, F32)
+    still = lambda *dims: pl.BlockSpec(dims, lambda i: (0, 0))
+    experts = sums.shape[0] - 8
     return pl.pallas_call(
         unpack_kernel,
         grid=(steps,),
-        in_specs=[piece(0), piece(1), piece(2), pl.BlockSpec((1, kinds, shard_rows, width), lambda i: (i, 0, 0, 0))],
+        in_specs=[piece(0), piece(1), piece(2), pl.BlockSpec((1, kinds, shard_rows, width), lambda i: (i, 0, 0, 0)),
+            pl.BlockSpec(sums.shape, lambda i: (0, 0)), pl.BlockSpec(memory_space=pltpu.SMEM),
+        ],
         out_specs=(
             pl.BlockSpec((1, eff, half), lambda i: (i // 2, i % 2, 0)),
             pl.BlockSpec((1, eff, half), lambda i: (i // 2, i % 2, 0)),
             pl.BlockSpec((1, eff, half), lambda i: (i // 2, 0, i % 2)),
             row(width), row(key_width), row(key_width), row(width),
+            still(experts, width), still(1, width), still(1, width), still(1, HEAD), still(1, HEAD), still(1, 1),
         ),
         out_shape=(
             shape(owned, width, eff), shape(owned, width, eff), shape(owned, eff, width),
             shape(width, width), shape(width, key_width), shape(width, key_width), shape(width, width),
+            shape(experts, width), shape(1, width), shape(1, width), shape(1, HEAD), shape(1, HEAD), shape(1, 1),
         ),
         compiler_params=pltpu.CompilerParams(vmem_limit_bytes=48 * MIB),
         name="unpack",
-    )(total, total, total, dense)
+    )(total, total, total, dense, sums, scale)
 
 
 def per_device(
@@ -2106,21 +2132,18 @@
             h, q, qraw, kraw, kv, mixed, invl, after, soft, tokens, pick, xe, gate_part, up_part, hidden,
             block_output, out_grad, loss_row, unused_grads, dpart, weighted, gate_grad, up_grad,
         ) = front(
-            slot_lengths, block_input, teacher, routes, w_query, w_key, w_value, w_out, w_gate, w_up, w_down,
-            ag, fg, qg, kg, cosine, sine, router, scale, group, 1,
+            slot_lengths, block_input, teacher, jnp.swapaxes(routes, 1, 2), w_query, w_key, w_value, w_out,
+            w_gate, w_up, w_down, ag, fg, qg, kg, cosine, sine, w_router.T, scale, group, 1,
         )
         total, input_grad, dense, sums = tail(
             slot_lengths, dpart, xe, gate_grad, up_grad, hidden, weighted, q, kv, mixed, invl, soft, out_grad, after,
-            qraw, kraw, block_input, h, tokens, w_out, w_query, w_key, w_value, fg, router, cosine, sine, ag, qg, kg,
+            qraw, kraw, block_input, h, tokens, w_out, w_query, w_key, w_value, fg, w_router.T, cosine, sine, ag, qg, kg,
             loss_row, expert_total, 2,
         )[:4]
-        unpacked = unpack(total, dense, w_key.shape[1])
-        expert_grads, dense = unpacked[:3], unpacked[3:]
-        tops = sums[expert_total : expert_total + 5]
-        small = (
-            tops[2, :HEAD] + tops[2, HEAD : 2 * HEAD], tops[3, :HEAD] + tops[3, HEAD : 2 * HEAD], tops[0], tops[1],
-            sums[:expert_total].T, jnp.sum(tops[4]),
-        )
+        unpacked = unpack(total, dense, sums, (1.0 / (count_all * width))[None], w_key.shape[1])
+        expert_grads, dense = unpacked[:3], unpacked[3:7]
+        router_grad, attn_gg, ffn_gg, query_gg, key_gg, loss = unpacked[7:]
+        small = (query_gg[0], key_gg[0], attn_gg[0], ffn_gg[0], router_grad.T, loss[0, 0])
     else:
         h, q, kv_local, qraw, kraw = project(block_input, ag, w_query, w_key, w_value, qg, kg, cosine, sine)
         kv = plane_gather(kv_local)
@@ -2158,8 +2181,9 @@
         expert_grads = [grad.astype(F32) for grad in expert_grads]
         dense = [dense[0], dense[1][:, :key_width], dense[1][:, key_width:], dense[2]]
         block_output = output.astype(BF16)
+        small = small[:5] + (small[5] / (count_all * width),)
     return (
-        small[5] / (count_all * width), block_output, input_grad, dense[0], dense[1], dense[2], dense[3],
+        small[5], block_output, input_grad, dense[0], dense[1], dense[2], dense[3],
         small[0], small[1], small[2], small[3], small[4], expert_grads[0], expert_grads[1], expert_grads[2],
     )
 

time: 614 us -> 605 us (0.985)
  no operation moved by 1% of the time
where the time goes in v5:
time: 605 us; the launch traced here: 595 us
  Pallas kernels  585 us (97%)
    pallas_call x1, Pallas kernels, tail(): pl.pallas_call(tail_kernel, in_specs=[smem] + [hbm] * 22 + [vmem] * 8, ou...  359 us
    pallas_call x1, Pallas kernels, front(): pl.pallas_call(front_kernel, in_specs=[smem, hbm, hbm, vmem] + [hbm] * 7...  205 us
    pallas_call x1, Pallas kernels, unpack(): pl.pallas_call(unpack_kernel, grid=(steps,), in_specs=[piece(0), piece(1)...  20.8 us

profile of v5, /device:TPU:0, one launch (start us, length us, event | category | flops | bytes accessed | tf_op | source)
XLA Modules:
  0.0 595.0 jit_solution(7719010370401573831)
XLA Ops:
  0.7 1.3 reduce_sum.9
  2.7 1.2 dynamic_slice.3.sc_ref
  3.9 1.3 maximum_bitcast_fusion
  5.3 1.0 fusion
  6.2 205.1 %front.1 = (bf16[4,128,1024]{2,1,0:T(8,128)(2,1)}, bf16[4,128,1024]{2,1,0:T(8,128)(2,1)}, f32[4,128,1024]{2,1,0:T(8,128)}, f32[4,128,512]{2,1,0:T(8,128)}, bf16[...) custom-call(s32[4]{0:T(128)} %dynamic_slice.3.sc_ref, ...), custom_call_target="tpu_custom_call" | custom-call | tf_op jit(solution)/shard_map/front/pallas_call | solution.py:1270
  211.3 359.4 %tail.1 = (bf16[24,512,512]{2,1,0:T(8,128)(2,1)}, f32[4,128,1024]{2,1,0:T(8,128)}, bf16[8,3,128,1024]{3,2,1,0:T(8,128)(2,1)}, f32[40,1024]{1,0:T(8,128)}, bf16[2...) custom-call(s32[4]{0:T(128)} %dynamic_slice.3.sc_ref, ...), custom_call_target="tpu_custom_call" | custom-call | tf_op jit(solution)/shard_map/tail/pallas_call | solution.py:2006
  570.7 0.0 copy-start
  570.7 0.9 copy-done
  571.6 0.0 copy-start.2
  571.6 0.0 copy-start.1
  571.6 20.8 %unpack.1 = (f32[4,1024,512]{2,1,0:T(8,128)}, f32[4,1024,512]{2,1,0:T(8,128)}, f32[4,512,1024]{2,1,0:T(8,128)}, f32[1024,1024]{1,0:T(8,128)}, f32[1024,512]{1,0:...) custom-call(bf16[24,512,512]{2,1,0:T(8,128)(2,1)} %get-tuple-element, ...), custom_call_target="tpu_custom_call" | custom-call | tf_op jit(solution)/shard_map/unpack/pallas_call | solution.py:2079
  592.4 0.0 copy-done.2
  592.4 1.0 copy.33
  593.4 0.0 copy-done.1
  593.4 1.3 copy.34
  (2 shorter events, 0.0 us)
Async XLA Ops:
  570.7 0.9 copy-start
  571.6 20.8 %copy-start.2 = (bf16[4,128,1024]{2,1,0:T(8,128)(2,1)S(1)}, bf16[4,128,1024]{2,1,0:T(8,128)(2,1)}, u32[]{:S(2)}) copy-start(bf16[4,128,1024]{2,1,0:T(8,128)(2,1)} %get-tuple-element.109) | copy-start | bytes 3145732
  571.6 21.8 %copy-start.1 = (f32[4,128,1024]{2,1,0:T(8,128)S(1)}, f32[4,128,1024]{2,1,0:T(8,128)}, u32[]{:S(2)}) copy-start(f32[4,128,1024]{2,1,0:T(8,128)} %get-tuple-element.110) | copy-start | bytes 6291460
